TPU v7x, 256 devices: a whole 4x4x8 slice. The times are simulated.
256 devices in a mesh: section: 4 (over x_hi, core), lat: 8 (over z), lon: 8 (over x_lo, y).
Axes of the slice: x: 4 (x_hi: 2, x_lo: 2; x = x_hi * 2 + x_lo), y: 4, z: 8, core: 2. Of those that a mesh axis runs over, the one named last changes fastest.
Arguments:
- states: bfloat16 [4, 1, 192, 96, 192], P('section', None, 'lat', 'lon'), may hold values from -60 to 60
- loss_grads: bfloat16 [4, 1, 192, 96, 192], P('section', None, 'lat', 'lon'), may hold values from -6 to 6
- land_sea: int32 [192, 96], P('lat', 'lon'), may hold values 0 or 1
- land_embed: float32 [192], replicated, may hold values from -4 to 4
- gain_attn: float32 [192], replicated, may hold values from 0.5 to 1.5
- gain_mlp: float32 [192], replicated, may hold values from 0.5 to 1.5
- w_qkv: bfloat16 [192, 576], replicated, may hold values from -0.4375 to 0.4375
- w_out: bfloat16 [192, 192], replicated, may hold values from -0.4375 to 0.4375
- w_up: bfloat16 [192, 768], replicated, may hold values from -0.4375 to 0.4375
- w_down: bfloat16 [768, 192], replicated, may hold values from -0.21875 to 0.21875
Outputs:
- state_grads: float32 [4, 1, 192, 96, 192], P('section', None, 'lat', 'lon')
- grad_qkv: float32 [192, 576], replicated
- grad_out: float32 [192, 192], replicated
- grad_up: float32 [192, 768], replicated
- grad_down: float32 [768, 192], replicated
- grad_land: float32 [192], replicated
- grad_gain_attn: float32 [192], replicated
- grad_gain_mlp: float32 [192], replicated
All inputs are finite; a program needn't handle non-finite values. No bound on the sum of `land_sea` on one device may be relied on, other than what follows from the above.
Results may differ from a plain program's by a relative error of at most 0.015.
Values may be sent and summed in bfloat16 or wider, within the bound.
No kernel may reach another device: no remote copies, remote signals or barrier semaphores. Data moves between devices by JAX's collectives and lax.ppermute only.
A program may use at most 64 MiB of HBM per device.

v0:
```python
import jax
import jax.numpy as jnp
from jax import lax
from jax.sharding import PartitionSpec as P

HEADS = 6
HEAD_DIM = 32
WIN_LAT = 6
WIN_LON = 12


EPS = 1e-05


def shifted(value, axis, steps):
    count = lax.axis_size(axis)
    pairs = [(source, (source + steps) % count) for source in range(count)]
    return lax.ppermute(value, axis, pairs)


def shifted_2(block, axis, distance):
    devices = range(lax.axis_size(axis))
    route = [(i - distance, i) for i in devices if i - distance in devices]
    return lax.ppermute(block, axis, route)


def normalize(field, gain):
    centre = jnp.mean(field, axis=-1, keepdims=True)
    offset = field - centre
    spread = jnp.mean(offset * offset, axis=-1, keepdims=True)
    return offset * lax.rsqrt(spread + EPS) * gain


def exact_gelu(values):
    return jax.nn.gelu(values, approximate=False)


def to_windows(field):
    depth, height, breadth, width = field.shape
    grid = field.reshape(depth, height // WIN_LAT, WIN_LAT, breadth // WIN_LON, WIN_LON, width)
    grid = grid.transpose(1, 3, 0, 2, 4, 5)
    return grid.reshape(height // WIN_LAT, breadth // WIN_LON, depth * WIN_LAT * WIN_LON, width)


def from_windows(blocks, depth):
    band_count, cell_count, tokens, width = blocks.shape
    grid = blocks.reshape(band_count, cell_count, depth, WIN_LAT, WIN_LON, width)
    grid = grid.transpose(2, 0, 3, 1, 4, 5)
    return grid.reshape(depth, band_count * WIN_LAT, cell_count * WIN_LON, width)


def allowed_pairs(first_row, total_rows, band_count, depth):
    row_ids = first_row + jnp.arange(band_count * WIN_LAT, dtype=jnp.int32)
    source = (row_ids + WIN_LAT // 2) % total_rows
    labels = (source < WIN_LAT // 2).astype(jnp.int32).reshape(band_count, 1, WIN_LAT, 1)
    labels = jnp.broadcast_to(labels, (band_count, depth, WIN_LAT, WIN_LON))
    labels = labels.reshape(band_count, depth * WIN_LAT * WIN_LON)
    return (labels[:, :, None] == labels[:, None, :]).astype(jnp.float32)


def heads_of(block):
    band_count, cell_count, tokens, width = block.shape
    return block.reshape(band_count, cell_count, tokens, HEADS, width // HEADS)


def merge_heads(block):
    band_count, cell_count, tokens, heads, size = block.shape
    return block.reshape(band_count, cell_count, tokens, heads * size)


def attend(qkv_win, allow):
    width = qkv_win.shape[-1] // 3
    query = heads_of(qkv_win[..., :width])
    keys = heads_of(qkv_win[..., width : 2 * width])
    values = heads_of(qkv_win[..., 2 * width :])
    scores = jnp.einsum(
        "abqhd,abkhd->abhqk", query, keys, preferred_element_type=jnp.float32
    ) * HEAD_DIM ** (-0.5)
    weights = jnp.exp(scores) * allow[:, None, None]
    probs = weights / jnp.sum(weights, axis=-1, keepdims=True)
    mixed = jnp.einsum(
        "abhqk,abkhd->abqhd", probs.astype(jnp.bfloat16), values, preferred_element_type=jnp.float32
    )
    return (probs, merge_heads(mixed).astype(jnp.bfloat16))


def attend_back(qkv_win, probs, d_mixed):
    width = qkv_win.shape[-1] // 3
    query = heads_of(qkv_win[..., :width])
    keys = heads_of(qkv_win[..., width : 2 * width])
    values = heads_of(qkv_win[..., 2 * width :])
    d_heads = heads_of(d_mixed)
    d_probs = jnp.einsum("abqhd,abkhd->abhqk", d_heads, values, preferred_element_type=jnp.float32)
    d_values = jnp.einsum(
        "abhqk,abqhd->abkhd",
        probs.astype(jnp.bfloat16),
        d_heads,
        preferred_element_type=jnp.float32,
    )
    d_scores = (
        probs * (d_probs - jnp.sum(probs * d_probs, axis=-1, keepdims=True)) * HEAD_DIM ** (-0.5)
    )
    d_scores = d_scores.astype(jnp.bfloat16)
    d_query = jnp.einsum("abhqk,abkhd->abqhd", d_scores, keys, preferred_element_type=jnp.float32)
    d_keys = jnp.einsum("abhqk,abqhd->abkhd", d_scores, query, preferred_element_type=jnp.float32)
    joined = jnp.concatenate(
        [merge_heads(d_query), merge_heads(d_keys), merge_heads(d_values)], axis=-1
    )
    return joined.astype(jnp.bfloat16)


def rows_ahead(field):
    half = WIN_LAT // 2
    piece = field[:, :half]
    arrived = shifted(piece, "lat", -1)
    return jnp.concatenate([field[:, half:], arrived], axis=1)


def rows_behind(field):
    half = WIN_LAT // 2
    piece = field[:, -half:]
    arrived = shifted(piece, "lat", 1)
    return jnp.concatenate([arrived, field[:, :-half]], axis=1)


def cols_ahead(field):
    half = WIN_LON // 2
    arrived = shifted(field[:, :, :half], "lon", -1)
    return jnp.concatenate([field[:, :, half:], arrived], axis=2)


def cols_behind(field):
    half = WIN_LON // 2
    arrived = shifted(field[:, :, -half:], "lon", 1)
    return jnp.concatenate([arrived, field[:, :, :-half]], axis=2)


def roll_ahead(field):
    return cols_ahead(rows_ahead(field))


def roll_behind(field):
    return cols_behind(rows_behind(field))


def forward(
    state, land, first_row, total_rows, land_embed, gain_attn, gain_mlp, w_qkv, w_out, w_up
):
    depth, height, breadth, width = state.shape
    embedded = state.astype(jnp.float32) + land * land_embed
    normed, attn_back = jax.vjp(normalize, embedded, gain_attn)
    normed = normed.astype(jnp.bfloat16)
    rolled = roll_ahead(normed).reshape(-1, width)
    qkv = jnp.dot(rolled, w_qkv, preferred_element_type=jnp.float32).astype(jnp.bfloat16)
    qkv_win = to_windows(qkv.reshape(depth, height, breadth, 3 * width))
    allow = allowed_pairs(first_row, total_rows, height // WIN_LAT, depth)
    probs, mixed_win = attend(qkv_win, allow)
    mixed = from_windows(mixed_win, depth).reshape(-1, width)
    projected = jnp.dot(mixed, w_out, preferred_element_type=jnp.float32).astype(jnp.bfloat16)
    hidden_in = embedded + roll_behind(projected.reshape(depth, height, breadth, width)).astype(
        jnp.float32
    )
    normed_mlp, mlp_back = jax.vjp(normalize, hidden_in, gain_mlp)
    normed_mlp = normed_mlp.astype(jnp.bfloat16).reshape(-1, width)
    pre_act = jnp.dot(normed_mlp, w_up, preferred_element_type=jnp.float32)
    activated, gelu_back = jax.vjp(exact_gelu, pre_act)
    activated = activated.astype(jnp.bfloat16)
    return (attn_back, rolled, qkv_win, probs, mixed, mlp_back, normed_mlp, gelu_back, activated)


def backward(saved, cotangent, land, w_qkv, w_out, w_up, w_down, with_weights):
    attn_back, rolled, qkv_win, probs, mixed, mlp_back, normed_mlp, gelu_back, activated = saved
    depth, height, breadth, width = cotangent.shape
    cot_round = cotangent.astype(jnp.bfloat16).reshape(-1, width)
    d_act = jnp.dot(cot_round, w_down.T, preferred_element_type=jnp.float32)
    d_pre = gelu_back(d_act)[0].astype(jnp.bfloat16)
    d_normed_mlp = jnp.dot(d_pre, w_up.T, preferred_element_type=jnp.float32).reshape(
        depth, height, breadth, width
    )
    d_hidden, gain_mlp_part = mlp_back(d_normed_mlp)
    d_hidden = cotangent + d_hidden
    d_projected = roll_ahead(d_hidden.astype(jnp.bfloat16)).reshape(-1, width)
    d_mixed = jnp.dot(d_projected, w_out.T, preferred_element_type=jnp.float32).astype(jnp.bfloat16)
    d_qkv_win = attend_back(
        qkv_win, probs, to_windows(d_mixed.reshape(depth, height, breadth, width))
    )
    d_qkv = from_windows(d_qkv_win, depth).reshape(-1, 3 * width)
    d_rolled = jnp.dot(d_qkv, w_qkv.T, preferred_element_type=jnp.float32).astype(jnp.bfloat16)
    d_normed = roll_behind(d_rolled.reshape(depth, height, breadth, width)).astype(jnp.float32)
    d_embedded, gain_attn_part = attn_back(d_normed)
    d_state = d_hidden + d_embedded
    if not with_weights:
        return (d_state, None)
    part_down = jnp.dot(activated.T, cot_round, preferred_element_type=jnp.float32)
    part_up = jnp.dot(normed_mlp.T, d_pre, preferred_element_type=jnp.float32)
    part_out = jnp.dot(mixed.T, d_projected, preferred_element_type=jnp.float32)
    part_qkv = jnp.dot(rolled.T, d_qkv, preferred_element_type=jnp.float32)
    part_land = jnp.sum(d_state * land, axis=(0, 1, 2))
    return (
        d_state,
        (part_qkv, part_out, part_up, part_down, part_land, gain_attn_part, gain_mlp_part),
    )


def local(
    states, loss_grads, land_sea, land_embed, gain_attn, gain_mlp, w_qkv, w_out, w_up, w_down
):
    depth = states.shape[1]
    band_rows = states.shape[2]
    breadth = states.shape[3]
    total_rows = band_rows * lax.axis_size("lat")
    section_count = lax.axis_size("section")
    land = land_sea.astype(jnp.float32)[None, :, :, None]
    first_row = lax.axis_index("lat") * band_rows
    saved = forward(
        states[0], land, first_row, total_rows, land_embed, gain_attn, gain_mlp, w_qkv, w_out, w_up
    )
    own_loss = loss_grads[0].astype(jnp.float32)
    incoming = jnp.zeros(own_loss.shape, jnp.float32)
    for number in range(section_count - 1):
        d_state, unused = backward(
            saved, own_loss + incoming, land, w_qkv, w_out, w_up, w_down, False
        )
        incoming = shifted_2(d_state.astype(jnp.bfloat16), "section", -1).astype(jnp.float32)
    d_state, parts = backward(saved, own_loss + incoming, land, w_qkv, w_out, w_up, w_down, True)
    d_out = d_state[None]
    totals = lax.psum(
        (parts[0], parts[1], parts[2], parts[3], parts[4], parts[5], parts[6]),
        ("section", "lat", "lon"),
    )
    cell_total = section_count * depth * total_rows * breadth * lax.axis_size("lon")
    factor = float(cell_total) ** (-0.5)
    return (
        d_out,
        totals[0] * factor,
        totals[1] * factor,
        totals[2] * factor,
        totals[3] * factor,
        totals[4] * factor,
        totals[5] * factor,
        totals[6] * factor,
    )


def solution(mesh):
    return jax.shard_map(
        local,
        mesh=mesh,
        in_specs=(
            P("section", None, "lat", "lon", None),
            P("section", None, "lat", "lon", None),
            P("lat", "lon"),
            P(),
            P(),
            P(),
            P(),
            P(),
            P(),
            P(),
        ),
        out_specs=(P("section", None, "lat", "lon", None), P(), P(), P(), P(), P(), P(), P()),
        check_vma=False,
    )
```

profile of v0, /device:TPU:4, one launch (start us, length us, event | category | flops | bytes accessed | tf_op | source)
XLA Modules:
  0.0 482.5 jit_solution(2849508610521910310)
XLA Ops:
  11.1 5.9 %collective-permute-start = (bf16[1,3,12,192]{3,2,1,0:T(8,128)(2,1)S(1)}, bf16[1,3,12,192]{3,2,1,0:T(8,128)(2,1)S(1)}, u32[]{:S(2)}, u32[]{:S(2)}) collective-permute-start(bf16[1,3,12,192]{3,2,1,0:T(8,128)(2,1)S(1)} %slice.185), channel_id=1, source_target_pairs={{0,56},{8,0},{16,8},{24,16},{32,24},{40,32},{48,40},{56,48},{1,57}... | collective-permute-start | bytes 41480 | tf_op jit(solution)/shard_map/ppermute | solution.py:18
  18.6 3.7 collective-permute-start.1
  30.4 5.3 %collective-permute-done.2 = bf16[1,3,12,192]{3,2,1,0:T(8,128)(2,1)S(1)} collective-permute-done((bf16[1,3,12,192]{3,2,1,0:T(8,128)(2,1)S(1)}, bf16[1,3,12,192]{3,2,1,0:T(8,128)(2,1)S(1)}, u32[]{:S(2)}, u32[]{:S(2)}) %collective-permute-start.2) | collective-permute-done | bytes 13856 | tf_op jit(solution)/shard_map/ppermute | solution.py:18
  37.5 5.5 %collective-permute-done.3 = bf16[1,24,6,192]{3,2,1,0:T(8,128)(2,1)S(1)} collective-permute-done((bf16[1,24,6,192]{3,2,1,0:T(8,128)(2,1)S(1)}, bf16[1,24,6,192]{3,2,1,0:T(8,128)(2,1)S(1)}, u32[]{:S(2)}, u32[]{:S(2)}) %collective-permute-start.3) | collective-permute-done | bytes 55328 | tf_op jit(solution)/shard_map/ppermute | solution.py:18
  44.6 3.2 fusion.35
  54.9 2.6 collective-permute-start.5
  57.5 2.6 collective-permute-done.5
  70.3 5.0 %collective-permute-done.6 = bf16[1,3,12,192]{3,2,1,0:T(8,128)(2,1)S(1)} collective-permute-done((bf16[1,3,12,192]{3,2,1,0:T(8,128)(2,1)S(1)}, bf16[1,3,12,192]{3,2,1,0:T(8,128)(2,1)S(1)}, u32[]{:S(2)}, u32[]{:S(2)}) %collective-permute-start.6) | collective-permute-done | bytes 13856 | tf_op jit(solution)/shard_map/ppermute | solution.py:18
  75.4 6.7 %collective-permute-done.7 = bf16[1,24,6,192]{3,2,1,0:T(8,128)(2,1)S(1)} collective-permute-done((bf16[1,24,6,192]{3,2,1,0:T(8,128)(2,1)S(1)}, bf16[1,24,6,192]{3,2,1,0:T(8,128)(2,1)S(1)}, u32[]{:S(2)}, u32[]{:S(2)}) %collective-permute-start.7) | collective-permute-done | bytes 55328 | tf_op jit(solution)/shard_map/ppermute | solution.py:18
  85.6 3.2 collective-permute-done.8
  99.1 2.6 collective-permute-done.10
  106.6 3.0 fusion.27
  114.9 5.0 %collective-permute-done.11 = bf16[1,3,12,192]{3,2,1,0:T(8,128)(2,1)S(1)} collective-permute-done((bf16[1,3,12,192]{3,2,1,0:T(8,128)(2,1)S(1)}, bf16[1,3,12,192]{3,2,1,0:T(8,128)(2,1)S(1)}, u32[]{:S(2)}, u32[]{:S(2)}) %collective-permute-start.11) | collective-permute-done | bytes 13856 | tf_op jit(solution)/shard_map/ppermute | solution.py:18
  120.2 6.7 %collective-permute-done.12 = bf16[1,24,6,192]{3,2,1,0:T(8,128)(2,1)S(1)} collective-permute-done((bf16[1,24,6,192]{3,2,1,0:T(8,128)(2,1)S(1)}, bf16[1,24,6,192]{3,2,1,0:T(8,128)(2,1)S(1)}, u32[]{:S(2)}, u32[]{:S(2)}) %collective-permute-start.12) | collective-permute-done | bytes 55328 | tf_op jit(solution)/shard_map/ppermute | solution.py:18
  130.4 3.2 collective-permute-done.13
  141.8 2.5 collective-permute-start.15
  151.3 3.0 fusion.30
  159.6 5.0 %collective-permute-done.16 = bf16[1,3,12,192]{3,2,1,0:T(8,128)(2,1)S(1)} collective-permute-done((bf16[1,3,12,192]{3,2,1,0:T(8,128)(2,1)S(1)}, bf16[1,3,12,192]{3,2,1,0:T(8,128)(2,1)S(1)}, u32[]{:S(2)}, u32[]{:S(2)}) %collective-permute-start.16) | collective-permute-done | bytes 13856 | tf_op jit(solution)/shard_map/ppermute | solution.py:18
  164.8 7.1 %collective-permute-done.17 = bf16[1,24,6,192]{3,2,1,0:T(8,128)(2,1)S(1)} collective-permute-done((bf16[1,24,6,192]{3,2,1,0:T(8,128)(2,1)S(1)}, bf16[1,24,6,192]{3,2,1,0:T(8,128)(2,1)S(1)}, u32[]{:S(2)}, u32[]{:S(2)}) %collective-permute-start.17) | collective-permute-done | bytes 55328 | tf_op jit(solution)/shard_map/ppermute | solution.py:18
  175.6 3.0 collective-permute-done.18
  202.9 3.1 collective-permute-done.21
  207.0 5.8 %collective-permute-done.22 = bf16[1,24,6,192]{3,2,1,0:T(8,128)(2,1)S(1)} collective-permute-done((bf16[1,24,6,192]{3,2,1,0:T(8,128)(2,1)S(1)}, bf16[1,24,6,192]{3,2,1,0:T(8,128)(2,1)S(1)}, u32[]{:S(2)}, u32[]{:S(2)}) %collective-permute-start.22) | collective-permute-done | bytes 55328 | tf_op jit(solution)/shard_map/ppermute | solution.py:18
  214.8 72.6 %all-reduce = (f32[192]{0:T(256)S(1)}, f32[192]{0:T(256)S(1)}, f32[192]{0:T(256)S(1)}) all-reduce(f32[192]{0:T(256)S(1)} %get-tuple-element.19, f32[192]{0:T(256)S(1)} %get-tuple-element.18, f32[192]{0:T(256)S(1)} %get-tuple-element.16), channel_id=1, replica_groups=mesh['section'=4,'lat'=8,'lon'=8] {'section','lat','lon'}, use_global_device_ids=true, to_apply=%region_30.31 | all-reduce | flops 576 | bytes 4608 | tf_op jit(solution)/shard_map/psum | solution.py:227
  288.5 182.1 %all-reduce.4.cloned.1.call-done = (f32[192,576]{1,0:T(8,128)}, f32[192,192]{1,0:T(8,128)}, f32[192,768]{1,0:T(8,128)}, f32[768,192]{0,1:T(8,128)}) async-done(((f32[192,576]{1,0:T(8,128)}, f32[192,192]{1,0:T(8,128)}, f32[192,768]{1,0:T(8,128)}, f32[768,192]{0,1:T(8,128)}), (f32[192,576]{1,0:T(8,128)}, f32[192,192]{1,0:T(8,128)}, f32[192,768]{1,0:T(8,128)}, ...) | async-done | bytes 1769488 | tf_op jit(solution)/shard_map/psum | solution.py:227
  (323 shorter events, 118.5 us)
Async XLA Ops:
  7.2 463.5 %all-reduce.4.cloned.1.call-start = ((), (), s32[]{:S(2)}) async-start(), calls=%async_computation | async-start | bytes 3735552 | tf_op jit(solution)/shard_map/psum | solution.py:227
  11.1 7.5 %collective-permute-start = (bf16[1,3,12,192]{3,2,1,0:T(8,128)(2,1)S(1)}, bf16[1,3,12,192]{3,2,1,0:T(8,128)(2,1)S(1)}, u32[]{:S(2)}, u32[]{:S(2)}) collective-permute-start(bf16[1,3,12,192]{3,2,1,0:T(8,128)(2,1)S(1)} %slice.185), channel_id=1, source_target_pairs={{0,56},{8,0},{16,8},{24,16},{32,24},{40,32},{48,40},{56,48},{1,57}... | collective-permute-start | bytes 41480 | tf_op jit(solution)/shard_map/ppermute | solution.py:18
  18.6 5.9 %collective-permute-start.1 = (bf16[1,24,6,192]{3,2,1,0:T(8,128)(2,1)S(1)}, bf16[1,24,6,192]{3,2,1,0:T(8,128)(2,1)S(1)}, u32[]{:S(2)}, u32[]{:S(2)}) collective-permute-start(bf16[1,24,6,192]{3,2,1,0:T(8,128)(2,1)S(1)} %get-tuple-element.42), channel_id=1, source_target_pairs={{0,7},{1,0},{2,1},{3,2},{4,3},{5,4},{6,5},{7,6},{8,15},{9,8},{10,9... | collective-permute-start | bytes 165896 | tf_op jit(solution)/shard_map/ppermute | solution.py:18
  30.3 5.4 %collective-permute-start.2 = (bf16[1,3,12,192]{3,2,1,0:T(8,128)(2,1)S(1)}, bf16[1,3,12,192]{3,2,1,0:T(8,128)(2,1)S(1)}, u32[]{:S(2)}, u32[]{:S(2)}) collective-permute-start(bf16[1,3,12,192]{3,2,1,0:T(8,128)(2,1)S(1)} %slice.191), channel_id=1, source_target_pairs={{0,8},{8,16},{16,24},{24,32},{32,40},{40,48},{48,56},{56,0},{1,9},... | collective-permute-start | bytes 41480 | tf_op jit(solution)/shard_map/ppermute | solution.py:18
  35.8 7.2 %collective-permute-start.3 = (bf16[1,24,6,192]{3,2,1,0:T(8,128)(2,1)S(1)}, bf16[1,24,6,192]{3,2,1,0:T(8,128)(2,1)S(1)}, u32[]{:S(2)}, u32[]{:S(2)}) collective-permute-start(bf16[1,24,6,192]{3,2,1,0:T(8,128)(2,1)S(1)} %fusion.160), channel_id=1, source_target_pairs={{0,1},{1,2},{2,3},{3,4},{4,5},{5,6},{6,7},{7,0},{8,9},{9,10},{10,1... | collective-permute-start | bytes 165896 | tf_op jit(solution)/shard_map/ppermute | solution.py:18
  51.0 3.9 collective-permute-start.4
  54.9 5.2 %collective-permute-start.5 = (bf16[1,24,6,192]{3,2,1,0:T(8,128)(2,1)S(1)}, bf16[1,24,6,192]{3,2,1,0:T(8,128)(2,1)S(1)}, u32[]{:S(2)}, u32[]{:S(2)}) collective-permute-start(bf16[1,24,6,192]{3,2,1,0:T(8,128)(2,1)S(1)} %get-tuple-element.40), channel_id=1, source_target_pairs={{0,7},{1,0},{2,1},{3,2},{4,3},{5,4},{6,5},{7,6},{8,15},{9,8},{10,9... | collective-permute-start | bytes 165896 | tf_op jit(solution)/shard_map/ppermute | solution.py:18
  70.2 5.1 %collective-permute-start.6 = (bf16[1,3,12,192]{3,2,1,0:T(8,128)(2,1)S(1)}, bf16[1,3,12,192]{3,2,1,0:T(8,128)(2,1)S(1)}, u32[]{:S(2)}, u32[]{:S(2)}) collective-permute-start(bf16[1,3,12,192]{3,2,1,0:T(8,128)(2,1)S(1)} %slice.199), channel_id=1, source_target_pairs={{0,8},{8,16},{16,24},{24,32},{32,40},{40,48},{48,56},{56,0},{1,9},... | collective-permute-start | bytes 41480 | tf_op jit(solution)/shard_map/ppermute | solution.py:18
  75.3 6.8 %collective-permute-start.7 = (bf16[1,24,6,192]{3,2,1,0:T(8,128)(2,1)S(1)}, bf16[1,24,6,192]{3,2,1,0:T(8,128)(2,1)S(1)}, u32[]{:S(2)}, u32[]{:S(2)}) collective-permute-start(bf16[1,24,6,192]{3,2,1,0:T(8,128)(2,1)S(1)} %fusion.158), channel_id=1, source_target_pairs={{0,1},{1,2},{2,3},{3,4},{4,5},{5,6},{6,7},{7,0},{8,9},{9,10},{10,1... | collective-permute-start | bytes 165896 | tf_op jit(solution)/shard_map/ppermute | solution.py:18
  83.7 5.1 %collective-permute-start.8 = (bf16[1,24,12,192]{3,2,1,0:T(8,128)(2,1)S(1)}, bf16[1,24,12,192]{3,2,1,0:T(8,128)(2,1)S(1)}, u32[]{:S(2)}, u32[]{:S(2)}) collective-permute-start(bf16[1,24,12,192]{3,2,1,0:T(8,128)(2,1)S(1)} %add_convert_fusion.6), channel_id=1, source_target_pairs={{64,0},{128,64},{192,128},{65,1},{129,65},{193,129},{66,2},{130,66... | collective-permute-start | bytes 331784 | tf_op jit(solution)/shard_map/ppermute | solution.py:24
  93.1 3.9 collective-permute-start.9
  97.1 4.7 collective-permute-start.10
  114.8 5.1 %collective-permute-start.11 = (bf16[1,3,12,192]{3,2,1,0:T(8,128)(2,1)S(1)}, bf16[1,3,12,192]{3,2,1,0:T(8,128)(2,1)S(1)}, u32[]{:S(2)}, u32[]{:S(2)}) collective-permute-start(bf16[1,3,12,192]{3,2,1,0:T(8,128)(2,1)S(1)} %slice.207), channel_id=1, source_target_pairs={{0,8},{8,16},{16,24},{24,32},{32,40},{40,48},{48,56},{56,0},{1,9},... | collective-permute-start | bytes 41480 | tf_op jit(solution)/shard_map/ppermute | solution.py:18
  119.9 7.0 %collective-permute-start.12 = (bf16[1,24,6,192]{3,2,1,0:T(8,128)(2,1)S(1)}, bf16[1,24,6,192]{3,2,1,0:T(8,128)(2,1)S(1)}, u32[]{:S(2)}, u32[]{:S(2)}) collective-permute-start(bf16[1,24,6,192]{3,2,1,0:T(8,128)(2,1)S(1)} %fusion.156), channel_id=1, source_target_pairs={{0,1},{1,2},{2,3},{3,4},{4,5},{5,6},{6,7},{7,0},{8,9},{9,10},{10,1... | collective-permute-start | bytes 165896 | tf_op jit(solution)/shard_map/ppermute | solution.py:18
  128.5 5.1 %collective-permute-start.13 = (bf16[1,24,12,192]{3,2,1,0:T(8,128)(2,1)S(1)}, bf16[1,24,12,192]{3,2,1,0:T(8,128)(2,1)S(1)}, u32[]{:S(2)}, u32[]{:S(2)}) collective-permute-start(bf16[1,24,12,192]{3,2,1,0:T(8,128)(2,1)S(1)} %add_convert_fusion.5), channel_id=1, source_target_pairs={{64,0},{128,64},{192,128},{65,1},{129,65},{193,129},{66,2},{130,66... | collective-permute-start | bytes 331784 | tf_op jit(solution)/shard_map/ppermute | solution.py:24
  137.9 3.9 collective-permute-start.14
  141.8 4.7 collective-permute-start.15
  159.5 5.1 %collective-permute-start.16 = (bf16[1,3,12,192]{3,2,1,0:T(8,128)(2,1)S(1)}, bf16[1,3,12,192]{3,2,1,0:T(8,128)(2,1)S(1)}, u32[]{:S(2)}, u32[]{:S(2)}) collective-permute-start(bf16[1,3,12,192]{3,2,1,0:T(8,128)(2,1)S(1)} %slice.215), channel_id=1, source_target_pairs={{0,8},{8,16},{16,24},{24,32},{32,40},{40,48},{48,56},{56,0},{1,9},... | collective-permute-start | bytes 41480 | tf_op jit(solution)/shard_map/ppermute | solution.py:18
  164.7 7.2 %collective-permute-start.17 = (bf16[1,24,6,192]{3,2,1,0:T(8,128)(2,1)S(1)}, bf16[1,24,6,192]{3,2,1,0:T(8,128)(2,1)S(1)}, u32[]{:S(2)}, u32[]{:S(2)}) collective-permute-start(bf16[1,24,6,192]{3,2,1,0:T(8,128)(2,1)S(1)} %fusion.154), channel_id=1, source_target_pairs={{0,1},{1,2},{2,3},{3,4},{4,5},{5,6},{6,7},{7,0},{8,9},{9,10},{10,1... | collective-permute-start | bytes 165896 | tf_op jit(solution)/shard_map/ppermute | solution.py:18
  173.5 5.1 %collective-permute-start.18 = (bf16[1,24,12,192]{3,2,1,0:T(8,128)(2,1)S(1)}, bf16[1,24,12,192]{3,2,1,0:T(8,128)(2,1)S(1)}, u32[]{:S(2)}, u32[]{:S(2)}) collective-permute-start(bf16[1,24,12,192]{3,2,1,0:T(8,128)(2,1)S(1)} %add_convert_fusion.4), channel_id=1, source_target_pairs={{64,0},{128,64},{192,128},{65,1},{129,65},{193,129},{66,2},{130,66... | collective-permute-start | bytes 331784 | tf_op jit(solution)/shard_map/ppermute | solution.py:24
  184.3 3.9 collective-permute-start.19
  188.2 4.7 collective-permute-start.20
  200.9 5.1 %collective-permute-start.21 = (bf16[1,3,12,192]{3,2,1,0:T(8,128)(2,1)S(1)}, bf16[1,3,12,192]{3,2,1,0:T(8,128)(2,1)S(1)}, u32[]{:S(2)}, u32[]{:S(2)}) collective-permute-start(bf16[1,3,12,192]{3,2,1,0:T(8,128)(2,1)S(1)} %slice.223), channel_id=1, source_target_pairs={{0,8},{8,16},{16,24},{24,32},{32,40},{40,48},{48,56},{56,0},{1,9},... | collective-permute-start | bytes 41480 | tf_op jit(solution)/shard_map/ppermute | solution.py:18
  206.0 6.8 %collective-permute-start.22 = (bf16[1,24,6,192]{3,2,1,0:T(8,128)(2,1)S(1)}, bf16[1,24,6,192]{3,2,1,0:T(8,128)(2,1)S(1)}, u32[]{:S(2)}, u32[]{:S(2)}) collective-permute-start(bf16[1,24,6,192]{3,2,1,0:T(8,128)(2,1)S(1)} %fusion.152), channel_id=1, source_target_pairs={{0,1},{1,2},{2,3},{3,4},{4,5},{5,6},{6,7},{7,0},{8,9},{9,10},{10,1... | collective-permute-start | bytes 165896 | tf_op jit(solution)/shard_map/ppermute | solution.py:18
  (39 other events, 124.9 us)
Sparse Core Ops, SparseCore 0:
  207.2 263.4 all-reduce.3
where the time goes:
time: 492 us; the launch traced here: 483 us
  waiting for transfers between devices  264 us (54%)
  blocking collectives  72.6 us (15%)
  matrix products  48.2 us (10%)
  starting transfers between devices  34.5 us (7%)
  local copies, waits for them, and re-layouts  27.9 us (6%)
  other arithmetic  19.3 us (4%)
  between operations  15.7 us (3%)
    psum x1, waiting for transfers between devices, local(): lax.psum((parts[0], parts[1], parts[2], parts[3], parts[4], parts[5], par...  182 us
    ppermute x20, waiting for transfers between devices, shifted(): return lax.ppermute(value, axis, pairs)  72.9 us
    psum x1, blocking collectives, local(): lax.psum((parts[0], parts[1], parts[2], parts[3], parts[4], parts[5], par...  72.6 us
    ppermute x20, starting transfers between devices, shifted(): return lax.ppermute(value, axis, pairs)  28.5 us
    unnamed x82, local copies, waits for them, and re-layouts  13.5 us
    dot_general x4, matrix products, attend_back(): jnp.einsum('abhqk,abqhd->abkhd', d_scores, query, preferred_element_type=...  10.2 us
  transfers between devices with their start and end apart: 24, of which 24 were waited for; matrix products, arithmetic and copies ran while one was open for 2% of the time, Pallas kernels for 0%

commit v1 on v0

v1 whole, which is shorter than its diff:
```python
import jax
import jax.numpy as jnp
from jax import lax
from jax.experimental import pallas as pl
from jax.experimental.pallas import tpu as pltpu
from jax.sharding import PartitionSpec as P

CH = 192
HEADS = 6
HEAD_DIM = 32
MLP = 768
HALF_LAT = 3
HALF_LON = 6
QUAD = HALF_LAT * HALF_LON
WIN = 4 * QUAD
STEPS = 4
TOK = STEPS * WIN
MSG = 512
GROUPS = 64
UNIT = 16
USED = 55
PART = USED * UNIT
SCALE = HEAD_DIM ** (-0.5)
EPS = 1e-05
F32 = jnp.float32
BF16 = jnp.bfloat16
VMEM_LIMIT = 60 * 1024 * 1024


def nn(a, b):
    return lax.dot_general(a, b, (((1,), (0,)), ((), ())), preferred_element_type=F32)


def nt(a, b):
    return lax.dot_general(a, b, (((1,), (1,)), ((), ())), preferred_element_type=F32)


def tn(a, b):
    return lax.dot_general(a, b, (((0,), (0,)), ((), ())), preferred_element_type=F32)


def mean_of(v):
    return jnp.sum(v, axis=-1, keepdims=True) * (1.0 / CH)


def pack_kernel(states, loss, land, out, cells):
    for k in range(4):
        for rh in range(2):
            for r in range(HALF_LAT):
                row = 6 * k + 3 * rh + r
                st = states[row].astype(F32)
                lo = loss[row].astype(F32)
                la = land[row].astype(F32)
                for ch in range(2):
                    q = 2 * rh + ch
                    here = slice(6 * r, 6 * r + 6)
                    cols = slice(6 * ch, 6 * ch + 6)
                    wide = jnp.broadcast_to(la[cols], (6, 64))
                    cells[k, q, here, 0:192] = st[cols]
                    cells[k, q, here, 192:256] = wide
                    cells[k, q, here, 256:448] = lo[cols]
                    cells[k, q, here, 448:512] = wide
    out[...] = cells[...].astype(BF16)


def main_kernel(
    own, right, below, corner, embed, gain_a, gain_m, wqkv, wout, wup, wdown,
    grads_out, msg_out,
    x, qkv, probs, qm_all, emb, xh1, r1, hid_xh, r2, gp, act, normed_s, mixed_s, nm_s,
    cot_s, dpre_s, dproj_s, dqkv_s, dstate, small,
):
    last = jnp.logical_and(lax.axis_index("lat") == 7, lax.axis_index("section") == 3)
    closed = jnp.where(last, 0.0, 1.0).astype(F32)
    for s in range(STEPS):
        for q, piece in enumerate((own, right, below, corner)):
            at = WIN * s + QUAD * q
            x[at : at + QUAD, :] = piece[s].astype(F32)
    land_full = lambda rows: jnp.concatenate([x[rows, 448:512]] * 3, axis=1)
    le = embed[...]
    ga = gain_a[...]
    gm = gain_m[...]
    col_head = lax.broadcasted_iota(jnp.int32, (1, CH), 1) // HEAD_DIM
    masks = [(col_head == h).astype(F32) for h in range(HEADS)]
    row_half = lax.broadcasted_iota(jnp.int32, (WIN, WIN), 0) // (2 * QUAD)
    key_half = lax.broadcasted_iota(jnp.int32, (WIN, WIN), 1) // (2 * QUAD)
    allow1 = jnp.where(row_half == key_half, 1.0, closed).astype(F32)
    allow = jnp.concatenate([allow1] * HEADS, axis=0)

    def spread(v):
        return jnp.concatenate([v * m for m in masks], axis=0).astype(BF16)

    def gathered(v):
        total = v[0:WIN] * masks[0]
        for h in range(1, HEADS):
            total = total + v[WIN * h : WIN * h + WIN] * masks[h]
        return total

    for s in range(STEPS):
        rows = slice(WIN * s, WIN * s + WIN)
        land = x[rows, 192:256][:, 0:1]
        e = x[rows, 0:CH] + land * le
        emb[rows, :] = e
        off = e - mean_of(e)
        r = lax.rsqrt(mean_of(off * off) + EPS)
        xh = off * r
        xh1[rows, :] = xh
        r1[rows, :] = r
        normed_s[rows, :] = (xh * ga)
    normed = normed_s[...].astype(BF16)
    qkv[...] = nn(normed, wqkv[...]).astype(BF16).astype(F32)
    for s in range(STEPS):
        rows = slice(WIN * s, WIN * s + WIN)
        qm = spread(qkv[rows, 0:CH])
        qm_all[s] = qm
        keys = qkv[rows, CH : 2 * CH].astype(BF16)
        values = qkv[rows, 2 * CH : 3 * CH].astype(BF16)
        weights = jnp.exp(nt(qm, keys) * SCALE) * allow
        p = weights / jnp.sum(weights, axis=-1, keepdims=True)
        probs[s] = p
        mixed_s[rows, :] = gathered(nn(p.astype(BF16), values))
    mixed = mixed_s[...].astype(BF16)
    projected = nn(mixed, wout[...]).astype(BF16).astype(F32)
    hid = emb[...] + projected
    off = hid - mean_of(hid)
    r = lax.rsqrt(mean_of(off * off) + EPS)
    xh = off * r
    hid_xh[...] = xh
    r2[...] = r
    nm = (xh * gm).astype(BF16)
    nm_s[...] = nm
    for j in range(MLP // 256):
        cols = slice(256 * j, 256 * j + 256)
        pre = nn(nm_s[...], wup[:, cols])
        cdf = 0.5 * (1.0 + lax.erf(pre * (0.5 ** 0.5)))
        pdf = jnp.exp(pre * pre * -0.5) * 0.3989422804014327
        act[:, cols] = (pre * cdf).astype(BF16)
        gp[:, cols] = cdf + pre * pdf

    gain_m_sum = jnp.zeros((1, CH), F32)
    gain_a_sum = jnp.zeros((1, CH), F32)
    land_sum = jnp.zeros((1, CH), F32)
    incoming = None
    wq = wqkv[:, 0:CH]
    wk = wqkv[:, CH : 2 * CH]
    wv = wqkv[:, 2 * CH : 3 * CH]
    for s in range(STEPS - 1, -1, -1):
        rows = slice(WIN * s, WIN * s + WIN)
        cot = x[rows, 256:448]
        if incoming is not None:
            cot = cot + incoming
        cotb = cot.astype(BF16)
        cot_s[rows, :] = cotb.astype(F32)
        d_pre = gp[rows, :] * nt(cotb, wdown[...])
        dpre_b = d_pre.astype(BF16)
        dpre_s[rows, :] = dpre_b.astype(F32)
        dy = nt(dpre_b, wup[...])
        xh = hid_xh[rows, :]
        gain_m_sum = gain_m_sum + jnp.sum(dy * xh, axis=0, keepdims=True)
        dxh = dy * gm
        d_hid = cot + r2[rows, :] * (dxh - mean_of(dxh) - xh * mean_of(dxh * xh))
        dproj = d_hid.astype(BF16)
        dproj_s[rows, :] = dproj.astype(F32)
        d_mixed = nt(dproj, wout[...]).astype(BF16).astype(F32)
        dm = spread(d_mixed)
        keys = qkv[rows, CH : 2 * CH].astype(BF16)
        values = qkv[rows, 2 * CH : 3 * CH].astype(BF16)
        p = probs[s]
        dp = nt(dm, values)
        dv = tn(p.astype(BF16), dm).astype(BF16)
        ds = (p * (dp - jnp.sum(p * dp, axis=-1, keepdims=True)) * SCALE).astype(BF16)
        dq = gathered(nn(ds, keys)).astype(BF16)
        dk = tn(ds, qm_all[s]).astype(BF16)
        dqkv_s[rows, 0:CH] = dq.astype(F32)
        dqkv_s[rows, CH : 2 * CH] = dk.astype(F32)
        dqkv_s[rows, 2 * CH : 3 * CH] = dv.astype(F32)
        d_rolled = nt(dq, wq) + nt(dk, wk) + nt(dv, wv)
        dy = d_rolled.astype(BF16).astype(F32)
        xh = xh1[rows, :]
        gain_a_sum = gain_a_sum + jnp.sum(dy * xh, axis=0, keepdims=True)
        dxh = dy * ga
        d_state = d_hid + r1[rows, :] * (dxh - mean_of(dxh) - xh * mean_of(dxh * xh))
        land = x[rows, 192:256][:, 0:1]
        land_sum = land_sum + jnp.sum(d_state * land, axis=0, keepdims=True)
        d_round = d_state.astype(BF16)
        incoming = d_round.astype(F32)
        dstate[...] = incoming
        for q in range(4):
            grads_out[q, s] = dstate[QUAD * q : QUAD * q + QUAD, :].astype(BF16)

    factor = float(STEPS * 192 * 96) ** (-0.5)

    def put(tile, value):
        for j in range(value.shape[1] // 128):
            at = (tile + j) * CH
            left = at
            done = 0
            while done < CH:
                part, row = divmod(left, PART)
                n = min(CH - done, PART - row)
                msg_out[part, row : row + n, :] = value[done : done + n, 128 * j : 128 * j + 128]
                done += n
                left += n

    cot_all = cot_s[...].astype(BF16)
    put(12, (tn(cot_all, act[...]) * factor).astype(BF16))
    put(6, (tn(nm_s[...], dpre_s[...].astype(BF16)) * factor).astype(BF16))
    g_qkv = tn(normed_s[...].astype(BF16), dqkv_s[...].astype(BF16)) * factor
    g_out = tn(mixed_s[...].astype(BF16), dproj_s[...].astype(BF16)) * factor
    put(0, jnp.concatenate([g_qkv, g_out], axis=1).astype(BF16))
    small[...] = jnp.zeros_like(small)
    for i, total in enumerate((land_sum, gain_a_sum, gain_m_sum)):
        total = total * factor
        small[2 * i : 2 * i + 1, :] = total[:, 0:128]
        small[2 * i + 1 : 2 * i + 2, 0:64] = total[:, 128:192]
    at = 18 * CH - 3 * PART
    msg_out[3, at:PART, :] = small[...].astype(BF16)


SMALL_ROWS = 4 * PART - 18 * CH


def unpack_kernel(msg, grads, state_out, g_qkv, g_out, g_up, g_down, g_land, g_ga, g_gm, cells):
    def rows_of(at, count):
        pieces = []
        done = 0
        while done < count:
            part, row = divmod(at + done, PART)
            n = min(count - done, PART - row)
            pieces.append(msg[part, row : row + n, :].astype(F32))
            done += n
        return pieces[0] if len(pieces) == 1 else jnp.concatenate(pieces, axis=0)

    for j in range(4):
        g_qkv[:, 128 * j : 128 * j + 128] = rows_of(j * CH, CH)
    mid = rows_of(4 * CH, CH)
    tail = rows_of(5 * CH, CH)
    g_qkv[:, 512:576] = mid[:, 0:64]
    g_out[...] = jnp.concatenate([mid[:, 64:128], tail], axis=1)
    for j in range(6):
        g_up[:, 128 * j : 128 * j + 128] = rows_of((6 + j) * CH, CH)
    for j in range(6):
        g_down[128 * j : 128 * j + 128, :] = rows_of((12 + j) * CH, CH).T
    small = rows_of(18 * CH, 16)
    for i, out in enumerate((g_land, g_ga, g_gm)):
        out[...] = jnp.concatenate([small[2 * i : 2 * i + 1, :], small[2 * i + 1 : 2 * i + 2, 0:64]], axis=1)
    cells[...] = grads[...].astype(F32)
    for k in range(4):
        for rh in range(2):
            for r in range(HALF_LAT):
                for ch in range(2):
                    state_out[6 * k + 3 * rh + r, 6 * ch : 6 * ch + 6, :] = cells[
                        k, 2 * rh + ch, 6 * r : 6 * r + 6, :
                    ]


def hop(value, rows, cols):
    pairs = []
    for k in range(4):
        for a in range(8):
            for b in range(8):
                band = (4 * a + k + rows) % 32
                to = ((band % 4) * 8 + band // 4) * 8 + (b + cols) % 8
                pairs.append(((k * 8 + a) * 8 + b, to))
    return lax.ppermute(value, ("section", "lat", "lon"), pairs)


def exchange(value, axis):
    return lax.all_to_all(value, axis, 0, 0, tiled=True)


def local(
    states, loss_grads, land_sea, land_embed, gain_attn, gain_mlp, w_qkv, w_out, w_up, w_down
):
    params = pltpu.CompilerParams(vmem_limit_bytes=VMEM_LIMIT)
    shape = jax.ShapeDtypeStruct
    packed = pl.pallas_call(
        pack_kernel,
        out_shape=shape((4, 4, QUAD, MSG), BF16),
        scratch_shapes=[pltpu.VMEM((4, 4, QUAD, MSG), F32)],
        compiler_params=params,
        name="pack_cells",
    )(states[0, 0], loss_grads[0, 0], land_sea[..., None])
    cells = exchange(packed, "section")
    right = hop(cells[:, 2], 0, -1)
    below = hop(cells[:, 1], -1, 0)
    corner = hop(cells[:, 0], -1, -1)
    vm = pltpu.VMEM
    grads, msg = pl.pallas_call(
        main_kernel,
        out_shape=(
            shape((4, STEPS, QUAD, CH), BF16),
            shape((4, PART, 128), BF16),
        ),
        scratch_shapes=[
            vm((TOK, MSG), F32),
            vm((TOK, 3 * CH), F32),
            vm((STEPS, HEADS * WIN, WIN), F32),
            vm((STEPS, HEADS * WIN, CH), BF16),
            vm((TOK, CH), F32),
            vm((TOK, CH), F32),
            vm((TOK, 1), F32),
            vm((TOK, CH), F32),
            vm((TOK, 1), F32),
            vm((TOK, MLP), F32),
            vm((TOK, MLP), BF16),
            vm((TOK, CH), F32),
            vm((TOK, CH), F32),
            vm((TOK, CH), BF16),
            vm((TOK, CH), F32),
            vm((TOK, MLP), F32),
            vm((TOK, CH), F32),
            vm((TOK, 3 * CH), F32),
            vm((WIN, CH), F32),
            vm((SMALL_ROWS, 128), F32),
        ],
        compiler_params=params,
        name="window_steps",
    )(
        cells[:, 3], right, below, corner,
        land_embed[None], gain_attn[None], gain_mlp[None], w_qkv, w_out, w_up, w_down,
    )

    home = jnp.stack([hop(grads[3], 1, 1), hop(grads[2], 1, 0), hop(grads[1], 0, 1), grads[0]], axis=1)
    home = exchange(home, "section")

    parts = exchange(msg, "section")
    part = jnp.sum(parts.astype(F32), axis=0).astype(BF16)
    part = jnp.pad(part, ((0, (GROUPS - USED) * UNIT), (0, 0))).reshape(GROUPS, UNIT, 128)
    mine = exchange(part, ("lat", "lon"))
    mine = jnp.sum(mine.astype(F32), axis=0).astype(BF16)
    whole = exchange(jnp.broadcast_to(mine[None], (GROUPS, UNIT, 128)), ("lat", "lon"))
    whole = whole.reshape(GROUPS * UNIT, 128)[:PART]
    msg = exchange(jnp.broadcast_to(whole[None], (4, PART, 128)), "section")

    outs = pl.pallas_call(
        unpack_kernel,
        out_shape=(
            shape((24, 12, CH), F32),
            shape((CH, 3 * CH), F32),
            shape((CH, CH), F32),
            shape((CH, MLP), F32),
            shape((MLP, CH), F32),
            shape((1, CH), F32),
            shape((1, CH), F32),
            shape((1, CH), F32),
        ),
        scratch_shapes=[pltpu.VMEM((4, 4, QUAD, CH), F32)],
        compiler_params=params,
        name="unpack_sums",
    )(msg, home)
    return (
        outs[0][None, None], outs[1], outs[2], outs[3], outs[4], outs[5][0], outs[6][0], outs[7][0],
    )


def solution(mesh):
    cell = P("section", None, "lat", "lon", None)
    return jax.shard_map(
        local,
        mesh=mesh,
        in_specs=(cell, cell, P("lat", "lon"), P(), P(), P(), P(), P(), P(), P()),
        out_specs=(cell, P(), P(), P(), P(), P(), P(), P()),
        check_vma=False,
    )
```

time: 492 us -> 139 us (0.28)
  the two profiles are of different devices: /device:TPU:4 before, /device:TPU:1 now
where the time goes in v1:
time: 139 us; the launch traced here: 138 us
  blocking collectives  51.6 us (37%)
  starting transfers between devices  31.5 us (23%)
  waiting for transfers between devices  23.4 us (17%)
  local copies, waits for them, and re-layouts  15.4 us (11%)
  Pallas kernels  15.2 us (11%)
    all_to_all x3, blocking collectives, exchange(): return lax.all_to_all(value, axis, 0, 0, tiled=True)  51.6 us
    all_to_all x3, waiting for transfers between devices, exchange(): return lax.all_to_all(value, axis, 0, 0, tiled=True)  18.3 us
    all_to_all x3, starting transfers between devices, exchange(): return lax.all_to_all(value, axis, 0, 0, tiled=True)  18.2 us
    ppermute x6, starting transfers between devices, hop(): return lax.ppermute(value, ('section', 'lat', 'lon'), pairs)  13.3 us
    pallas_call x1, Pallas kernels, local(): pl.pallas_call(main_kernel, out_shape=(shape((4, STEPS, QUAD, CH), BF16),...  10.3 us
    unnamed x21, local copies, waits for them, and re-layouts  7.28 us
    ppermute x6, waiting for transfers between devices, hop(): return lax.ppermute(value, ('section', 'lat', 'lon'), pairs)  5.09 us
    pallas_call x1, Pallas kernels, local(): pl.pallas_call(unpack_kernel, out_shape=(shape((24, 12, CH), F32), shape(...  2.82 us
  transfers between devices with their start and end apart: 9, of which 5 were waited for; matrix products, arithmetic and copies ran while one was open for 2% of the time, Pallas kernels for 0%

profile of v1, /device:TPU:1, one launch (start us, length us, event | category | flops | bytes accessed | tf_op | source)
XLA Modules:
  0.0 138.2 jit_solution(6963656461648360910)
XLA Ops:
  0.6 1.6 %copy.47.land = s32[24,12,1]{2,1,0:T(8,128)} copy(s32[24,12,1]{0,1,2:T(8,128)} %bitcast.47) | data formatting | bytes 2304 | tf_op jit(solution)/shard_map/broadcast_in_dim | solution.py:282
  2.2 1.7 %copy_bitcast_fusion = (bf16[24,12,192]{2,1,0:T(8,128)(2,1)}, bf16[24,12,192]{2,1,0:T(8,128)(2,1)}) fusion(bf16[1,1,24,12,192]{4,2,3,1,0:T(8,128)(2,1)S(1)} %copy-done.3, bf16[1,1,24,12,192]{4,2,3,1,0:T(8,128)(2,1)} %param.10), kind=kLoop, calls=%fused_computation.1 | loop fusion | bytes 442368 | tf_op jit(solution)/shard_map/squeeze | solution.py:282
  3.9 2.0 %pack_cells.1 = bf16[4,4,18,512]{3,2,1,0:T(8,128)(2,1)} custom-call(bf16[24,12,192]{2,1,0:T(8,128)(2,1)} %get-tuple-element.69.states, bf16[24,12,192]{2,1,0:T(8,128)(2,1)} %get-tuple-element.68.loss, s32[24,12,1]{2,1,0:T(8,128)} %copy.47.land), custom_call_target="tpu_custom_call" | custom-call | tf_op jit(solution)/shard_map/pack_cells/pallas_call | solution.py:276
  6.0 1.1 copy.48
  7.1 12.9 %all_to_all.30 = bf16[4,4,18,512]{3,1,2,0:T(4,128)(2,1)S(1)} all-to-all(bf16[4,4,18,512]{3,1,2,0:T(4,128)(2,1)S(1)} %copy.48), channel_id=1, replica_groups=mesh['section'=4,'lat'=8,'lon'=8] {'section'}, dimensions={0} | all-to-all | bytes 589824 | tf_op jit(solution)/shard_map/all_to_all | solution.py:268
  20.6 2.8 %collective-permute-start = (bf16[4,18,512]{2,1,0:T(8,128)(2,1)S(1)}, bf16[4,18,512]{2,1,0:T(8,128)(2,1)S(1)}, u32[]{:S(2)}, u32[]{:S(2)}) collective-permute-start(bf16[4,18,512]{2,1,0:T(8,128)(2,1)S(1)} %bitcast.43), channel_id=1, source_target_pairs={{0,7},{1,0},{2,1},{3,2},{4,3},{5,4},{6,5},{7,6},{8,15},{9,8},{10,9... | collective-permute-start | bytes 221192 | tf_op jit(solution)/shard_map/ppermute | solution.py:264
  24.3 5.3 %collective-permute-start.2 = (bf16[4,18,512]{2,1,0:T(8,128)(2,1)S(1)}, bf16[4,18,512]{2,1,0:T(8,128)(2,1)S(1)}, u32[]{:S(2)}, u32[]{:S(2)}) collective-permute-start(bf16[4,18,512]{2,1,0:T(8,128)(2,1)S(1)} %bitcast.41), channel_id=1, source_target_pairs={{0,255},{1,248},{2,249},{3,250},{4,251},{5,252},{6,253},{7,254},{8... | collective-permute-start | bytes 221192 | tf_op jit(solution)/shard_map/ppermute | solution.py:264
  29.5 0.9 copy.53.wdown
  31.8 10.3 %window_steps.1 = (bf16[4,4,18,192]{3,2,1,0:T(8,128)(2,1)}, bf16[4,880,128]{2,1,0:T(8,128)(2,1)}) custom-call(bf16[4,18,512]{2,1,0:T(8,128)(2,1)} %bitcast.39, bf16[4,18,512]{2,1,0:T(8,128)(2,1)} %copy-done.4, bf16[4,18,512]{2,1,0:T(8,128)(2,1)} %copy-done.5, bf16[4,18,512]{2,1,0:T(8,128)(2,1)} %copy-done.6, f32[1,192]{1,0:T(1,128)} %bitcast.48, ...), custom_call_target="tpu_custom_call" | custom-call | tf_op jit(solution)/shard_map/window_steps/pallas_call | solution.py:288
  42.1 19.5 %all_to_all.31 = bf16[4,880,128]{2,1,0:T(8,128)(2,1)S(1)} all-to-all(bf16[4,880,128]{2,1,0:T(8,128)(2,1)} %get-tuple-element.18), channel_id=1, replica_groups=mesh['section'=4,'lat'=8,'lon'=8] {'section'}, dimensions={0} | all-to-all | bytes 1802240 | tf_op jit(solution)/shard_map/all_to_all | solution.py:268
  61.9 19.1 %all_to_all.32 = bf16[64,16,128]{2,1,0:T(8,128)(2,1)S(1)} all-to-all(bf16[64,16,128]{2,1,0:T(8,128)(2,1)S(1)} %bitcast.37), channel_id=1, replica_groups=mesh['section'=4,'lat'=8,'lon'=8] {'lat','lon'}, dimensions={0} | all-to-all | bytes 524288 | tf_op jit(solution)/shard_map/all_to_all | solution.py:268
  81.8 6.8 %all-to-all-start.3 = ((bf16[64,16,128]{2,1,0:T(8,128)(2,1)}), bf16[64,16,128]{2,1,0:T(8,128)(2,1)S(1)}, u32[]{:S(2)}, u32[]{:S(2)}) async-start(bf16[64,16,128]{2,1,0:T(8,128)(2,1)} %broadcast_in_dim.33), calls=%async_computation.3 | async-start | bytes 524288 | tf_op jit(solution)/shard_map/all_to_all | solution.py:268
  88.6 3.2 %collective-permute-start.3 = (bf16[4,18,192]{2,1,0:T(8,128)(2,1)S(1)}, bf16[4,18,192]{2,1,0:T(8,128)(2,1)S(1)}, u32[]{:S(2)}, u32[]{:S(2)}) collective-permute-start(bf16[4,18,192]{2,1,0:T(8,128)(2,1)S(1)} %get-tuple-element.64), channel_id=1, source_target_pairs={{0,65},{1,66},{2,67},{3,68},{4,69},{5,70},{6,71},{7,64},{8,73},{9,... | collective-permute-start | bytes 82952 | tf_op jit(solution)/shard_map/ppermute | solution.py:264
  91.8 1.2 collective-permute-start.5
  93.0 3.4 %collective-permute-done.3 = bf16[4,18,192]{2,1,0:T(8,128)(2,1)S(1)} collective-permute-done((bf16[4,18,192]{2,1,0:T(8,128)(2,1)S(1)}, bf16[4,18,192]{2,1,0:T(8,128)(2,1)S(1)}, u32[]{:S(2)}, u32[]{:S(2)}) %collective-permute-start.3) | collective-permute-done | bytes 27680 | tf_op jit(solution)/shard_map/ppermute | solution.py:264
  96.4 1.7 %collective-permute-done.5 = bf16[4,18,192]{2,1,0:T(8,128)(2,1)S(1)} collective-permute-done((bf16[4,18,192]{2,1,0:T(8,128)(2,1)S(1)}, bf16[4,18,192]{2,1,0:T(8,128)(2,1)S(1)}, u32[]{:S(2)}, u32[]{:S(2)}) %collective-permute-start.5) | collective-permute-done | bytes 27680 | tf_op jit(solution)/shard_map/ppermute | solution.py:264
  99.2 6.9 %all-to-all-start.5 = ((bf16[4,4,18,192]{3,1,2,0:T(4,128)(2,1)}), bf16[4,4,18,192]{3,1,2,0:T(4,128)(2,1)S(1)}, u32[]{:S(2)}, u32[]{:S(2)}) async-start(bf16[4,4,18,192]{3,1,2,0:T(4,128)(2,1)} %copy.54), calls=%async_computation.5 | async-start | bytes 294912 | tf_op jit(solution)/shard_map/all_to_all | solution.py:268
  106.1 5.2 %all-to-all-done.5 = bf16[4,4,18,192]{3,1,2,0:T(4,128)(2,1)S(1)} async-done(((bf16[4,4,18,192]{3,1,2,0:T(4,128)(2,1)}), bf16[4,4,18,192]{3,1,2,0:T(4,128)(2,1)S(1)}, u32[]{:S(2)}, u32[]{:S(2)}) %all-to-all-start.5) | async-done | bytes 110624 | tf_op jit(solution)/shard_map/all_to_all | solution.py:268
  111.3 1.0 broadcast_in_dim.35
  112.3 4.6 %all-to-all-start.4 = ((bf16[4,880,128]{2,1,0:T(8,128)(2,1)}), bf16[4,880,128]{2,1,0:T(8,128)(2,1)S(1)}, u32[]{:S(2)}, u32[]{:S(2)}) async-start(bf16[4,880,128]{2,1,0:T(8,128)(2,1)} %broadcast_in_dim.35), calls=%async_computation.4 | async-start | bytes 1802240 | tf_op jit(solution)/shard_map/all_to_all | solution.py:268
  117.6 12.8 %all-to-all-done.4.msg = bf16[4,880,128]{2,1,0:T(8,128)(2,1)S(1)} async-done(((bf16[4,880,128]{2,1,0:T(8,128)(2,1)}), bf16[4,880,128]{2,1,0:T(8,128)(2,1)S(1)}, u32[]{:S(2)}, u32[]{:S(2)}) %all-to-all-start.4) | async-done | bytes 901152 | tf_op jit(solution)/shard_map/all_to_all | solution.py:268
  131.3 2.8 %unpack_sums.1 = (f32[24,12,192]{2,1,0:T(8,128)}, f32[192,576]{1,0:T(8,128)}, f32[192,192]{1,0:T(8,128)}, f32[192,768]{1,0:T(8,128)}, f32[768,192]{1,0:T(8,128)}...) custom-call(bf16[4,880,128]{2,1,0:T(8,128)(2,1)} %copy-done, bf16[4,4,18,192]{3,2,1,0:T(8,128)(2,1)} %copy.55.grads), custom_call_target="tpu_custom_call" | custom-call | tf_op jit(solution)/shard_map/unpack_sums/pallas_call | solution.py:335
  134.1 1.9 %copy.56 = f32[1,1,24,12,192]{4,2,3,1,0:T(8,128)} copy(f32[1,1,24,12,192]{4,3,2,1,0:T(8,128)} %bitcast.40) | data formatting | bytes 442368
  136.0 2.2 %copy.57 = f32[768,192]{0,1:T(8,128)} copy(f32[768,192]{1,0:T(8,128)} %get-tuple-element.56) | data formatting | bytes 1179648
  (35 shorter events, 6.5 us)
Async XLA Ops:
  0.6 1.6 %copy-start.3 = (bf16[1,1,24,12,192]{4,2,3,1,0:T(8,128)(2,1)S(1)}, bf16[1,1,24,12,192]{4,2,3,1,0:T(8,128)(2,1)}, u32[]{:S(2)}) copy-start(bf16[1,1,24,12,192]{4,2,3,1,0:T(8,128)(2,1)} %param.11) | copy-start | bytes 331780
  20.5 9.0 %copy-start.1 = (bf16[768,192]{0,1:T(8,128)(2,1)S(1)}, bf16[768,192]{0,1:T(8,128)(2,1)}, u32[]{:S(2)}) copy-start(bf16[768,192]{0,1:T(8,128)(2,1)} %param.19) | copy-start | bytes 884740
  20.6 10.5 %collective-permute-start = (bf16[4,18,512]{2,1,0:T(8,128)(2,1)S(1)}, bf16[4,18,512]{2,1,0:T(8,128)(2,1)S(1)}, u32[]{:S(2)}, u32[]{:S(2)}) collective-permute-start(bf16[4,18,512]{2,1,0:T(8,128)(2,1)S(1)} %bitcast.43), channel_id=1, source_target_pairs={{0,7},{1,0},{2,1},{3,2},{4,3},{5,4},{6,5},{7,6},{8,15},{9,8},{10,9... | collective-permute-start | bytes 221192 | tf_op jit(solution)/shard_map/ppermute | solution.py:264
  23.4 7.7 %collective-permute-start.1 = (bf16[4,18,512]{2,1,0:T(8,128)(2,1)S(1)}, bf16[4,18,512]{2,1,0:T(8,128)(2,1)S(1)}, u32[]{:S(2)}, u32[]{:S(2)}) collective-permute-start(bf16[4,18,512]{2,1,0:T(8,128)(2,1)S(1)} %bitcast.42), channel_id=1, source_target_pairs={{0,248},{1,249},{2,250},{3,251},{4,252},{5,253},{6,254},{7,255},{8... | collective-permute-start | bytes 221192 | tf_op jit(solution)/shard_map/ppermute | solution.py:264
  24.3 6.9 %collective-permute-start.2 = (bf16[4,18,512]{2,1,0:T(8,128)(2,1)S(1)}, bf16[4,18,512]{2,1,0:T(8,128)(2,1)S(1)}, u32[]{:S(2)}, u32[]{:S(2)}) collective-permute-start(bf16[4,18,512]{2,1,0:T(8,128)(2,1)S(1)} %bitcast.41), channel_id=1, source_target_pairs={{0,255},{1,248},{2,249},{3,250},{4,251},{5,252},{6,253},{7,254},{8... | collective-permute-start | bytes 221192 | tf_op jit(solution)/shard_map/ppermute | solution.py:264
  31.1 0.6 copy-start.4
  31.1 0.7 copy-start.5
  31.2 0.6 copy-start.6
  81.8 6.8 %copy-start.2 = (bf16[4,4,18,192]{3,2,1,0:T(8,128)(2,1)S(1)}, bf16[4,4,18,192]{3,2,1,0:T(8,128)(2,1)}, u32[]{:S(2)}) copy-start(bf16[4,4,18,192]{3,2,1,0:T(8,128)(2,1)} %get-tuple-element.19) | copy-start | bytes 331780
  81.8 17.4 %all-to-all-start.3 = ((bf16[64,16,128]{2,1,0:T(8,128)(2,1)}), bf16[64,16,128]{2,1,0:T(8,128)(2,1)S(1)}, u32[]{:S(2)}, u32[]{:S(2)}) async-start(bf16[64,16,128]{2,1,0:T(8,128)(2,1)} %broadcast_in_dim.33), calls=%async_computation.3 | async-start | bytes 524288 | tf_op jit(solution)/shard_map/all_to_all | solution.py:268
  88.6 7.7 %collective-permute-start.3 = (bf16[4,18,192]{2,1,0:T(8,128)(2,1)S(1)}, bf16[4,18,192]{2,1,0:T(8,128)(2,1)S(1)}, u32[]{:S(2)}, u32[]{:S(2)}) collective-permute-start(bf16[4,18,192]{2,1,0:T(8,128)(2,1)S(1)} %get-tuple-element.64), channel_id=1, source_target_pairs={{0,65},{1,66},{2,67},{3,68},{4,69},{5,70},{6,71},{7,64},{8,73},{9,... | collective-permute-start | bytes 82952 | tf_op jit(solution)/shard_map/ppermute | solution.py:264
  91.8 6.2 %collective-permute-start.5 = (bf16[4,18,192]{2,1,0:T(8,128)(2,1)S(1)}, bf16[4,18,192]{2,1,0:T(8,128)(2,1)S(1)}, u32[]{:S(2)}, u32[]{:S(2)}) collective-permute-start(bf16[4,18,192]{2,1,0:T(8,128)(2,1)S(1)} %get-tuple-element.66), channel_id=1, source_target_pairs={{0,1},{1,2},{2,3},{3,4},{4,5},{5,6},{6,7},{7,0},{8,9},{9,10},{10,1... | collective-permute-start | bytes 82952 | tf_op jit(solution)/shard_map/ppermute | solution.py:264
  93.0 5.1 %collective-permute-start.4 = (bf16[4,18,192]{2,1,0:T(8,128)(2,1)S(1)}, bf16[4,18,192]{2,1,0:T(8,128)(2,1)S(1)}, u32[]{:S(2)}, u32[]{:S(2)}) collective-permute-start(bf16[4,18,192]{2,1,0:T(8,128)(2,1)S(1)} %get-tuple-element.67), channel_id=1, source_target_pairs={{0,64},{1,65},{2,66},{3,67},{4,68},{5,69},{6,70},{7,71},{8,72},{9,... | collective-permute-start | bytes 82952 | tf_op jit(solution)/shard_map/ppermute | solution.py:264
  99.2 12.1 %all-to-all-start.5 = ((bf16[4,4,18,192]{3,1,2,0:T(4,128)(2,1)}), bf16[4,4,18,192]{3,1,2,0:T(4,128)(2,1)S(1)}, u32[]{:S(2)}, u32[]{:S(2)}) async-start(bf16[4,4,18,192]{3,1,2,0:T(4,128)(2,1)} %copy.54), calls=%async_computation.5 | async-start | bytes 294912 | tf_op jit(solution)/shard_map/all_to_all | solution.py:268
  112.3 18.1 %all-to-all-start.4 = ((bf16[4,880,128]{2,1,0:T(8,128)(2,1)}), bf16[4,880,128]{2,1,0:T(8,128)(2,1)S(1)}, u32[]{:S(2)}, u32[]{:S(2)}) async-start(bf16[4,880,128]{2,1,0:T(8,128)(2,1)} %broadcast_in_dim.35), calls=%async_computation.4 | async-start | bytes 1802240 | tf_op jit(solution)/shard_map/all_to_all | solution.py:268
  130.4 0.9 copy-start

commit v2 on v1

v2 whole, which is shorter than its diff:
```python
import jax
import jax.numpy as jnp
from jax import lax
from jax.experimental import pallas as pl
from jax.experimental.pallas import tpu as pltpu
from jax.sharding import Mesh
from jax.sharding import PartitionSpec as P

CH = 192
HEADS = 6
HEAD_DIM = 32
MLP = 768
ROWS = 24
WIN_LAT = 6
WIN_LON = 12
WIN = WIN_LAT * WIN_LON
HALF = WIN // 2
STEPS = 4
TOK = STEPS * WIN
MSG = 512
EDGE = 8
GROUP = 16
UNIT = 112
SUMS = GROUP * UNIT
BLOCK = 48
QUARTER = 4 * BLOCK
SENT = SUMS + 2 * QUARTER
SCALE = HEAD_DIM ** (-0.5)
EPS = 1e-05
F32 = jnp.float32
BF16 = jnp.bfloat16
AXES = ("xh", "core", "lat", "lon")
MIB = 1024 * 1024


def nn(a, b):
    return lax.dot_general(a, b, (((1,), (0,)), ((), ())), preferred_element_type=F32)


def nt(a, b):
    return lax.dot_general(a, b, (((1,), (1,)), ((), ())), preferred_element_type=F32)


def tn(a, b):
    return lax.dot_general(a, b, (((0,), (0,)), ((), ())), preferred_element_type=F32)


def mean_of(v):
    return jnp.sum(v, axis=-1, keepdims=True) * (1.0 / CH)


def pack_kernel(states, loss, land, kept, to_lon, to_lat, to_both):
    mask = land[...].astype(F32)
    for c in range(WIN_LON):
        column = jnp.broadcast_to(mask[c : c + 1, :], (64, ROWS)).T
        cell = jnp.concatenate(
            [states[c].astype(F32), column, loss[c].astype(F32), column], axis=1
        )
        wide, edge = (to_lon, to_both) if c < 6 else (kept, to_lat)
        wide[c % 6] = cell.astype(BF16)
        edge[c % 6] = cell[0:EDGE].astype(BF16)


def window_kernel(kept, from_lon, from_lat, from_both, out, cells):
    for c in range(WIN_LON):
        wide, edge = (kept, from_lat) if c < 6 else (from_lon, from_both)
        column = wide[c % 6].astype(F32)
        after = edge[c % 6].astype(F32)
        for k in range(3):
            cells[k, 6 * c : 6 * c + 6, :] = column[6 * k + 3 : 6 * k + 9]
        cells[3, 6 * c : 6 * c + 3, :] = column[21:24]
        cells[3, 6 * c + 3 : 6 * c + 6, :] = after[0:3]
    out[...] = cells[...].astype(BF16)


def main_kernel(
    cells, embed, gain_a, gain_m, wqkv, wout, wup, wdown_t,
    send_out, keep_out,
    x, qkv, probs, qm_all, emb, xh1, r1, hid_xh, r2, gp, act, normed_s, mixed_s, nm_s,
    cot_s, dpre_s, dproj_s, dqkv_s, dstate, small, msg,
):
    core = lax.axis_index("core")
    third = jnp.logical_and(lax.axis_index("xh") == 1, core == 1)
    last = jnp.logical_and(lax.axis_index("lat") == 7, third)
    closed = jnp.where(last, 0.0, 1.0).astype(F32)
    for s in range(STEPS):
        x[WIN * s : WIN * s + WIN, :] = cells[s].astype(F32)
    le = embed[...]
    ga = gain_a[...]
    gm = gain_m[...]
    col_head = lax.broadcasted_iota(jnp.int32, (1, CH), 1) // HEAD_DIM
    masks = [(col_head == h).astype(F32) for h in range(HEADS)]
    row_half = lax.rem(lax.broadcasted_iota(jnp.int32, (WIN, WIN), 0), WIN_LAT) // 3
    key_half = lax.rem(lax.broadcasted_iota(jnp.int32, (WIN, WIN), 1), WIN_LAT) // 3
    allow1 = jnp.where(row_half == key_half, 1.0, closed).astype(F32)
    allow = jnp.concatenate([allow1] * HEADS, axis=0)

    def spread(v):
        return jnp.concatenate([v * m for m in masks], axis=0).astype(BF16)

    def gathered(v):
        total = v[0:WIN] * masks[0]
        for h in range(1, HEADS):
            total = total + v[WIN * h : WIN * h + WIN] * masks[h]
        return total

    for s in range(STEPS):
        rows = slice(WIN * s, WIN * s + WIN)
        land = x[rows, 192:256][:, 0:1]
        e = x[rows, 0:CH] + land * le
        emb[rows, :] = e
        off = e - mean_of(e)
        r = lax.rsqrt(mean_of(off * off) + EPS)
        xh = off * r
        xh1[rows, :] = xh
        r1[rows, :] = r
        normed_s[rows, :] = xh * ga
    normed = normed_s[...].astype(BF16)
    qkv[...] = nn(normed, wqkv[...]).astype(BF16).astype(F32)
    for s in range(STEPS):
        rows = slice(WIN * s, WIN * s + WIN)
        qm = spread(qkv[rows, 0:CH])
        qm_all[s] = qm
        keys = qkv[rows, CH : 2 * CH].astype(BF16)
        values = qkv[rows, 2 * CH : 3 * CH].astype(BF16)
        weights = jnp.exp(nt(qm, keys) * SCALE) * allow
        p = weights / jnp.sum(weights, axis=-1, keepdims=True)
        probs[s] = p
        mixed_s[rows, :] = gathered(nn(p.astype(BF16), values))
    mixed = mixed_s[...].astype(BF16)
    projected = nn(mixed, wout[...]).astype(BF16).astype(F32)
    hid = emb[...] + projected
    off = hid - mean_of(hid)
    r = lax.rsqrt(mean_of(off * off) + EPS)
    xh = off * r
    hid_xh[...] = xh
    r2[...] = r
    nm_s[...] = (xh * gm).astype(BF16)
    for j in range(MLP // 256):
        cols = slice(256 * j, 256 * j + 256)
        pre = nn(nm_s[...], wup[:, cols])
        cdf = 0.5 * (1.0 + lax.erf(pre * (0.5 ** 0.5)))
        pdf = jnp.exp(pre * pre * -0.5) * 0.3989422804014327
        act[:, cols] = (pre * cdf).astype(BF16)
        gp[:, cols] = cdf + pre * pdf

    gain_m_sum = jnp.zeros((1, CH), F32)
    gain_a_sum = jnp.zeros((1, CH), F32)
    land_sum = jnp.zeros((1, CH), F32)
    incoming = None
    wq = wqkv[:, 0:CH]
    wk = wqkv[:, CH : 2 * CH]
    wv = wqkv[:, 2 * CH : 3 * CH]
    zero_rows = jnp.zeros((BLOCK - HALF, 128), F32)
    dstate[...] = jnp.zeros_like(dstate)
    for s in range(STEPS - 1, -1, -1):
        rows = slice(WIN * s, WIN * s + WIN)
        cot = x[rows, 256:448]
        if incoming is not None:
            cot = cot + incoming
        cotb = cot.astype(BF16)
        cot_s[rows, :] = cotb.astype(F32)
        d_pre = gp[rows, :] * nn(cotb, wdown_t[...])
        dpre_b = d_pre.astype(BF16)
        dpre_s[rows, :] = dpre_b.astype(F32)
        dy = nt(dpre_b, wup[...])
        xh = hid_xh[rows, :]
        gain_m_sum = gain_m_sum + jnp.sum(dy * xh, axis=0, keepdims=True)
        dxh = dy * gm
        d_hid = cot + r2[rows, :] * (dxh - mean_of(dxh) - xh * mean_of(dxh * xh))
        dproj = d_hid.astype(BF16)
        dproj_s[rows, :] = dproj.astype(F32)
        d_mixed = nt(dproj, wout[...]).astype(BF16).astype(F32)
        dm = spread(d_mixed)
        keys = qkv[rows, CH : 2 * CH].astype(BF16)
        values = qkv[rows, 2 * CH : 3 * CH].astype(BF16)
        p = probs[s]
        dp = nt(dm, values)
        dv = tn(p.astype(BF16), dm).astype(BF16)
        ds = (p * (dp - jnp.sum(p * dp, axis=-1, keepdims=True)) * SCALE).astype(BF16)
        dq = gathered(nn(ds, keys)).astype(BF16)
        dk = tn(ds, qm_all[s]).astype(BF16)
        dqkv_s[rows, 0:CH] = dq.astype(F32)
        dqkv_s[rows, CH : 2 * CH] = dk.astype(F32)
        dqkv_s[rows, 2 * CH : 3 * CH] = dv.astype(F32)
        d_rolled = nt(dq, wq) + nt(dk, wk) + nt(dv, wv)
        dy = d_rolled.astype(BF16).astype(F32)
        xh = xh1[rows, :]
        gain_a_sum = gain_a_sum + jnp.sum(dy * xh, axis=0, keepdims=True)
        dxh = dy * ga
        d_state = d_hid + r1[rows, :] * (dxh - mean_of(dxh) - xh * mean_of(dxh * xh))
        land = x[rows, 192:256][:, 0:1]
        land_sum = land_sum + jnp.sum(d_state * land, axis=0, keepdims=True)
        incoming = d_state.astype(BF16).astype(F32)
        dstate[:, 0:CH] = incoming
        for half in range(2):
            piece = dstate[HALF * half : HALF * half + HALF, :]
            for tile in range(2):
                at = SUMS + QUARTER * (s // 2) + BLOCK * (2 * half + tile)
                block = jnp.concatenate([piece[:, 128 * tile : 128 * tile + 128], zero_rows], axis=0)
                msg[s % 2, at : at + BLOCK, :] = block.astype(BF16)

    factor = float(STEPS * 192 * 96) ** (-0.5)

    def put(tile, value):
        for j in range(value.shape[1] // 128):
            start = (tile + j) * CH
            done = 0
            while done < CH:
                part, row = divmod(start + done, SUMS)
                n = min(CH - done, SUMS - row)
                msg[part, row : row + n, :] = value[done : done + n, 128 * j : 128 * j + 128]
                done += n

    cot_all = cot_s[...].astype(BF16)
    put(12, (tn(cot_all, act[...]) * factor).astype(BF16))
    put(6, (tn(nm_s[...], dpre_s[...].astype(BF16)) * factor).astype(BF16))
    g_qkv = tn(normed_s[...].astype(BF16), dqkv_s[...].astype(BF16)) * factor
    g_out = tn(mixed_s[...].astype(BF16), dproj_s[...].astype(BF16)) * factor
    put(0, jnp.concatenate([g_qkv, g_out], axis=1).astype(BF16))
    small[...] = jnp.zeros_like(small)
    for i, total in enumerate((land_sum, gain_a_sum, gain_m_sum)):
        total = total * factor
        small[2 * i : 2 * i + 1, :] = total[:, 0:128]
        small[2 * i + 1 : 2 * i + 2, 0:64] = total[:, 128:192]
    msg[1, 18 * CH - SUMS : SUMS, :] = small[...].astype(BF16)
    send_out[...] = msg[1 - core]
    keep_out[...] = msg[core]


SMALL_ROWS = 2 * SUMS - 18 * CH


def pair_kernel(kept, arrived, chunks, x_send, x_keep):
    core = lax.axis_index("core")
    here = lax.axis_index("xh")
    for g in range(GROUP):
        at = UNIT * g
        total = kept[at : at + UNIT, :].astype(F32) + arrived[at : at + UNIT, :].astype(F32)
        chunks[g] = total.astype(BF16)
    own = pl.ds(pl.multiple_of(SUMS + QUARTER * here, 64), QUARTER)
    other = pl.ds(pl.multiple_of(SUMS + QUARTER * (1 - here), 64), QUARTER)
    x_send[core] = kept[other, :]
    x_send[1 - core] = arrived[other, :]
    x_keep[core] = kept[own, :]
    x_keep[1 - core] = arrived[own, :]


def group_kernel(terms, kept, arrived, total_out, near, to_lon, to_lat, to_both):
    here = lax.axis_index("xh")
    total = terms[0].astype(F32)
    for g in range(1, GROUP):
        total = total + terms[g].astype(F32)
    total = total.astype(BF16)
    for g in range(8):
        total_out[g] = total
    half = QUARTER // 2
    for c in range(2):
        near[2 * here + c] = kept[c, 0:half, :]
        near[2 * (1 - here) + c] = arrived[c, 0:half, :]
        to_lon[2 * here + c] = kept[c, half:QUARTER, :]
        to_lon[2 * (1 - here) + c] = arrived[c, half:QUARTER, :]
    to_lat[...] = near[3]
    to_both[...] = to_lon[3]


def column_kernel(terms, total_out):
    total = terms[0].astype(F32)
    for g in range(1, 8):
        total = total + terms[g].astype(F32)
    total = total.astype(BF16)
    for g in range(GROUP):
        total_out[g] = total


def unpack_kernel(
    own, other, near, from_lon, from_lat, from_both,
    state_out, g_qkv, g_out, g_up, g_down, g_land, g_ga, g_gm, msg,
):
    core = lax.axis_index("core")
    for g in range(GROUP):
        msg[core, UNIT * g : UNIT * g + UNIT, :] = own[g]
        msg[1 - core, UNIT * g : UNIT * g + UNIT, :] = other[g]

    def rows_of(start, count):
        pieces = []
        done = 0
        while done < count:
            part, row = divmod(start + done, SUMS)
            n = min(count - done, SUMS - row)
            pieces.append(msg[part, row : row + n, :].astype(F32))
            done += n
        return pieces[0] if len(pieces) == 1 else jnp.concatenate(pieces, axis=0)

    for j in range(4):
        g_qkv[:, 128 * j : 128 * j + 128] = rows_of(j * CH, CH)
    mid = rows_of(4 * CH, CH)
    tail = rows_of(5 * CH, CH)
    g_qkv[:, 512:576] = mid[:, 0:64]
    g_out[...] = jnp.concatenate([mid[:, 64:128], tail], axis=1)
    for j in range(6):
        g_up[:, 128 * j : 128 * j + 128] = rows_of((6 + j) * CH, CH)
        g_down[:, 128 * j : 128 * j + 128] = rows_of((12 + j) * CH, CH)
    little = rows_of(18 * CH, 16)
    for i, out in enumerate((g_land, g_ga, g_gm)):
        out[...] = jnp.concatenate(
            [little[2 * i : 2 * i + 1, :], little[2 * i + 1 : 2 * i + 2, 0:64]], axis=1
        )
    for first, wide, edge in ((6, near, from_lat), (0, from_lon, from_both)):
        for tile, lanes in ((0, slice(0, 128)), (1, slice(128, 192))):
            n = lanes.stop - lanes.start
            at = slice(BLOCK * tile, BLOCK * tile + BLOCK)
            before = edge[at, :].astype(F32)
            for c in range(6):
                state_out[first + c, 0:3, lanes] = before[6 * c + 3 : 6 * c + 6, 0:n]
            for k in range(4):
                block = wide[k, at, :].astype(F32)
                tall = 6 if k < 3 else 3
                for c in range(6):
                    state_out[first + c, 6 * k + 3 : 6 * k + 3 + tall, lanes] = block[
                        6 * c : 6 * c + tall, 0:n
                    ]


def hop(value, rows, cols):
    pairs = []
    for k in range(4):
        for a in range(8):
            for b in range(8):
                to = (k * 8 + (a + rows) % 8) * 8 + (b + cols) % 8
                pairs.append(((k * 8 + a) * 8 + b, to))
    return lax.ppermute(value, AXES, pairs)


def swap(value, axis):
    return lax.ppermute(value, axis, [(0, 1), (1, 0)])


def exchange(value, axis):
    return lax.all_to_all(value, axis, 0, 0, tiled=True)


def call(kernel, name, outs, scratch=(), mib=8):
    return pl.pallas_call(
        kernel,
        out_shape=tuple(jax.ShapeDtypeStruct(dims, kind) for dims, kind in outs),
        scratch_shapes=[pltpu.VMEM(dims, kind) for dims, kind in scratch],
        compiler_params=pltpu.CompilerParams(vmem_limit_bytes=mib * MIB),
        name=name,
    )


def local(
    states, loss_grads, land_sea, land_embed, gain_attn, gain_mlp, w_qkv, w_out, w_up, w_down
):
    kept, to_lon, to_lat, to_both = call(
        pack_kernel,
        "pack_cells",
        [((6, ROWS, MSG), BF16)] * 2 + [((6, EDGE, MSG), BF16)] * 2,
    )(states[0, 0].transpose(1, 0, 2), loss_grads[0, 0].transpose(1, 0, 2), land_sea.T)
    from_lon = hop(to_lon, 0, -1)
    from_lat = hop(to_lat, -1, 0)
    from_both = hop(to_both, -1, -1)
    (packed,) = call(
        window_kernel, "cut_windows", [((4, WIN, MSG), BF16)], [((4, WIN, MSG), F32)]
    )(kept, from_lon, from_lat, from_both)
    cells = exchange(packed, ("xh", "core"))
    send, keep = call(
        main_kernel,
        "window_steps",
        [((SENT, 128), BF16)] * 2,
        [
            ((TOK, MSG), F32),
            ((TOK, 3 * CH), F32),
            ((STEPS, HEADS * WIN, WIN), F32),
            ((STEPS, HEADS * WIN, CH), BF16),
            ((TOK, CH), F32),
            ((TOK, CH), F32),
            ((TOK, 1), F32),
            ((TOK, CH), F32),
            ((TOK, 1), F32),
            ((TOK, MLP), F32),
            ((TOK, MLP), BF16),
            ((TOK, CH), F32),
            ((TOK, CH), F32),
            ((TOK, CH), BF16),
            ((TOK, CH), F32),
            ((TOK, MLP), F32),
            ((TOK, CH), F32),
            ((TOK, 3 * CH), F32),
            ((WIN, 256), F32),
            ((SMALL_ROWS, 128), F32),
            ((2, SENT, 128), BF16),
        ],
        mib=24,
    )(
        cells, land_embed[None], gain_attn[None], gain_mlp[None], w_qkv, w_out, w_up, w_down.T
    )

    chunks, x_send, x_keep = call(
        pair_kernel,
        "sum_cores",
        [((GROUP, UNIT, 128), BF16)] + [((2, QUARTER, 128), BF16)] * 2,
    )(keep, swap(send, "core"))
    x_arrived = swap(x_send, "xh")
    terms = exchange(chunks, ("xh", "lon"))
    partial, near, to_lon, to_lat, to_both = call(
        group_kernel,
        "sum_group",
        [((8, UNIT, 128), BF16)]
        + [((4, QUARTER // 2, 128), BF16)] * 2
        + [((QUARTER // 2, 128), BF16)] * 2,
    )(terms, x_keep, x_arrived)
    from_lon = hop(to_lon, 0, 1)
    from_lat = hop(to_lat, 1, 0)
    from_both = hop(to_both, 1, 1)
    terms, from_lon, from_lat, from_both = lax.optimization_barrier(
        (exchange(partial, "lat"), from_lon, from_lat, from_both)
    )
    (total,) = call(column_kernel, "sum_column", [((GROUP, UNIT, 128), BF16)])(terms)
    own = exchange(total, ("xh", "lon"))
    outs = call(
        unpack_kernel,
        "unpack_sums",
        [
            ((WIN_LON, ROWS, CH), F32),
            ((CH, 3 * CH), F32),
            ((CH, CH), F32),
            ((CH, MLP), F32),
            ((CH, MLP), F32),
            ((1, CH), F32),
            ((1, CH), F32),
            ((1, CH), F32),
        ],
        [((2, SUMS, 128), BF16)],
        mib=16,
    )(own, swap(own, "core"), near, from_lon, from_lat, from_both)
    return (
        outs[0].transpose(1, 0, 2)[None, None],
        outs[1], outs[2], outs[3], outs[4].T, outs[5][0], outs[6][0], outs[7][0],
    )


def solution(mesh):
    halves = Mesh(mesh.devices.reshape(2, 2, *mesh.devices.shape[1:]), AXES)
    cell = P(("xh", "core"), None, "lat", "lon", None)
    return jax.shard_map(
        local,
        mesh=halves,
        in_specs=(cell, cell, P("lat", "lon"), P(), P(), P(), P(), P(), P(), P()),
        out_specs=(cell, P(), P(), P(), P(), P(), P(), P()),
        check_vma=False,
    )
```

time: 139 us -> 91.6 us (0.66)
  blocking collectives: 51.6 us -> 25.3 us
  local copies, waits for them, and re-layouts: 15.4 us -> 3.18 us
  waiting for transfers between devices: 23.4 us -> 19.3 us
  Pallas kernels: 15.2 us -> 11.6 us
    all_to_all x3 -> x2, blocking collectives: 51.6 us -> 25.3 us  [exchange(): return lax.all_to_all(value, axis, 0, 0, tiled=True)]
    all_to_all x3 -> x2, waiting for transfers between devices: 18.3 us -> 0.01 us  [exchange(): return lax.all_to_all(value, axis, 0, 0, tiled=True)]
    ppermute x6 -> x9, waiting for transfers between devices: 5.09 us -> 19.3 us  [the longest x3 10.5 us: swap(): return lax.ppermute(value, axis, [(0, 1), (1, 0)])]
    all_to_all x3 -> x2, starting transfers between devices: 18.2 us -> 6.97 us  [exchange(): return lax.all_to_all(value, axis, 0, 0, tiled=True)]
    ppermute x6 -> x9, starting transfers between devices: 13.3 us -> 24 us  [the longest x6 15.7 us: hop(): return lax.ppermute(value, AXES, pairs)]
    unnamed x21 -> x20, local copies, waits for them, and re-layouts: 7.28 us -> 3.18 us
    pallas_call x3 -> x7, Pallas kernels: 15.2 us -> 11.6 us  [the longest x1 8.08 us: local(): call(main_kernel, 'window_steps', [((SENT, 128), BF16)] * 2, [((TOK, MSG)...]
    broadcast_in_dim x3 -> x0, local copies, waits for them, and re-layouts: 3.35 us -> none  [the longest x1 1.58 us: local(): land_sea[..., None]]
  transfers between devices with their start and end apart: 9 -> 11, of which waited for: 5 -> 7; matrix products, arithmetic and copies ran while one was open for 2% -> 0% of each run, Pallas kernels for 0% -> 0%
where the time goes in v2:
time: 91.6 us; the launch traced here: 91.1 us
  starting transfers between devices  30.9 us (34%)
  blocking collectives  25.3 us (28%)
  waiting for transfers between devices  19.3 us (21%)
  Pallas kernels  11.6 us (13%)
  local copies, waits for them, and re-layouts  3.18 us (3%)
    all_to_all x2, blocking collectives, exchange(): return lax.all_to_all(value, axis, 0, 0, tiled=True)  25.3 us
    ppermute x6, starting transfers between devices, hop(): return lax.ppermute(value, AXES, pairs)  15.7 us
    ppermute x3, waiting for transfers between devices, swap(): return lax.ppermute(value, axis, [(0, 1), (1, 0)])  10.5 us
    ppermute x6, waiting for transfers between devices, hop(): return lax.ppermute(value, AXES, pairs)  8.79 us
    ppermute x3, starting transfers between devices, swap(): return lax.ppermute(value, axis, [(0, 1), (1, 0)])  8.24 us
    pallas_call x1, Pallas kernels, local(): call(main_kernel, 'window_steps', [((SENT, 128), BF16)] * 2, [((TOK, MSG)...  8.08 us
    all_to_all x2, starting transfers between devices, exchange(): return lax.all_to_all(value, axis, 0, 0, tiled=True)  6.97 us
    unnamed x20, local copies, waits for them, and re-layouts  3.18 us
  transfers between devices with their start and end apart: 11, of which 7 were waited for; matrix products, arithmetic and copies ran while one was open for 0% of the time, Pallas kernels for 0%

profile of v2, /device:TPU:1, one launch (start us, length us, event | category | flops | bytes accessed | tf_op | source)
XLA Modules:
  0.0 91.1 jit_solution(12724459983567525224)
XLA Ops:
  0.6 0.9 copy-done.3
  1.5 0.9 copy-done.4
  3.4 4.6 %collective-permute-start = (bf16[6,24,512]{2,1,0:T(8,128)(2,1)S(1)}, bf16[6,24,512]{2,1,0:T(8,128)(2,1)S(1)}, u32[]{:S(2)}, u32[]{:S(2)}) collective-permute-start(bf16[6,24,512]{2,1,0:T(8,128)(2,1)S(1)} %get-tuple-element.35), channel_id=1, source_target_pairs={{0,7},{1,0},{2,1},{3,2},{4,3},{5,4},{6,5},{7,6},{8,15},{9,8},{10,9... | collective-permute-start | bytes 442376 | tf_op jit(solution)/shard_map/ppermute | solution.py:332
  8.0 5.6 %collective-permute-start.1 = (bf16[6,8,512]{2,1,0:T(8,128)(2,1)S(1)}, bf16[6,8,512]{2,1,0:T(8,128)(2,1)S(1)}, u32[]{:S(2)}, u32[]{:S(2)}) collective-permute-start(bf16[6,8,512]{2,1,0:T(8,128)(2,1)S(1)} %get-tuple-element.36), channel_id=1, source_target_pairs={{0,56},{1,57},{2,58},{3,59},{4,60},{5,61},{6,62},{7,63},{8,0},{9,1... | collective-permute-start | bytes 147464 | tf_op jit(solution)/shard_map/ppermute | solution.py:332
  13.6 0.9 collective-permute-start.2
  14.8 2.7 %collective-permute-done.2.from_both = bf16[6,8,512]{2,1,0:T(8,128)(2,1)S(1)} collective-permute-done((bf16[6,8,512]{2,1,0:T(8,128)(2,1)S(1)}, bf16[6,8,512]{2,1,0:T(8,128)(2,1)S(1)}, u32[]{:S(2)}, u32[]{:S(2)}) %collective-permute-start.2) | collective-permute-done | bytes 49184 | tf_op jit(solution)/shard_map/ppermute | solution.py:332
  17.6 13.6 %all_to_all.20.cells = bf16[4,72,512]{2,1,0:T(8,128)(2,1)S(1)} all-to-all(bf16[4,72,512]{2,1,0:T(8,128)(2,1)S(1)} %cut_windows.1), channel_id=1, replica_groups=mesh['xh'=2,'core'=2,'lat'=8,'lon'=8] {'xh','core'}, dimensions={0} | all-to-all | bytes 589824 | tf_op jit(solution)/shard_map/all_to_all | solution.py:340
  31.9 8.1 %window_steps.1 = (bf16[2176,128]{1,0:T(8,128)(2,1)S(1)}, bf16[2176,128]{1,0:T(8,128)(2,1)S(1)}) custom-call(bf16[4,72,512]{2,1,0:T(8,128)(2,1)S(1)} %all_to_all.20.cells, f32[1,192]{1,0:T(1,128)S(1)} %bitcast.22, f32[1,192]{1,0:T(1,128)S(1)} %bitcast.23, f32[1,192]{1,0:T(1,128)S(1)} %bitcast.24, bf16[192,576]{1,0:T(8,128)(2,1)S(1)} %copy-done.2, ...), custom_call_target="tpu_custom_call" | custom-call | tf_op jit(solution)/shard_map/window_steps/pallas_call | solution.py:368
  40.7 1.6 %collective-permute-done.3.arrived = bf16[2176,128]{1,0:T(8,128)(2,1)S(1)} collective-permute-done((bf16[2176,128]{1,0:T(8,128)(2,1)S(1)}, bf16[2176,128]{1,0:T(8,128)(2,1)S(1)}, u32[]{:S(2)}, u32[]{:S(2)}) %collective-permute-start.3) | collective-permute-done | bytes 557088 | tf_op jit(solution)/shard_map/ppermute | solution.py:336
  42.2 0.9 sum_cores.1
  43.1 3.6 %all-to-all-start.1 = ((bf16[16,112,128]{2,1,0:T(8,128)(2,1)}), bf16[16,112,128]{2,1,0:T(8,128)(2,1)S(1)}, u32[]{:S(2)}, u32[]{:S(2)}) async-start(bf16[16,112,128]{2,1,0:T(8,128)(2,1)} %get-tuple-element.40), calls=%async_computation.1 | async-start | bytes 917504 | tf_op jit(solution)/shard_map/all_to_all | solution.py:340
  46.7 2.8 %collective-permute-start.4 = (bf16[2,192,128]{2,1,0:T(8,128)(2,1)S(1)}, bf16[2,192,128]{2,1,0:T(8,128)(2,1)S(1)}, u32[]{:S(2)}, u32[]{:S(2)}) collective-permute-start(bf16[2,192,128]{2,1,0:T(8,128)(2,1)S(1)} %get-tuple-element.42), channel_id=1, source_target_pairs={{0,128},{128,0},{1,129},{129,1},{2,130},{130,2},{3,131},{131,3},{4... | collective-permute-start | bytes 294920 | tf_op jit(solution)/shard_map/ppermute | solution.py:336
  49.5 7.5 %collective-permute-done.4.arrived = bf16[2,192,128]{2,1,0:T(8,128)(2,1)S(1)} collective-permute-done((bf16[2,192,128]{2,1,0:T(8,128)(2,1)S(1)}, bf16[2,192,128]{2,1,0:T(8,128)(2,1)S(1)}, u32[]{:S(2)}, u32[]{:S(2)}) %collective-permute-start.4) | collective-permute-done | bytes 98336 | tf_op jit(solution)/shard_map/ppermute | solution.py:336
  57.0 0.8 sum_group.1
  57.8 3.4 %all-to-all-start.2 = ((bf16[8,112,128]{2,1,0:T(8,128)(2,1)}), bf16[8,112,128]{2,1,0:T(8,128)(2,1)S(1)}, u32[]{:S(2)}, u32[]{:S(2)}) async-start(bf16[8,112,128]{2,1,0:T(8,128)(2,1)} %get-tuple-element.43), calls=%async_computation.2 | async-start | bytes 458752 | tf_op jit(solution)/shard_map/all_to_all | solution.py:340
  61.2 1.3 %collective-permute-start.5 = (bf16[4,96,128]{2,1,0:T(8,128)(2,1)S(1)}, bf16[4,96,128]{2,1,0:T(8,128)(2,1)S(1)}, u32[]{:S(2)}, u32[]{:S(2)}) collective-permute-start(bf16[4,96,128]{2,1,0:T(8,128)(2,1)S(1)} %get-tuple-element.44), channel_id=1, source_target_pairs={{0,1},{1,2},{2,3},{3,4},{4,5},{5,6},{6,7},{7,0},{8,9},{9,10},{10,1... | collective-permute-start | bytes 294920 | tf_op jit(solution)/shard_map/ppermute | solution.py:332
  62.5 1.3 %collective-permute-start.6 = (bf16[96,128]{1,0:T(8,128)(2,1)S(1)}, bf16[96,128]{1,0:T(8,128)(2,1)S(1)}, u32[]{:S(2)}, u32[]{:S(2)}) collective-permute-start(bf16[96,128]{1,0:T(8,128)(2,1)S(1)} %get-tuple-element.45), channel_id=1, source_target_pairs={{0,8},{1,9},{2,10},{3,11},{4,12},{5,13},{6,14},{7,15},{8,16},{9,17... | collective-permute-start | bytes 73736 | tf_op jit(solution)/shard_map/ppermute | solution.py:332
  63.7 2.1 %collective-permute-start.7 = (bf16[96,128]{1,0:T(8,128)(2,1)S(1)}, bf16[96,128]{1,0:T(8,128)(2,1)S(1)}, u32[]{:S(2)}, u32[]{:S(2)}) collective-permute-start(bf16[96,128]{1,0:T(8,128)(2,1)S(1)} %get-tuple-element.46), channel_id=1, source_target_pairs={{0,9},{1,10},{2,11},{3,12},{4,13},{5,14},{6,15},{7,8},{8,17},{9,18... | collective-permute-start | bytes 73736 | tf_op jit(solution)/shard_map/ppermute | solution.py:332
  65.8 0.9 collective-permute-done.6.from_lat
  66.8 4.9 %collective-permute-done.7.from_both = bf16[96,128]{1,0:T(8,128)(2,1)S(1)} collective-permute-done((bf16[96,128]{1,0:T(8,128)(2,1)S(1)}, bf16[96,128]{1,0:T(8,128)(2,1)S(1)}, u32[]{:S(2)}, u32[]{:S(2)}) %collective-permute-start.7) | collective-permute-done | bytes 24608 | tf_op jit(solution)/shard_map/ppermute | solution.py:332
  71.8 11.7 %all_to_all.21.own = bf16[16,112,128]{2,1,0:T(8,128)(2,1)S(1)} all-to-all(bf16[16,112,128]{2,1,0:T(8,128)(2,1)S(1)} %sum_column.1), channel_id=1, replica_groups=mesh['xh'=2,'core'=2,'lat'=8,'lon'=8] {'xh','lon'}, dimensions={0} | all-to-all | bytes 917504 | tf_op jit(solution)/shard_map/all_to_all | solution.py:340
  83.5 4.8 %collective-permute-start.8 = (bf16[16,112,128]{2,1,0:T(8,128)(2,1)S(1)}, bf16[16,112,128]{2,1,0:T(8,128)(2,1)S(1)}, u32[]{:S(2)}, u32[]{:S(2)}) collective-permute-start(bf16[16,112,128]{2,1,0:T(8,128)(2,1)S(1)} %all_to_all.21.own), channel_id=1, source_target_pairs={{0,64},{64,0},{1,65},{65,1},{2,66},{66,2},{3,67},{67,3},{4,68},{68... | collective-permute-start | bytes 1376264 | tf_op jit(solution)/shard_map/ppermute | solution.py:336
  88.3 1.4 %collective-permute-done.8.other = bf16[16,112,128]{2,1,0:T(8,128)(2,1)S(1)} collective-permute-done((bf16[16,112,128]{2,1,0:T(8,128)(2,1)S(1)}, bf16[16,112,128]{2,1,0:T(8,128)(2,1)S(1)}, u32[]{:S(2)}, u32[]{:S(2)}) %collective-permute-start.8) | collective-permute-done | bytes 458784 | tf_op jit(solution)/shard_map/ppermute | solution.py:336
  89.7 1.4 %unpack_sums.1 = (f32[12,24,192]{2,1,0:T(8,128)}, f32[192,576]{1,0:T(8,128)}, f32[192,192]{1,0:T(8,128)}, f32[192,768]{1,0:T(8,128)}, f32[192,768]{1,0:T(8,128)}...) custom-call(bf16[16,112,128]{2,1,0:T(8,128)(2,1)S(1)} %all_to_all.21.own, ...), custom_call_target="tpu_custom_call" | custom-call | tf_op jit(solution)/shard_map/unpack_sums/pallas_call | solution.py:422
  (27 shorter events, 2.7 us)
Async XLA Ops:
  0.6 0.9 copy-start.3
  1.5 0.9 copy-start.4
  2.5 0.7 copy-start.6
  3.4 14.0 %collective-permute-start = (bf16[6,24,512]{2,1,0:T(8,128)(2,1)S(1)}, bf16[6,24,512]{2,1,0:T(8,128)(2,1)S(1)}, u32[]{:S(2)}, u32[]{:S(2)}) collective-permute-start(bf16[6,24,512]{2,1,0:T(8,128)(2,1)S(1)} %get-tuple-element.35), channel_id=1, source_target_pairs={{0,7},{1,0},{2,1},{3,2},{4,3},{5,4},{6,5},{7,6},{8,15},{9,8},{10,9... | collective-permute-start | bytes 442376 | tf_op jit(solution)/shard_map/ppermute | solution.py:332
  8.0 6.8 %collective-permute-start.1 = (bf16[6,8,512]{2,1,0:T(8,128)(2,1)S(1)}, bf16[6,8,512]{2,1,0:T(8,128)(2,1)S(1)}, u32[]{:S(2)}, u32[]{:S(2)}) collective-permute-start(bf16[6,8,512]{2,1,0:T(8,128)(2,1)S(1)} %get-tuple-element.36), channel_id=1, source_target_pairs={{0,56},{1,57},{2,58},{3,59},{4,60},{5,61},{6,62},{7,63},{8,0},{9,1... | collective-permute-start | bytes 147464 | tf_op jit(solution)/shard_map/ppermute | solution.py:332
  13.6 3.8 %collective-permute-start.2 = (bf16[6,8,512]{2,1,0:T(8,128)(2,1)S(1)}, bf16[6,8,512]{2,1,0:T(8,128)(2,1)S(1)}, u32[]{:S(2)}, u32[]{:S(2)}) collective-permute-start(bf16[6,8,512]{2,1,0:T(8,128)(2,1)S(1)} %get-tuple-element.37), channel_id=1, source_target_pairs={{0,63},{1,56},{2,57},{3,58},{4,59},{5,60},{6,61},{7,62},{8,7},{9,0... | collective-permute-start | bytes 147464 | tf_op jit(solution)/shard_map/ppermute | solution.py:332
  17.4 13.8 %copy-start.2 = (bf16[192,576]{1,0:T(8,128)(2,1)S(1)}, bf16[192,576]{1,0:T(8,128)(2,1)}, u32[]{:S(2)}) copy-start(bf16[192,576]{1,0:T(8,128)(2,1)} %wqkv.1) | copy-start | bytes 663556
  17.4 13.8 %copy-start.5 = (bf16[192,192]{1,0:T(8,128)(2,1)S(1)}, bf16[192,192]{1,0:T(8,128)(2,1)}, u32[]{:S(2)}) copy-start(bf16[192,192]{1,0:T(8,128)(2,1)} %wout.1) | copy-start | bytes 221188
  17.6 13.7 %copy-start = (bf16[192,768]{1,0:T(8,128)(2,1)S(1)}, bf16[192,768]{1,0:T(8,128)(2,1)}, u32[]{:S(2)}) copy-start(bf16[192,768]{1,0:T(8,128)(2,1)} %wup.1) | copy-start | bytes 884740
  17.6 13.7 %copy-start.1 = (bf16[768,192]{0,1:T(8,128)(2,1)S(1)}, bf16[768,192]{0,1:T(8,128)(2,1)}, u32[]{:S(2)}) copy-start(bf16[768,192]{0,1:T(8,128)(2,1)} %param.19) | copy-start | bytes 884740
  17.6 13.7 %copy-start.8 = (f32[192]{0:T(256)S(1)}, f32[192]{0:T(256)}, u32[]{:S(2)}) copy-start(f32[192]{0:T(256)} %param.14) | copy-start | bytes 2308
  17.6 13.7 %copy-start.9 = (f32[192]{0:T(256)S(1)}, f32[192]{0:T(256)}, u32[]{:S(2)}) copy-start(f32[192]{0:T(256)} %param.15) | copy-start | bytes 2308
  31.2 0.7 copy-start.7
  40.0 2.2 %collective-permute-start.3 = (bf16[2176,128]{1,0:T(8,128)(2,1)S(1)}, bf16[2176,128]{1,0:T(8,128)(2,1)S(1)}, u32[]{:S(2)}, u32[]{:S(2)}) collective-permute-start(bf16[2176,128]{1,0:T(8,128)(2,1)S(1)} %get-tuple-element.39), channel_id=1, source_target_pairs={{0,64},{64,0},{1,65},{65,1},{2,66},{66,2},{3,67},{67,3},{4,68},{68... | collective-permute-start | bytes 1671176 | tf_op jit(solution)/shard_map/ppermute | solution.py:336
  43.1 13.9 %all-to-all-start.1 = ((bf16[16,112,128]{2,1,0:T(8,128)(2,1)}), bf16[16,112,128]{2,1,0:T(8,128)(2,1)S(1)}, u32[]{:S(2)}, u32[]{:S(2)}) async-start(bf16[16,112,128]{2,1,0:T(8,128)(2,1)} %get-tuple-element.40), calls=%async_computation.1 | async-start | bytes 917504 | tf_op jit(solution)/shard_map/all_to_all | solution.py:340
  46.7 10.3 %collective-permute-start.4 = (bf16[2,192,128]{2,1,0:T(8,128)(2,1)S(1)}, bf16[2,192,128]{2,1,0:T(8,128)(2,1)S(1)}, u32[]{:S(2)}, u32[]{:S(2)}) collective-permute-start(bf16[2,192,128]{2,1,0:T(8,128)(2,1)S(1)} %get-tuple-element.42), channel_id=1, source_target_pairs={{0,128},{128,0},{1,129},{129,1},{2,130},{130,2},{3,131},{131,3},{4... | collective-permute-start | bytes 294920 | tf_op jit(solution)/shard_map/ppermute | solution.py:336
  57.8 13.9 %all-to-all-start.2 = ((bf16[8,112,128]{2,1,0:T(8,128)(2,1)}), bf16[8,112,128]{2,1,0:T(8,128)(2,1)S(1)}, u32[]{:S(2)}, u32[]{:S(2)}) async-start(bf16[8,112,128]{2,1,0:T(8,128)(2,1)} %get-tuple-element.43), calls=%async_computation.2 | async-start | bytes 458752 | tf_op jit(solution)/shard_map/all_to_all | solution.py:340
  61.2 10.5 %collective-permute-start.5 = (bf16[4,96,128]{2,1,0:T(8,128)(2,1)S(1)}, bf16[4,96,128]{2,1,0:T(8,128)(2,1)S(1)}, u32[]{:S(2)}, u32[]{:S(2)}) collective-permute-start(bf16[4,96,128]{2,1,0:T(8,128)(2,1)S(1)} %get-tuple-element.44), channel_id=1, source_target_pairs={{0,1},{1,2},{2,3},{3,4},{4,5},{5,6},{6,7},{7,0},{8,9},{9,10},{10,1... | collective-permute-start | bytes 294920 | tf_op jit(solution)/shard_map/ppermute | solution.py:332
  62.5 4.3 %collective-permute-start.6 = (bf16[96,128]{1,0:T(8,128)(2,1)S(1)}, bf16[96,128]{1,0:T(8,128)(2,1)S(1)}, u32[]{:S(2)}, u32[]{:S(2)}) collective-permute-start(bf16[96,128]{1,0:T(8,128)(2,1)S(1)} %get-tuple-element.45), channel_id=1, source_target_pairs={{0,8},{1,9},{2,10},{3,11},{4,12},{5,13},{6,14},{7,15},{8,16},{9,17... | collective-permute-start | bytes 73736 | tf_op jit(solution)/shard_map/ppermute | solution.py:332
  63.7 8.0 %collective-permute-start.7 = (bf16[96,128]{1,0:T(8,128)(2,1)S(1)}, bf16[96,128]{1,0:T(8,128)(2,1)S(1)}, u32[]{:S(2)}, u32[]{:S(2)}) collective-permute-start(bf16[96,128]{1,0:T(8,128)(2,1)S(1)} %get-tuple-element.46), channel_id=1, source_target_pairs={{0,9},{1,10},{2,11},{3,12},{4,13},{5,14},{6,15},{7,8},{8,17},{9,18... | collective-permute-start | bytes 73736 | tf_op jit(solution)/shard_map/ppermute | solution.py:332
  83.5 6.2 %collective-permute-start.8 = (bf16[16,112,128]{2,1,0:T(8,128)(2,1)S(1)}, bf16[16,112,128]{2,1,0:T(8,128)(2,1)S(1)}, u32[]{:S(2)}, u32[]{:S(2)}) collective-permute-start(bf16[16,112,128]{2,1,0:T(8,128)(2,1)S(1)} %all_to_all.21.own), channel_id=1, source_target_pairs={{0,64},{64,0},{1,65},{65,1},{2,66},{66,2},{3,67},{67,3},{4,68},{68... | collective-permute-start | bytes 1376264 | tf_op jit(solution)/shard_map/ppermute | solution.py:336

commit v3 on v2

--- a/solution.py
+++ b/solution.py
@@ -18,7 +18,6 @@
 STEPS = 4
 TOK = STEPS * WIN
 MSG = 512
-EDGE = 8
 GROUP = 16
 UNIT = 112
 SUMS = GROUP * UNIT
@@ -49,45 +48,82 @@
     return jnp.sum(v, axis=-1, keepdims=True) * (1.0 / CH)
 
 
-def pack_kernel(states, loss, land, kept, to_lon, to_lat, to_both):
+def pack_kernel(
+    states_in, loss_in, land_in, embed_in, gain_a_in, gain_m_in,
+    keep_out, send_out, edge_out, vectors_out,
+    states, loss, land, vectors, cells, edges, sems,
+):
+    pairs = (
+        (states_in, states), (loss_in, loss), (land_in, land),
+        (embed_in, vectors.at[0:1]), (gain_a_in, vectors.at[1:2]), (gain_m_in, vectors.at[2:3]),
+    )
+    copies = [
+        pltpu.make_async_copy(source, target, sems.at[i])
+        for i, (source, target) in enumerate(pairs)
+    ]
+    for copy in copies:
+        copy.start()
+    for copy in copies:
+        copy.wait()
+    core = lax.axis_index("core")
     mask = land[...].astype(F32)
+    nothing = jnp.zeros((3, MSG), F32)
     for c in range(WIN_LON):
         column = jnp.broadcast_to(mask[c : c + 1, :], (64, ROWS)).T
         cell = jnp.concatenate(
             [states[c].astype(F32), column, loss[c].astype(F32), column], axis=1
         )
-        wide, edge = (to_lon, to_both) if c < 6 else (kept, to_lat)
-        wide[c % 6] = cell.astype(BF16)
-        edge[c % 6] = cell[0:EDGE].astype(BF16)
-
-
-def window_kernel(kept, from_lon, from_lat, from_both, out, cells):
-    for c in range(WIN_LON):
-        wide, edge = (kept, from_lat) if c < 6 else (from_lon, from_both)
-        column = wide[c % 6].astype(F32)
-        after = edge[c % 6].astype(F32)
+        part, at = (1, 6 * c) if c < 6 else (0, 6 * (c - 6))
         for k in range(3):
-            cells[k, 6 * c : 6 * c + 6, :] = column[6 * k + 3 : 6 * k + 9]
-        cells[3, 6 * c : 6 * c + 3, :] = column[21:24]
-        cells[3, 6 * c + 3 : 6 * c + 6, :] = after[0:3]
-    out[...] = cells[...].astype(BF16)
+            cells[k % 2, k // 2, part, at : at + 6, :] = cell[6 * k + 3 : 6 * k + 9]
+        cells[1, 1, part, at : at + 3, :] = cell[21:24]
+        cells[1, 1, part, at + 3 : at + 6, :] = nothing
+        edges[part, at // 2 : at // 2 + 3, :] = cell[0:3]
+    keep_out[...] = cells[core].astype(BF16)
+    send_out[...] = cells[1 - core].astype(BF16)
+    edge_out[...] = edges[...].astype(BF16)
+    vectors_out[...] = vectors[...]
+
+
+def sort_kernel(kept, arrived, edge0, edge1, near_own, near_x, lon_own, lon_x, cells):
+    core = lax.axis_index("core")
+    here = lax.axis_index("xh")
+    cells[core] = kept[...].astype(F32)
+    cells[1 - core] = arrived[...].astype(F32)
+
+    @pl.when(core == 1)
+    def _():
+        for step, edge in enumerate((edge0, edge1)):
+            for part in range(2):
+                rows = edge[part].astype(F32)
+                for c in range(6):
+                    cells[step, 1, part, 6 * c + 3 : 6 * c + 6, :] = rows[3 * c : 3 * c + 3]
+
+    for step in range(2):
+        near_own[step] = cells[step, here, 0].astype(BF16)
+        near_x[step] = cells[step, 1 - here, 0].astype(BF16)
+        lon_own[step] = cells[step, here, 1].astype(BF16)
+        lon_x[step] = cells[step, 1 - here, 1].astype(BF16)
 
 
 def main_kernel(
-    cells, embed, gain_a, gain_m, wqkv, wout, wup, wdown_t,
+    near_own, near_x, lon_own, lon_x, vectors, wqkv, wout, wup, wdown_t,
     send_out, keep_out,
     x, qkv, probs, qm_all, emb, xh1, r1, hid_xh, r2, gp, act, normed_s, mixed_s, nm_s,
     cot_s, dpre_s, dproj_s, dqkv_s, dstate, small, msg,
 ):
     core = lax.axis_index("core")
-    third = jnp.logical_and(lax.axis_index("xh") == 1, core == 1)
-    last = jnp.logical_and(lax.axis_index("lat") == 7, third)
+    here = lax.axis_index("xh")
+    last = jnp.logical_and(lax.axis_index("lat") == 7, jnp.logical_and(here == 1, core == 1))
     closed = jnp.where(last, 0.0, 1.0).astype(F32)
-    for s in range(STEPS):
-        x[WIN * s : WIN * s + WIN, :] = cells[s].astype(F32)
-    le = embed[...]
-    ga = gain_a[...]
-    gm = gain_m[...]
+    for step in range(2):
+        x[2 * here + step, 0:HALF, :] = near_own[step].astype(F32)
+        x[2 * here + step, HALF:WIN, :] = lon_own[step].astype(F32)
+        x[2 * (1 - here) + step, 0:HALF, :] = near_x[step].astype(F32)
+        x[2 * (1 - here) + step, HALF:WIN, :] = lon_x[step].astype(F32)
+    le = vectors[0:1, :]
+    ga = vectors[1:2, :]
+    gm = vectors[2:3, :]
     col_head = lax.broadcasted_iota(jnp.int32, (1, CH), 1) // HEAD_DIM
     masks = [(col_head == h).astype(F32) for h in range(HEADS)]
     row_half = lax.rem(lax.broadcasted_iota(jnp.int32, (WIN, WIN), 0), WIN_LAT) // 3
@@ -106,8 +142,8 @@
 
     for s in range(STEPS):
         rows = slice(WIN * s, WIN * s + WIN)
-        land = x[rows, 192:256][:, 0:1]
-        e = x[rows, 0:CH] + land * le
+        land = x[s, :, 192:256][:, 0:1]
+        e = x[s, :, 0:CH] + land * le
         emb[rows, :] = e
         off = e - mean_of(e)
         r = lax.rsqrt(mean_of(off * off) + EPS)
@@ -155,7 +191,7 @@
     dstate[...] = jnp.zeros_like(dstate)
     for s in range(STEPS - 1, -1, -1):
         rows = slice(WIN * s, WIN * s + WIN)
-        cot = x[rows, 256:448]
+        cot = x[s, :, 256:448]
         if incoming is not None:
             cot = cot + incoming
         cotb = cot.astype(BF16)
@@ -189,7 +225,7 @@
         gain_a_sum = gain_a_sum + jnp.sum(dy * xh, axis=0, keepdims=True)
         dxh = dy * ga
         d_state = d_hid + r1[rows, :] * (dxh - mean_of(dxh) - xh * mean_of(dxh * xh))
-        land = x[rows, 192:256][:, 0:1]
+        land = x[s, :, 192:256][:, 0:1]
         land_sum = land_sum + jnp.sum(d_state * land, axis=0, keepdims=True)
         incoming = d_state.astype(BF16).astype(F32)
         dstate[:, 0:CH] = incoming
@@ -246,14 +282,17 @@
     x_keep[1 - core] = arrived[own, :]
 
 
-def group_kernel(terms, kept, arrived, total_out, near, to_lon, to_lat, to_both):
-    here = lax.axis_index("xh")
+def group_kernel(terms, total_out):
     total = terms[0].astype(F32)
     for g in range(1, GROUP):
         total = total + terms[g].astype(F32)
     total = total.astype(BF16)
     for g in range(8):
         total_out[g] = total
+
+
+def column_kernel(terms, kept, arrived, total_out, near, to_lon, to_lat, to_both):
+    here = lax.axis_index("xh")
     half = QUARTER // 2
     for c in range(2):
         near[2 * here + c] = kept[c, 0:half, :]
@@ -262,9 +301,6 @@
         to_lon[2 * (1 - here) + c] = arrived[c, half:QUARTER, :]
     to_lat[...] = near[3]
     to_both[...] = to_lon[3]
-
-
-def column_kernel(terms, total_out):
     total = terms[0].astype(F32)
     for g in range(1, 8):
         total = total + terms[g].astype(F32)
@@ -322,13 +358,15 @@
                     ]
 
 
-def hop(value, rows, cols):
+def hop(value, rows, cols, xh=0, cores=((0, 0), (1, 1))):
     pairs = []
-    for k in range(4):
-        for a in range(8):
-            for b in range(8):
-                to = (k * 8 + (a + rows) % 8) * 8 + (b + cols) % 8
-                pairs.append(((k * 8 + a) * 8 + b, to))
+    for h in range(2):
+        for source, target in cores:
+            for a in range(8):
+                for b in range(8):
+                    k = 2 * ((h + xh) % 2) + target
+                    to = (k * 8 + (a + rows) % 8) * 8 + (b + cols) % 8
+                    pairs.append((((2 * h + source) * 8 + a) * 8 + b, to))
     return lax.ppermute(value, AXES, pairs)
 
 
@@ -340,37 +378,59 @@
     return lax.all_to_all(value, axis, 0, 0, tiled=True)
 
 
-def call(kernel, name, outs, scratch=(), mib=8):
+def call(kernel, name, outs, scratch=(), mib=8, from_hbm=0):
+    specs = {}
+    if from_hbm:
+        specs["in_specs"] = [pl.BlockSpec(memory_space=pltpu.HBM)] * from_hbm
     return pl.pallas_call(
         kernel,
         out_shape=tuple(jax.ShapeDtypeStruct(dims, kind) for dims, kind in outs),
-        scratch_shapes=[pltpu.VMEM(dims, kind) for dims, kind in scratch],
+        scratch_shapes=[pltpu.VMEM(dims, kind) if kind else dims for dims, kind in scratch],
         compiler_params=pltpu.CompilerParams(vmem_limit_bytes=mib * MIB),
         name=name,
+        **specs,
     )
 
 
 def local(
     states, loss_grads, land_sea, land_embed, gain_attn, gain_mlp, w_qkv, w_out, w_up, w_down
 ):
-    kept, to_lon, to_lat, to_both = call(
+    keep, send, edge, vectors = call(
         pack_kernel,
         "pack_cells",
-        [((6, ROWS, MSG), BF16)] * 2 + [((6, EDGE, MSG), BF16)] * 2,
-    )(states[0, 0].transpose(1, 0, 2), loss_grads[0, 0].transpose(1, 0, 2), land_sea.T)
-    from_lon = hop(to_lon, 0, -1)
-    from_lat = hop(to_lat, -1, 0)
-    from_both = hop(to_both, -1, -1)
-    (packed,) = call(
-        window_kernel, "cut_windows", [((4, WIN, MSG), BF16)], [((4, WIN, MSG), F32)]
-    )(kept, from_lon, from_lat, from_both)
-    cells = exchange(packed, ("xh", "core"))
+        [((2, 2, HALF, MSG), BF16)] * 2 + [((2, HALF // 2, MSG), BF16), ((8, CH), F32)],
+        [
+            ((WIN_LON, ROWS, CH), BF16),
+            ((WIN_LON, ROWS, CH), BF16),
+            ((WIN_LON, ROWS), jnp.int32),
+            ((8, CH), F32),
+            ((2, 2, 2, HALF, MSG), F32),
+            ((2, HALF // 2, MSG), F32),
+            (pltpu.SemaphoreType.DMA((6,)), None),
+        ],
+        from_hbm=6,
+    )(
+        states[0, 0].transpose(1, 0, 2), loss_grads[0, 0].transpose(1, 0, 2), land_sea.T,
+        land_embed[None], gain_attn[None], gain_mlp[None],
+    )
+    near_own, near_x, lon_own, lon_x = call(
+        sort_kernel,
+        "sort_windows",
+        [((2, HALF, MSG), BF16)] * 4,
+        [((2, 2, 2, HALF, MSG), F32)],
+    )(
+        keep, swap(send, "core"),
+        hop(edge, -1, 0, cores=((0, 1),)), hop(edge, -1, 0, cores=((1, 1),)),
+    )
+    near_x = hop(near_x, 0, 0, 1)
+    lon_own = hop(lon_own, 0, -1)
+    lon_x = hop(lon_x, 0, -1, 1)
     send, keep = call(
         main_kernel,
         "window_steps",
         [((SENT, 128), BF16)] * 2,
         [
-            ((TOK, MSG), F32),
+            ((STEPS, WIN, MSG), F32),
             ((TOK, 3 * CH), F32),
             ((STEPS, HEADS * WIN, WIN), F32),
             ((STEPS, HEADS * WIN, CH), BF16),
@@ -393,9 +453,7 @@
             ((2, SENT, 128), BF16),
         ],
         mib=24,
-    )(
-        cells, land_embed[None], gain_attn[None], gain_mlp[None], w_qkv, w_out, w_up, w_down.T
-    )
+    )(near_own, near_x, lon_own, lon_x, vectors, w_qkv, w_out, w_up, w_down.T)
 
     chunks, x_send, x_keep = call(
         pair_kernel,
@@ -403,22 +461,22 @@
         [((GROUP, UNIT, 128), BF16)] + [((2, QUARTER, 128), BF16)] * 2,
     )(keep, swap(send, "core"))
     x_arrived = swap(x_send, "xh")
-    terms = exchange(chunks, ("xh", "lon"))
-    partial, near, to_lon, to_lat, to_both = call(
-        group_kernel,
-        "sum_group",
-        [((8, UNIT, 128), BF16)]
+    (partial,) = call(group_kernel, "sum_group", [((8, UNIT, 128), BF16)])(
+        exchange(chunks, ("xh", "lon"))
+    )
+    total, near, to_lon, to_lat, to_both = call(
+        column_kernel,
+        "sum_column",
+        [((GROUP, UNIT, 128), BF16)]
         + [((4, QUARTER // 2, 128), BF16)] * 2
         + [((QUARTER // 2, 128), BF16)] * 2,
-    )(terms, x_keep, x_arrived)
+    )(exchange(partial, "lat"), x_keep, x_arrived)
     from_lon = hop(to_lon, 0, 1)
     from_lat = hop(to_lat, 1, 0)
     from_both = hop(to_both, 1, 1)
-    terms, from_lon, from_lat, from_both = lax.optimization_barrier(
-        (exchange(partial, "lat"), from_lon, from_lat, from_both)
-    )
-    (total,) = call(column_kernel, "sum_column", [((GROUP, UNIT, 128), BF16)])(terms)
-    own = exchange(total, ("xh", "lon"))
+    own, from_lon, from_lat, from_both = lax.optimization_barrier(
+        (exchange(total, ("xh", "lon")), from_lon, from_lat, from_both)
+    )
     outs = call(
         unpack_kernel,
         "unpack_sums",

time: 91.6 us -> 90.1 us (0.984)
  blocking collectives: 25.3 us -> 13 us
  waiting for transfers between devices: 19.3 us -> 27.4 us
  starting transfers between devices: 30.9 us -> 32.8 us
    all_to_all x2 -> x1, blocking collectives: 25.3 us -> 13 us  [exchange(): return lax.all_to_all(value, axis, 0, 0, tiled=True)]
    ppermute x6 -> x8, waiting for transfers between devices: 8.79 us -> 16.6 us  [hop(): return lax.ppermute(value, AXES, pairs)]
    all_to_all x2, waiting for transfers between devices: 0.01 us -> 3.74 us  [exchange(): return lax.all_to_all(value, axis, 0, 0, tiled=True)]
    ppermute x3 -> x4, waiting for transfers between devices: 10.5 us -> 7.05 us  [swap(): return lax.ppermute(value, axis, [(0, 1), (1, 0)])]
    pallas_call x5, Pallas kernels: 9.29 us -> 10.6 us  [the longest x1 8.15 us: local(): call(main_kernel, 'window_steps', [((SENT, 128), BF16)] * 2, [((STEPS, WI...]
    ppermute x3 -> x4, starting transfers between devices: 8.24 us -> 9.53 us  [swap(): return lax.ppermute(value, axis, [(0, 1), (1, 0)])]
    ppermute x6 -> x8, starting transfers between devices: 15.7 us -> 16.1 us  [hop(): return lax.ppermute(value, AXES, pairs)]
  transfers between devices with their start and end apart: 11 -> 14, of which waited for: 7 -> 9; matrix products, arithmetic and copies ran while one was open for 0% -> 0% of each run, Pallas kernels for 0% -> 0%
where the time goes in v3:
time: 90.1 us; the launch traced here: 89.7 us
  starting transfers between devices  32.8 us (36%)
  waiting for transfers between devices  27.4 us (30%)
  blocking collectives  13 us (14%)
  Pallas kernels  12.2 us (14%)
  local copies, waits for them, and re-layouts  3.47 us (4%)
    ppermute x8, waiting for transfers between devices, hop(): return lax.ppermute(value, AXES, pairs)  16.6 us
    ppermute x8, starting transfers between devices, hop(): return lax.ppermute(value, AXES, pairs)  16.1 us
    all_to_all x1, blocking collectives, exchange(): return lax.all_to_all(value, axis, 0, 0, tiled=True)  13 us
    ppermute x4, starting transfers between devices, swap(): return lax.ppermute(value, axis, [(0, 1), (1, 0)])  9.53 us
    pallas_call x1, Pallas kernels, local(): call(main_kernel, 'window_steps', [((SENT, 128), BF16)] * 2, [((STEPS, WI...  8.15 us
    all_to_all x2, starting transfers between devices, exchange(): return lax.all_to_all(value, axis, 0, 0, tiled=True)  7.23 us
    ppermute x4, waiting for transfers between devices, swap(): return lax.ppermute(value, axis, [(0, 1), (1, 0)])  7.05 us
    all_to_all x2, waiting for transfers between devices, exchange(): return lax.all_to_all(value, axis, 0, 0, tiled=True)  3.74 us
  transfers between devices with their start and end apart: 14, of which 9 were waited for; matrix products, arithmetic and copies ran while one was open for 0% of the time, Pallas kernels for 0%

profile of v3, /device:TPU:1, one launch (start us, length us, event | category | flops | bytes accessed | tf_op | source)
XLA Modules:
  0.0 89.7 jit_solution(16658276386324137285)
XLA Ops:
  4.0 3.3 %collective-permute-start = (bf16[2,2,36,512]{3,2,1,0:T(8,128)(2,1)S(1)}, bf16[2,2,36,512]{3,2,1,0:T(8,128)(2,1)S(1)}, u32[]{:S(2)}, u32[]{:S(2)}) collective-permute-start(bf16[2,2,36,512]{3,2,1,0:T(8,128)(2,1)S(1)} %get-tuple-element.39), channel_id=1, source_target_pairs={{0,64},{64,0},{1,65},{65,1},{2,66},{66,2},{3,67},{67,3},{4,68},{68... | collective-permute-start | bytes 442376 | tf_op jit(solution)/shard_map/ppermute | solution.py:374
  7.3 5.7 %collective-permute-start.2 = (bf16[2,18,512]{2,1,0:T(8,128)(2,1)S(1)}, bf16[2,18,512]{2,1,0:T(8,128)(2,1)S(1)}, u32[]{:S(2)}, u32[]{:S(2)}) collective-permute-start(bf16[2,18,512]{2,1,0:T(8,128)(2,1)S(1)} %get-tuple-element.40), channel_id=1, source_target_pairs={{64,120},{65,121},{66,122},{67,123},{68,124},{69,125},{70,126},{71... | collective-permute-start | bytes 110600 | tf_op jit(solution)/shard_map/ppermute | solution.py:370
  13.0 1.3 %collective-permute-start.1 = (bf16[2,18,512]{2,1,0:T(8,128)(2,1)S(1)}, bf16[2,18,512]{2,1,0:T(8,128)(2,1)S(1)}, u32[]{:S(2)}, u32[]{:S(2)}) collective-permute-start(bf16[2,18,512]{2,1,0:T(8,128)(2,1)S(1)} %get-tuple-element.40), channel_id=1, source_target_pairs={{0,120},{1,121},{2,122},{3,123},{4,124},{5,125},{6,126},{7,127},{8... | collective-permute-start | bytes 110600 | tf_op jit(solution)/shard_map/ppermute | solution.py:370
  14.3 4.1 %collective-permute-done.1.edge0 = bf16[2,18,512]{2,1,0:T(8,128)(2,1)S(1)} collective-permute-done((bf16[2,18,512]{2,1,0:T(8,128)(2,1)S(1)}, bf16[2,18,512]{2,1,0:T(8,128)(2,1)S(1)}, u32[]{:S(2)}, u32[]{:S(2)}) %collective-permute-start.1) | collective-permute-done | bytes 36896 | tf_op jit(solution)/shard_map/ppermute | solution.py:370
  18.6 2.8 %collective-permute-start.3 = (bf16[2,36,512]{2,1,0:T(8,128)(2,1)S(1)}, bf16[2,36,512]{2,1,0:T(8,128)(2,1)S(1)}, u32[]{:S(2)}, u32[]{:S(2)}) collective-permute-start(bf16[2,36,512]{2,1,0:T(8,128)(2,1)S(1)} %get-tuple-element.42), channel_id=1, source_target_pairs={{0,128},{1,129},{2,130},{3,131},{4,132},{5,133},{6,134},{7,135},{8... | collective-permute-start | bytes 221192 | tf_op jit(solution)/shard_map/ppermute | solution.py:370
  21.4 2.8 %collective-permute-start.4 = (bf16[2,36,512]{2,1,0:T(8,128)(2,1)S(1)}, bf16[2,36,512]{2,1,0:T(8,128)(2,1)S(1)}, u32[]{:S(2)}, u32[]{:S(2)}) collective-permute-start(bf16[2,36,512]{2,1,0:T(8,128)(2,1)S(1)} %get-tuple-element.43), channel_id=1, source_target_pairs={{0,7},{1,0},{2,1},{3,2},{4,3},{5,4},{6,5},{7,6},{8,15},{9,8},{10,9... | collective-permute-start | bytes 221192 | tf_op jit(solution)/shard_map/ppermute | solution.py:370
  24.2 1.0 %collective-permute-start.5 = (bf16[2,36,512]{2,1,0:T(8,128)(2,1)S(1)}, bf16[2,36,512]{2,1,0:T(8,128)(2,1)S(1)}, u32[]{:S(2)}, u32[]{:S(2)}) collective-permute-start(bf16[2,36,512]{2,1,0:T(8,128)(2,1)S(1)} %get-tuple-element.44), channel_id=1, source_target_pairs={{0,135},{1,128},{2,129},{3,130},{4,131},{5,132},{6,133},{7,134},{8... | collective-permute-start | bytes 221192 | tf_op jit(solution)/shard_map/ppermute | solution.py:370
  25.2 1.4 %collective-permute-done.4.lon_own = bf16[2,36,512]{2,1,0:T(8,128)(2,1)S(1)} collective-permute-done((bf16[2,36,512]{2,1,0:T(8,128)(2,1)S(1)}, bf16[2,36,512]{2,1,0:T(8,128)(2,1)S(1)}, u32[]{:S(2)}, u32[]{:S(2)}) %collective-permute-start.4) | collective-permute-done | bytes 73760 | tf_op jit(solution)/shard_map/ppermute | solution.py:370
  26.6 4.2 %collective-permute-done.5.lon_x = bf16[2,36,512]{2,1,0:T(8,128)(2,1)S(1)} collective-permute-done((bf16[2,36,512]{2,1,0:T(8,128)(2,1)S(1)}, bf16[2,36,512]{2,1,0:T(8,128)(2,1)S(1)}, u32[]{:S(2)}, u32[]{:S(2)}) %collective-permute-start.5) | collective-permute-done | bytes 73760 | tf_op jit(solution)/shard_map/ppermute | solution.py:370
  30.8 0.9 %copy-done.2 = bf16[192,576]{1,0:T(8,128)(2,1)S(1)} copy-done((bf16[192,576]{1,0:T(8,128)(2,1)S(1)}, bf16[192,576]{1,0:T(8,128)(2,1)}, u32[]{:S(2)}) %copy-start.2) | copy-done | bytes 221208
  31.7 8.2 %window_steps.1 = (bf16[2176,128]{1,0:T(8,128)(2,1)S(1)}, bf16[2176,128]{1,0:T(8,128)(2,1)S(1)}) custom-call(bf16[2,36,512]{2,1,0:T(8,128)(2,1)S(1)} %get-tuple-element.41.near_own, bf16[2,36,512]{2,1,0:T(8,128)(2,1)S(1)} %collective-permute-done.3.near_x, bf16[2,36,512]{2,1,0:T(8,128)(2,1)S(1)} %collective-permute-done.4.lon_own, ...), custom_call_target="tpu_custom_call" | custom-call | tf_op jit(solution)/shard_map/window_steps/pallas_call | solution.py:428
  40.6 1.6 %collective-permute-done.6.arrived = bf16[2176,128]{1,0:T(8,128)(2,1)S(1)} collective-permute-done((bf16[2176,128]{1,0:T(8,128)(2,1)S(1)}, bf16[2176,128]{1,0:T(8,128)(2,1)S(1)}, u32[]{:S(2)}, u32[]{:S(2)}) %collective-permute-start.6) | collective-permute-done | bytes 557088 | tf_op jit(solution)/shard_map/ppermute | solution.py:374
  42.3 13.0 %all_to_all.15.terms = bf16[16,112,128]{2,1,0:T(8,128)(2,1)S(1)} all-to-all(bf16[16,112,128]{2,1,0:T(8,128)(2,1)S(1)} %get-tuple-element.48), channel_id=1, replica_groups=mesh['xh'=2,'core'=2,'lat'=8,'lon'=8] {'xh','lon'}, dimensions={0} | all-to-all | bytes 917504 | tf_op jit(solution)/shard_map/all_to_all | solution.py:378
  56.1 3.4 %all-to-all-start.1 = ((bf16[8,112,128]{2,1,0:T(8,128)(2,1)}), bf16[8,112,128]{2,1,0:T(8,128)(2,1)S(1)}, u32[]{:S(2)}, u32[]{:S(2)}) async-start(bf16[8,112,128]{2,1,0:T(8,128)(2,1)} %sum_group.1), calls=%async_computation.1 | async-start | bytes 458752 | tf_op jit(solution)/shard_map/all_to_all | solution.py:378
  59.5 1.0 %collective-permute-start.7 = (bf16[2,192,128]{2,1,0:T(8,128)(2,1)S(1)}, bf16[2,192,128]{2,1,0:T(8,128)(2,1)S(1)}, u32[]{:S(2)}, u32[]{:S(2)}) collective-permute-start(bf16[2,192,128]{2,1,0:T(8,128)(2,1)S(1)} %get-tuple-element.50), channel_id=1, source_target_pairs={{0,128},{128,0},{1,129},{129,1},{2,130},{130,2},{3,131},{131,3},{4... | collective-permute-start | bytes 294920 | tf_op jit(solution)/shard_map/ppermute | solution.py:374
  60.5 4.0 %collective-permute-done.7.arrived = bf16[2,192,128]{2,1,0:T(8,128)(2,1)S(1)} collective-permute-done((bf16[2,192,128]{2,1,0:T(8,128)(2,1)S(1)}, bf16[2,192,128]{2,1,0:T(8,128)(2,1)S(1)}, u32[]{:S(2)}, u32[]{:S(2)}) %collective-permute-start.7) | collective-permute-done | bytes 98336 | tf_op jit(solution)/shard_map/ppermute | solution.py:374
  64.6 3.7 %all-to-all-done.1.terms = bf16[8,112,128]{2,1,0:T(8,128)(2,1)S(1)} async-done(((bf16[8,112,128]{2,1,0:T(8,128)(2,1)}), bf16[8,112,128]{2,1,0:T(8,128)(2,1)S(1)}, u32[]{:S(2)}, u32[]{:S(2)}) %all-to-all-start.1) | async-done | bytes 229408 | tf_op jit(solution)/shard_map/all_to_all | solution.py:378
  69.1 3.8 %all-to-all-start.2 = ((bf16[16,112,128]{2,1,0:T(8,128)(2,1)}), bf16[16,112,128]{2,1,0:T(8,128)(2,1)S(1)}, u32[]{:S(2)}, u32[]{:S(2)}) async-start(bf16[16,112,128]{2,1,0:T(8,128)(2,1)} %get-tuple-element.51), calls=%async_computation.2 | async-start | bytes 917504 | tf_op jit(solution)/shard_map/all_to_all | solution.py:378
  73.0 1.4 %collective-permute-start.8 = (bf16[4,96,128]{2,1,0:T(8,128)(2,1)S(1)}, bf16[4,96,128]{2,1,0:T(8,128)(2,1)S(1)}, u32[]{:S(2)}, u32[]{:S(2)}) collective-permute-start(bf16[4,96,128]{2,1,0:T(8,128)(2,1)S(1)} %get-tuple-element.52), channel_id=1, source_target_pairs={{0,1},{1,2},{2,3},{3,4},{4,5},{5,6},{6,7},{7,0},{8,9},{9,10},{10,1... | collective-permute-start | bytes 294920 | tf_op jit(solution)/shard_map/ppermute | solution.py:370
  75.4 2.8 %collective-permute-done.9.from_lat = bf16[96,128]{1,0:T(8,128)(2,1)S(1)} collective-permute-done((bf16[96,128]{1,0:T(8,128)(2,1)S(1)}, bf16[96,128]{1,0:T(8,128)(2,1)S(1)}, u32[]{:S(2)}, u32[]{:S(2)}) %collective-permute-start.9) | collective-permute-done | bytes 24608 | tf_op jit(solution)/shard_map/ppermute | solution.py:370
  78.2 4.1 %collective-permute-done.10.from_both = bf16[96,128]{1,0:T(8,128)(2,1)S(1)} collective-permute-done((bf16[96,128]{1,0:T(8,128)(2,1)S(1)}, bf16[96,128]{1,0:T(8,128)(2,1)S(1)}, u32[]{:S(2)}, u32[]{:S(2)}) %collective-permute-start.10) | collective-permute-done | bytes 24608 | tf_op jit(solution)/shard_map/ppermute | solution.py:370
  82.4 4.4 %collective-permute-start.11 = (bf16[16,112,128]{2,1,0:T(8,128)(2,1)S(1)}, bf16[16,112,128]{2,1,0:T(8,128)(2,1)S(1)}, u32[]{:S(2)}, u32[]{:S(2)}) collective-permute-start(bf16[16,112,128]{2,1,0:T(8,128)(2,1)S(1)} %all-to-all-done.2.own), channel_id=1, source_target_pairs={{0,64},{64,0},{1,65},{65,1},{2,66},{66,2},{3,67},{67,3},{4,68},{68... | collective-permute-start | bytes 1376264 | tf_op jit(solution)/shard_map/ppermute | solution.py:374
  86.8 1.4 %collective-permute-done.11.other = bf16[16,112,128]{2,1,0:T(8,128)(2,1)S(1)} collective-permute-done((bf16[16,112,128]{2,1,0:T(8,128)(2,1)S(1)}, bf16[16,112,128]{2,1,0:T(8,128)(2,1)S(1)}, u32[]{:S(2)}, u32[]{:S(2)}) %collective-permute-start.11) | collective-permute-done | bytes 458784 | tf_op jit(solution)/shard_map/ppermute | solution.py:374
  88.2 1.4 %unpack_sums.1 = (f32[12,24,192]{2,1,0:T(8,128)}, f32[192,576]{1,0:T(8,128)}, f32[192,192]{1,0:T(8,128)}, f32[192,768]{1,0:T(8,128)}, f32[192,768]{1,0:T(8,128)}...) custom-call(bf16[16,112,128]{2,1,0:T(8,128)(2,1)S(1)} %all-to-all-done.2.own, ...), custom_call_target="tpu_custom_call" | custom-call | tf_op jit(solution)/shard_map/unpack_sums/pallas_call | solution.py:480
  (32 shorter events, 6.9 us)
Async XLA Ops:
  0.6 0.7 copy-start.6
  0.6 0.7 copy-start.8
  0.7 0.7 copy-start.9
  0.7 0.7 copy-start.7
  1.4 0.9 %copy-start.3 = (bf16[1,1,24,12,192]{4,2,3,1,0:T(8,128)(2,1)S(1)}, bf16[1,1,24,12,192]{4,2,3,1,0:T(8,128)(2,1)}, u32[]{:S(2)}) copy-start(bf16[1,1,24,12,192]{4,2,3,1,0:T(8,128)(2,1)} %param.10) | copy-start | bytes 331780
  2.3 0.9 %copy-start.4 = (bf16[1,1,24,12,192]{4,2,3,1,0:T(8,128)(2,1)S(1)}, bf16[1,1,24,12,192]{4,2,3,1,0:T(8,128)(2,1)}, u32[]{:S(2)}) copy-start(bf16[1,1,24,12,192]{4,2,3,1,0:T(8,128)(2,1)} %param.11) | copy-start | bytes 331780
  3.2 27.6 %copy-start.1 = (bf16[768,192]{0,1:T(8,128)(2,1)S(1)}, bf16[768,192]{0,1:T(8,128)(2,1)}, u32[]{:S(2)}) copy-start(bf16[768,192]{0,1:T(8,128)(2,1)} %param.19) | copy-start | bytes 884740
  3.9 26.8 %copy-start = (bf16[192,768]{1,0:T(8,128)(2,1)S(1)}, bf16[192,768]{1,0:T(8,128)(2,1)}, u32[]{:S(2)}) copy-start(bf16[192,768]{1,0:T(8,128)(2,1)} %wup.1) | copy-start | bytes 884740
  4.0 14.5 %collective-permute-start = (bf16[2,2,36,512]{3,2,1,0:T(8,128)(2,1)S(1)}, bf16[2,2,36,512]{3,2,1,0:T(8,128)(2,1)S(1)}, u32[]{:S(2)}, u32[]{:S(2)}) collective-permute-start(bf16[2,2,36,512]{3,2,1,0:T(8,128)(2,1)S(1)} %get-tuple-element.39), channel_id=1, source_target_pairs={{0,64},{64,0},{1,65},{65,1},{2,66},{66,2},{3,67},{67,3},{4,68},{68... | collective-permute-start | bytes 442376 | tf_op jit(solution)/shard_map/ppermute | solution.py:374
  7.3 7.0 %collective-permute-start.2 = (bf16[2,18,512]{2,1,0:T(8,128)(2,1)S(1)}, bf16[2,18,512]{2,1,0:T(8,128)(2,1)S(1)}, u32[]{:S(2)}, u32[]{:S(2)}) collective-permute-start(bf16[2,18,512]{2,1,0:T(8,128)(2,1)S(1)} %get-tuple-element.40), channel_id=1, source_target_pairs={{64,120},{65,121},{66,122},{67,123},{68,124},{69,125},{70,126},{71... | collective-permute-start | bytes 110600 | tf_op jit(solution)/shard_map/ppermute | solution.py:370
  13.0 5.4 %collective-permute-start.1 = (bf16[2,18,512]{2,1,0:T(8,128)(2,1)S(1)}, bf16[2,18,512]{2,1,0:T(8,128)(2,1)S(1)}, u32[]{:S(2)}, u32[]{:S(2)}) collective-permute-start(bf16[2,18,512]{2,1,0:T(8,128)(2,1)S(1)} %get-tuple-element.40), channel_id=1, source_target_pairs={{0,120},{1,121},{2,122},{3,123},{4,124},{5,125},{6,126},{7,127},{8... | collective-permute-start | bytes 110600 | tf_op jit(solution)/shard_map/ppermute | solution.py:370
  18.4 12.3 %copy-start.5 = (bf16[192,192]{1,0:T(8,128)(2,1)S(1)}, bf16[192,192]{1,0:T(8,128)(2,1)}, u32[]{:S(2)}) copy-start(bf16[192,192]{1,0:T(8,128)(2,1)} %wout.1) | copy-start | bytes 221188
  18.6 6.6 %collective-permute-start.3 = (bf16[2,36,512]{2,1,0:T(8,128)(2,1)S(1)}, bf16[2,36,512]{2,1,0:T(8,128)(2,1)S(1)}, u32[]{:S(2)}, u32[]{:S(2)}) collective-permute-start(bf16[2,36,512]{2,1,0:T(8,128)(2,1)S(1)} %get-tuple-element.42), channel_id=1, source_target_pairs={{0,128},{1,129},{2,130},{3,131},{4,132},{5,133},{6,134},{7,135},{8... | collective-permute-start | bytes 221192 | tf_op jit(solution)/shard_map/ppermute | solution.py:370
  21.4 5.2 %collective-permute-start.4 = (bf16[2,36,512]{2,1,0:T(8,128)(2,1)S(1)}, bf16[2,36,512]{2,1,0:T(8,128)(2,1)S(1)}, u32[]{:S(2)}, u32[]{:S(2)}) collective-permute-start(bf16[2,36,512]{2,1,0:T(8,128)(2,1)S(1)} %get-tuple-element.43), channel_id=1, source_target_pairs={{0,7},{1,0},{2,1},{3,2},{4,3},{5,4},{6,5},{7,6},{8,15},{9,8},{10,9... | collective-permute-start | bytes 221192 | tf_op jit(solution)/shard_map/ppermute | solution.py:370
  24.2 6.6 %collective-permute-start.5 = (bf16[2,36,512]{2,1,0:T(8,128)(2,1)S(1)}, bf16[2,36,512]{2,1,0:T(8,128)(2,1)S(1)}, u32[]{:S(2)}, u32[]{:S(2)}) collective-permute-start(bf16[2,36,512]{2,1,0:T(8,128)(2,1)S(1)} %get-tuple-element.44), channel_id=1, source_target_pairs={{0,135},{1,128},{2,129},{3,130},{4,131},{5,132},{6,133},{7,134},{8... | collective-permute-start | bytes 221192 | tf_op jit(solution)/shard_map/ppermute | solution.py:370
  30.8 0.9 %copy-start.2 = (bf16[192,576]{1,0:T(8,128)(2,1)S(1)}, bf16[192,576]{1,0:T(8,128)(2,1)}, u32[]{:S(2)}) copy-start(bf16[192,576]{1,0:T(8,128)(2,1)} %wqkv.1) | copy-start | bytes 663556
  39.9 2.3 %collective-permute-start.6 = (bf16[2176,128]{1,0:T(8,128)(2,1)S(1)}, bf16[2176,128]{1,0:T(8,128)(2,1)S(1)}, u32[]{:S(2)}, u32[]{:S(2)}) collective-permute-start(bf16[2176,128]{1,0:T(8,128)(2,1)S(1)} %get-tuple-element.47), channel_id=1, source_target_pairs={{0,64},{64,0},{1,65},{65,1},{2,66},{66,2},{3,67},{67,3},{4,68},{68... | collective-permute-start | bytes 1671176 | tf_op jit(solution)/shard_map/ppermute | solution.py:374
  56.1 12.2 %all-to-all-start.1 = ((bf16[8,112,128]{2,1,0:T(8,128)(2,1)}), bf16[8,112,128]{2,1,0:T(8,128)(2,1)S(1)}, u32[]{:S(2)}, u32[]{:S(2)}) async-start(bf16[8,112,128]{2,1,0:T(8,128)(2,1)} %sum_group.1), calls=%async_computation.1 | async-start | bytes 458752 | tf_op jit(solution)/shard_map/all_to_all | solution.py:378
  59.5 5.1 %collective-permute-start.7 = (bf16[2,192,128]{2,1,0:T(8,128)(2,1)S(1)}, bf16[2,192,128]{2,1,0:T(8,128)(2,1)S(1)}, u32[]{:S(2)}, u32[]{:S(2)}) collective-permute-start(bf16[2,192,128]{2,1,0:T(8,128)(2,1)S(1)} %get-tuple-element.50), channel_id=1, source_target_pairs={{0,128},{128,0},{1,129},{129,1},{2,130},{130,2},{3,131},{131,3},{4... | collective-permute-start | bytes 294920 | tf_op jit(solution)/shard_map/ppermute | solution.py:374
  69.1 13.2 %all-to-all-start.2 = ((bf16[16,112,128]{2,1,0:T(8,128)(2,1)}), bf16[16,112,128]{2,1,0:T(8,128)(2,1)S(1)}, u32[]{:S(2)}, u32[]{:S(2)}) async-start(bf16[16,112,128]{2,1,0:T(8,128)(2,1)} %get-tuple-element.51), calls=%async_computation.2 | async-start | bytes 917504 | tf_op jit(solution)/shard_map/all_to_all | solution.py:378
  73.0 9.4 %collective-permute-start.8 = (bf16[4,96,128]{2,1,0:T(8,128)(2,1)S(1)}, bf16[4,96,128]{2,1,0:T(8,128)(2,1)S(1)}, u32[]{:S(2)}, u32[]{:S(2)}) collective-permute-start(bf16[4,96,128]{2,1,0:T(8,128)(2,1)S(1)} %get-tuple-element.52), channel_id=1, source_target_pairs={{0,1},{1,2},{2,3},{3,4},{4,5},{5,6},{6,7},{7,0},{8,9},{9,10},{10,1... | collective-permute-start | bytes 294920 | tf_op jit(solution)/shard_map/ppermute | solution.py:370
  74.4 3.9 %collective-permute-start.9 = (bf16[96,128]{1,0:T(8,128)(2,1)S(1)}, bf16[96,128]{1,0:T(8,128)(2,1)S(1)}, u32[]{:S(2)}, u32[]{:S(2)}) collective-permute-start(bf16[96,128]{1,0:T(8,128)(2,1)S(1)} %get-tuple-element.53), channel_id=1, source_target_pairs={{0,8},{1,9},{2,10},{3,11},{4,12},{5,13},{6,14},{7,15},{8,16},{9,17... | collective-permute-start | bytes 73736 | tf_op jit(solution)/shard_map/ppermute | solution.py:370
  74.5 7.8 %collective-permute-start.10 = (bf16[96,128]{1,0:T(8,128)(2,1)S(1)}, bf16[96,128]{1,0:T(8,128)(2,1)S(1)}, u32[]{:S(2)}, u32[]{:S(2)}) collective-permute-start(bf16[96,128]{1,0:T(8,128)(2,1)S(1)} %get-tuple-element.54), channel_id=1, source_target_pairs={{0,9},{1,10},{2,11},{3,12},{4,13},{5,14},{6,15},{7,8},{8,17},{9,18... | collective-permute-start | bytes 73736 | tf_op jit(solution)/shard_map/ppermute | solution.py:370
  82.4 5.9 %collective-permute-start.11 = (bf16[16,112,128]{2,1,0:T(8,128)(2,1)S(1)}, bf16[16,112,128]{2,1,0:T(8,128)(2,1)S(1)}, u32[]{:S(2)}, u32[]{:S(2)}) collective-permute-start(bf16[16,112,128]{2,1,0:T(8,128)(2,1)S(1)} %all-to-all-done.2.own), channel_id=1, source_target_pairs={{0,64},{64,0},{1,65},{65,1},{2,66},{66,2},{3,67},{67,3},{4,68},{68... | collective-permute-start | bytes 1376264 | tf_op jit(solution)/shard_map/ppermute | solution.py:374

commit v4 on v3

--- a/solution.py
+++ b/solution.py
@@ -49,8 +49,8 @@
 
 
 def pack_kernel(
-    states_in, loss_in, land_in, embed_in, gain_a_in, gain_m_in,
-    keep_out, send_out, edge_out, vectors_out,
+    states_in, loss_in, land_in, embed_in, gain_a_in, gain_m_in, wqkv_in,
+    keep_out, send_out, edge_out, vectors_out, wqkv_out,
     states, loss, land, vectors, cells, edges, sems,
 ):
     pairs = (
@@ -61,8 +61,10 @@
         pltpu.make_async_copy(source, target, sems.at[i])
         for i, (source, target) in enumerate(pairs)
     ]
+    weights = pltpu.make_async_copy(wqkv_in, wqkv_out, sems.at[6])
     for copy in copies:
         copy.start()
+    weights.start()
     for copy in copies:
         copy.wait()
     core = lax.axis_index("core")
@@ -83,6 +85,7 @@
     send_out[...] = cells[1 - core].astype(BF16)
     edge_out[...] = edges[...].astype(BF16)
     vectors_out[...] = vectors[...]
+    weights.wait()
 
 
 def sort_kernel(kept, arrived, edge0, edge1, near_own, near_x, lon_own, lon_x, cells):
@@ -110,7 +113,7 @@
     near_own, near_x, lon_own, lon_x, vectors, wqkv, wout, wup, wdown_t,
     send_out, keep_out,
     x, qkv, probs, qm_all, emb, xh1, r1, hid_xh, r2, gp, act, normed_s, mixed_s, nm_s,
-    cot_s, dpre_s, dproj_s, dqkv_s, dstate, small, msg,
+    cot_s, dpre_s, dproj_s, dqkv_s, dstate, small, msg, sems,
 ):
     core = lax.axis_index("core")
     here = lax.axis_index("xh")
@@ -129,7 +132,7 @@
     row_half = lax.rem(lax.broadcasted_iota(jnp.int32, (WIN, WIN), 0), WIN_LAT) // 3
     key_half = lax.rem(lax.broadcasted_iota(jnp.int32, (WIN, WIN), 1), WIN_LAT) // 3
     allow1 = jnp.where(row_half == key_half, 1.0, closed).astype(F32)
-    allow = jnp.concatenate([allow1] * HEADS, axis=0)
+    allow = jnp.concatenate([allow1] * HEADS, axis=1)
 
     def spread(v):
         return jnp.concatenate([v * m for m in masks], axis=0).astype(BF16)
@@ -159,10 +162,10 @@
         qm_all[s] = qm
         keys = qkv[rows, CH : 2 * CH].astype(BF16)
         values = qkv[rows, 2 * CH : 3 * CH].astype(BF16)
-        weights = jnp.exp(nt(qm, keys) * SCALE) * allow
-        p = weights / jnp.sum(weights, axis=-1, keepdims=True)
+        weights = jnp.exp(nt(keys, qm) * SCALE) * allow
+        p = weights / jnp.sum(weights, axis=0, keepdims=True)
         probs[s] = p
-        mixed_s[rows, :] = gathered(nn(p.astype(BF16), values))
+        mixed_s[rows, :] = gathered(tn(p.astype(BF16), values))
     mixed = mixed_s[...].astype(BF16)
     projected = nn(mixed, wout[...]).astype(BF16).astype(F32)
     hid = emb[...] + projected
@@ -211,11 +214,11 @@
         keys = qkv[rows, CH : 2 * CH].astype(BF16)
         values = qkv[rows, 2 * CH : 3 * CH].astype(BF16)
         p = probs[s]
-        dp = nt(dm, values)
-        dv = tn(p.astype(BF16), dm).astype(BF16)
-        ds = (p * (dp - jnp.sum(p * dp, axis=-1, keepdims=True)) * SCALE).astype(BF16)
-        dq = gathered(nn(ds, keys)).astype(BF16)
-        dk = tn(ds, qm_all[s]).astype(BF16)
+        dp = nt(values, dm)
+        dv = nn(p.astype(BF16), dm).astype(BF16)
+        ds = (p * (dp - jnp.sum(p * dp, axis=0, keepdims=True)) * SCALE).astype(BF16)
+        dq = gathered(tn(ds, keys)).astype(BF16)
+        dk = nn(ds, qm_all[s]).astype(BF16)
         dqkv_s[rows, 0:CH] = dq.astype(F32)
         dqkv_s[rows, CH : 2 * CH] = dk.astype(F32)
         dqkv_s[rows, 2 * CH : 3 * CH] = dv.astype(F32)
@@ -260,8 +263,14 @@
         small[2 * i : 2 * i + 1, :] = total[:, 0:128]
         small[2 * i + 1 : 2 * i + 2, 0:64] = total[:, 128:192]
     msg[1, 18 * CH - SUMS : SUMS, :] = small[...].astype(BF16)
-    send_out[...] = msg[1 - core]
-    keep_out[...] = msg[core]
+    copies = [
+        pltpu.make_async_copy(msg.at[1 - core], send_out, sems.at[0]),
+        pltpu.make_async_copy(msg.at[core], keep_out, sems.at[1]),
+    ]
+    for copy in copies:
+        copy.start()
+    for copy in copies:
+        copy.wait()
 
 
 SMALL_ROWS = 2 * SUMS - 18 * CH
@@ -310,8 +319,7 @@
 
 
 def unpack_kernel(
-    own, other, near, from_lon, from_lat, from_both,
-    state_out, g_qkv, g_out, g_up, g_down, g_land, g_ga, g_gm, msg,
+    own, other, g_qkv, g_out, g_up, g_down, g_land, g_ga, g_gm, msg
 ):
     core = lax.axis_index("core")
     for g in range(GROUP):
@@ -342,6 +350,9 @@
         out[...] = jnp.concatenate(
             [little[2 * i : 2 * i + 1, :], little[2 * i + 1 : 2 * i + 2, 0:64]], axis=1
         )
+
+
+def state_kernel(near, from_lon, from_lat, from_both, state_out):
     for first, wide, edge in ((6, near, from_lat), (0, from_lon, from_both)):
         for tile, lanes in ((0, slice(0, 128)), (1, slice(128, 192))):
             n = lanes.stop - lanes.start
@@ -378,8 +389,10 @@
     return lax.all_to_all(value, axis, 0, 0, tiled=True)
 
 
-def call(kernel, name, outs, scratch=(), mib=8, from_hbm=0):
+def call(kernel, name, outs, scratch=(), mib=8, from_hbm=0, placed=False):
     specs = {}
+    if placed:
+        specs["out_specs"] = tuple(pl.BlockSpec(memory_space=pl.ANY) for _ in outs)
     if from_hbm:
         specs["in_specs"] = [pl.BlockSpec(memory_space=pltpu.HBM)] * from_hbm
     return pl.pallas_call(
@@ -395,10 +408,11 @@
 def local(
     states, loss_grads, land_sea, land_embed, gain_attn, gain_mlp, w_qkv, w_out, w_up, w_down
 ):
-    keep, send, edge, vectors = call(
+    keep, send, edge, vectors, w_qkv = call(
         pack_kernel,
         "pack_cells",
-        [((2, 2, HALF, MSG), BF16)] * 2 + [((2, HALF // 2, MSG), BF16), ((8, CH), F32)],
+        [((2, 2, HALF, MSG), BF16)] * 2 + [((2, HALF // 2, MSG), BF16), ((8, CH), F32)]
+        + [((CH, 3 * CH), BF16)],
         [
             ((WIN_LON, ROWS, CH), BF16),
             ((WIN_LON, ROWS, CH), BF16),
@@ -406,12 +420,17 @@
             ((8, CH), F32),
             ((2, 2, 2, HALF, MSG), F32),
             ((2, HALF // 2, MSG), F32),
-            (pltpu.SemaphoreType.DMA((6,)), None),
+            (pltpu.SemaphoreType.DMA((7,)), None),
         ],
-        from_hbm=6,
+        from_hbm=7,
     )(
-        states[0, 0].transpose(1, 0, 2), loss_grads[0, 0].transpose(1, 0, 2), land_sea.T,
-        land_embed[None], gain_attn[None], gain_mlp[None],
+        *(
+            pltpu.with_memory_space_constraint(value, pltpu.HBM)
+            for value in (
+                states[0, 0].transpose(1, 0, 2), loss_grads[0, 0].transpose(1, 0, 2), land_sea.T,
+                land_embed[None], gain_attn[None], gain_mlp[None], w_qkv,
+            )
+        )
     )
     near_own, near_x, lon_own, lon_x = call(
         sort_kernel,
@@ -432,7 +451,7 @@
         [
             ((STEPS, WIN, MSG), F32),
             ((TOK, 3 * CH), F32),
-            ((STEPS, HEADS * WIN, WIN), F32),
+            ((STEPS, WIN, HEADS * WIN), F32),
             ((STEPS, HEADS * WIN, CH), BF16),
             ((TOK, CH), F32),
             ((TOK, CH), F32),
@@ -451,9 +470,13 @@
             ((WIN, 256), F32),
             ((SMALL_ROWS, 128), F32),
             ((2, SENT, 128), BF16),
+            (pltpu.SemaphoreType.DMA((2,)), None),
         ],
         mib=24,
-    )(near_own, near_x, lon_own, lon_x, vectors, w_qkv, w_out, w_up, w_down.T)
+        placed=True,
+    )(
+        near_own, near_x, lon_own, lon_x, vectors, w_qkv, w_out, w_up, w_down.T
+    )
 
     chunks, x_send, x_keep = call(
         pair_kernel,
@@ -477,11 +500,13 @@
     own, from_lon, from_lat, from_both = lax.optimization_barrier(
         (exchange(total, ("xh", "lon")), from_lon, from_lat, from_both)
     )
+    (state_grads,) = call(state_kernel, "unpack_states", [((WIN_LON, ROWS, CH), F32)])(
+        near, from_lon, from_lat, from_both
+    )
     outs = call(
         unpack_kernel,
         "unpack_sums",
         [
-            ((WIN_LON, ROWS, CH), F32),
             ((CH, 3 * CH), F32),
             ((CH, CH), F32),
             ((CH, MLP), F32),
@@ -492,10 +517,10 @@
         ],
         [((2, SUMS, 128), BF16)],
         mib=16,
-    )(own, swap(own, "core"), near, from_lon, from_lat, from_both)
+    )(own, swap(own, "core"))
     return (
-        outs[0].transpose(1, 0, 2)[None, None],
-        outs[1], outs[2], outs[3], outs[4].T, outs[5][0], outs[6][0], outs[7][0],
+        state_grads.transpose(1, 0, 2)[None, None],
+        outs[0], outs[1], outs[2], outs[3].T, outs[4][0], outs[5][0], outs[6][0],
     )
 
 

time: 90.1 us -> 83.8 us (0.930)
  waiting for transfers between devices: 27.4 us -> 23.2 us
  local copies, waits for them, and re-layouts: 3.47 us -> 0.01 us
  Pallas kernels: 12.2 us -> 13.3 us
    ppermute x8, waiting for transfers between devices: 16.6 us -> 13.1 us  [hop(): return lax.ppermute(value, AXES, pairs)]
    unnamed x20 -> x6, local copies, waits for them, and re-layouts: 3.47 us -> 0.01 us
    pallas_call x1 -> x2, Pallas kernels: 1.44 us -> 2.14 us  [the longest x1 1.37 us: local(): call(unpack_kernel, 'unpack_sums', [((CH, 3 * CH), F32), ((CH, CH), F32),...]
  transfers between devices with their start and end apart: 14 -> 14, of which waited for: 9 -> 8; matrix products, arithmetic and copies ran while one was open for 0% -> 0% of each run, Pallas kernels for 0% -> 1%
where the time goes in v4:
time: 83.8 us; the launch traced here: 83.5 us
  starting transfers between devices  33.2 us (40%)
  waiting for transfers between devices  23.2 us (28%)
  Pallas kernels  13.3 us (16%)
  blocking collectives  13 us (16%)
    ppermute x8, starting transfers between devices, hop(): return lax.ppermute(value, AXES, pairs)  16.2 us
    ppermute x8, waiting for transfers between devices, hop(): return lax.ppermute(value, AXES, pairs)  13.1 us
    all_to_all x1, blocking collectives, exchange(): return lax.all_to_all(value, axis, 0, 0, tiled=True)  13 us
    ppermute x4, starting transfers between devices, swap(): return lax.ppermute(value, axis, [(0, 1), (1, 0)])  9.84 us
    pallas_call x1, Pallas kernels, local(): call(main_kernel, 'window_steps', [((SENT, 128), BF16)] * 2, [((STEPS, WI...  7.87 us
    all_to_all x2, starting transfers between devices, exchange(): return lax.all_to_all(value, axis, 0, 0, tiled=True)  7.24 us
    ppermute x4, waiting for transfers between devices, swap(): return lax.ppermute(value, axis, [(0, 1), (1, 0)])  6.28 us
    all_to_all x2, waiting for transfers between devices, exchange(): return lax.all_to_all(value, axis, 0, 0, tiled=True)  3.81 us
  transfers between devices with their start and end apart: 14, of which 8 were waited for; matrix products, arithmetic and copies ran while one was open for 0% of the time, Pallas kernels for 1%

profile of v4, /device:TPU:1, one launch (start us, length us, event | category | flops | bytes accessed | tf_op | source)
XLA Modules:
  0.0 83.5 jit_solution(5071193072327869377)
XLA Ops:
  0.6 1.4 %pack_cells.1 = (bf16[2,2,36,512]{3,2,1,0:T(8,128)(2,1)S(1)}, bf16[2,2,36,512]{3,2,1,0:T(8,128)(2,1)S(1)}, bf16[2,18,512]{2,1,0:T(8,128)(2,1)S(1)}, f32[8,192]{1,0:T(8,128)S(1)}, bf16[192,576]{1,0:T(8,128)(2,1)S(1)}) custom-call(bf16[12,24,192]{2,1,0:T(8,128)(2,1)} %bitcast.20, bf16[12,24,192]{2,1,0:T(8,128)(2,1)} %bitcast.21, s32[12,24]{1,0:T(8,128)} %bitcast.22, ...), custom_call_target="tpu_custom_call" | custom-call | tf_op jit(solution)/shard_map/pack_cells/pallas_call | solution.py:411
  2.1 3.3 %collective-permute-start = (bf16[2,2,36,512]{3,2,1,0:T(8,128)(2,1)S(1)}, bf16[2,2,36,512]{3,2,1,0:T(8,128)(2,1)S(1)}, u32[]{:S(2)}, u32[]{:S(2)}) collective-permute-start(bf16[2,2,36,512]{3,2,1,0:T(8,128)(2,1)S(1)} %get-tuple-element.39), channel_id=1, source_target_pairs={{0,64},{64,0},{1,65},{65,1},{2,66},{66,2},{3,67},{67,3},{4,68},{68... | collective-permute-start | bytes 442376 | tf_op jit(solution)/shard_map/ppermute | solution.py:385
  5.4 1.3 %collective-permute-start.1 = (bf16[2,18,512]{2,1,0:T(8,128)(2,1)S(1)}, bf16[2,18,512]{2,1,0:T(8,128)(2,1)S(1)}, u32[]{:S(2)}, u32[]{:S(2)}) collective-permute-start(bf16[2,18,512]{2,1,0:T(8,128)(2,1)S(1)} %get-tuple-element.40), channel_id=1, source_target_pairs={{0,120},{1,121},{2,122},{3,123},{4,124},{5,125},{6,126},{7,127},{8... | collective-permute-start | bytes 110600 | tf_op jit(solution)/shard_map/ppermute | solution.py:381
  6.7 5.7 %collective-permute-start.2 = (bf16[2,18,512]{2,1,0:T(8,128)(2,1)S(1)}, bf16[2,18,512]{2,1,0:T(8,128)(2,1)S(1)}, u32[]{:S(2)}, u32[]{:S(2)}) collective-permute-start(bf16[2,18,512]{2,1,0:T(8,128)(2,1)S(1)} %get-tuple-element.40), channel_id=1, source_target_pairs={{64,120},{65,121},{66,122},{67,123},{68,124},{69,125},{70,126},{71... | collective-permute-start | bytes 110600 | tf_op jit(solution)/shard_map/ppermute | solution.py:381
  12.5 1.1 %collective-permute-done.2.edge1 = bf16[2,18,512]{2,1,0:T(8,128)(2,1)S(1)} collective-permute-done((bf16[2,18,512]{2,1,0:T(8,128)(2,1)S(1)}, bf16[2,18,512]{2,1,0:T(8,128)(2,1)S(1)}, u32[]{:S(2)}, u32[]{:S(2)}) %collective-permute-start.2) | collective-permute-done | bytes 36896 | tf_op jit(solution)/shard_map/ppermute | solution.py:381
  13.7 2.8 %collective-permute-start.3 = (bf16[2,36,512]{2,1,0:T(8,128)(2,1)S(1)}, bf16[2,36,512]{2,1,0:T(8,128)(2,1)S(1)}, u32[]{:S(2)}, u32[]{:S(2)}) collective-permute-start(bf16[2,36,512]{2,1,0:T(8,128)(2,1)S(1)} %get-tuple-element.42), channel_id=1, source_target_pairs={{0,128},{1,129},{2,130},{3,131},{4,132},{5,133},{6,134},{7,135},{8... | collective-permute-start | bytes 221192 | tf_op jit(solution)/shard_map/ppermute | solution.py:381
  16.6 2.8 %collective-permute-start.4 = (bf16[2,36,512]{2,1,0:T(8,128)(2,1)S(1)}, bf16[2,36,512]{2,1,0:T(8,128)(2,1)S(1)}, u32[]{:S(2)}, u32[]{:S(2)}) collective-permute-start(bf16[2,36,512]{2,1,0:T(8,128)(2,1)S(1)} %get-tuple-element.43), channel_id=1, source_target_pairs={{0,7},{1,0},{2,1},{3,2},{4,3},{5,4},{6,5},{7,6},{8,15},{9,8},{10,9... | collective-permute-start | bytes 221192 | tf_op jit(solution)/shard_map/ppermute | solution.py:381
  19.3 1.0 %collective-permute-start.5 = (bf16[2,36,512]{2,1,0:T(8,128)(2,1)S(1)}, bf16[2,36,512]{2,1,0:T(8,128)(2,1)S(1)}, u32[]{:S(2)}, u32[]{:S(2)}) collective-permute-start(bf16[2,36,512]{2,1,0:T(8,128)(2,1)S(1)} %get-tuple-element.44), channel_id=1, source_target_pairs={{0,135},{1,128},{2,129},{3,130},{4,131},{5,132},{6,133},{7,134},{8... | collective-permute-start | bytes 221192 | tf_op jit(solution)/shard_map/ppermute | solution.py:381
  20.4 1.0 %collective-permute-done.4.lon_own = bf16[2,36,512]{2,1,0:T(8,128)(2,1)S(1)} collective-permute-done((bf16[2,36,512]{2,1,0:T(8,128)(2,1)S(1)}, bf16[2,36,512]{2,1,0:T(8,128)(2,1)S(1)}, u32[]{:S(2)}, u32[]{:S(2)}) %collective-permute-start.4) | collective-permute-done | bytes 73760 | tf_op jit(solution)/shard_map/ppermute | solution.py:381
  21.3 4.3 %collective-permute-done.5.lon_x = bf16[2,36,512]{2,1,0:T(8,128)(2,1)S(1)} collective-permute-done((bf16[2,36,512]{2,1,0:T(8,128)(2,1)S(1)}, bf16[2,36,512]{2,1,0:T(8,128)(2,1)S(1)}, u32[]{:S(2)}, u32[]{:S(2)}) %collective-permute-start.5) | collective-permute-done | bytes 73760 | tf_op jit(solution)/shard_map/ppermute | solution.py:381
  25.6 7.9 %window_steps.1 = (bf16[2176,128]{1,0:T(8,128)(2,1)S(1)}, bf16[2176,128]{1,0:T(8,128)(2,1)S(1)}) custom-call(bf16[2,36,512]{2,1,0:T(8,128)(2,1)S(1)} %get-tuple-element.41.near_own, bf16[2,36,512]{2,1,0:T(8,128)(2,1)S(1)} %collective-permute-done.3.near_x, bf16[2,36,512]{2,1,0:T(8,128)(2,1)S(1)} %collective-permute-done.4.lon_own, ...), custom_call_target="tpu_custom_call" | custom-call | tf_op jit(solution)/shard_map/window_steps/pallas_call | solution.py:447
  33.5 1.1 %collective-permute-start.6 = (bf16[2176,128]{1,0:T(8,128)(2,1)S(1)}, bf16[2176,128]{1,0:T(8,128)(2,1)S(1)}, u32[]{:S(2)}, u32[]{:S(2)}) collective-permute-start(bf16[2176,128]{1,0:T(8,128)(2,1)S(1)} %get-tuple-element.48), channel_id=1, source_target_pairs={{0,64},{64,0},{1,65},{65,1},{2,66},{66,2},{3,67},{67,3},{4,68},{68... | collective-permute-start | bytes 1671176 | tf_op jit(solution)/shard_map/ppermute | solution.py:385
  34.6 1.6 %collective-permute-done.6.arrived = bf16[2176,128]{1,0:T(8,128)(2,1)S(1)} collective-permute-done((bf16[2176,128]{1,0:T(8,128)(2,1)S(1)}, bf16[2176,128]{1,0:T(8,128)(2,1)S(1)}, u32[]{:S(2)}, u32[]{:S(2)}) %collective-permute-start.6) | collective-permute-done | bytes 557088 | tf_op jit(solution)/shard_map/ppermute | solution.py:385
  36.3 13.0 %all_to_all.15.terms = bf16[16,112,128]{2,1,0:T(8,128)(2,1)S(1)} all-to-all(bf16[16,112,128]{2,1,0:T(8,128)(2,1)S(1)} %get-tuple-element.49), channel_id=1, replica_groups=mesh['xh'=2,'core'=2,'lat'=8,'lon'=8] {'xh','lon'}, dimensions={0} | all-to-all | bytes 917504 | tf_op jit(solution)/shard_map/all_to_all | solution.py:389
  50.1 3.4 %all-to-all-start.1 = ((bf16[8,112,128]{2,1,0:T(8,128)(2,1)}), bf16[8,112,128]{2,1,0:T(8,128)(2,1)S(1)}, u32[]{:S(2)}, u32[]{:S(2)}) async-start(bf16[8,112,128]{2,1,0:T(8,128)(2,1)} %sum_group.1), calls=%async_computation.1 | async-start | bytes 458752 | tf_op jit(solution)/shard_map/all_to_all | solution.py:389
  53.5 1.0 %collective-permute-start.7 = (bf16[2,192,128]{2,1,0:T(8,128)(2,1)S(1)}, bf16[2,192,128]{2,1,0:T(8,128)(2,1)S(1)}, u32[]{:S(2)}, u32[]{:S(2)}) collective-permute-start(bf16[2,192,128]{2,1,0:T(8,128)(2,1)S(1)} %get-tuple-element.51), channel_id=1, source_target_pairs={{0,128},{128,0},{1,129},{129,1},{2,130},{130,2},{3,131},{131,3},{4... | collective-permute-start | bytes 294920 | tf_op jit(solution)/shard_map/ppermute | solution.py:385
  54.5 4.0 %collective-permute-done.7.arrived = bf16[2,192,128]{2,1,0:T(8,128)(2,1)S(1)} collective-permute-done((bf16[2,192,128]{2,1,0:T(8,128)(2,1)S(1)}, bf16[2,192,128]{2,1,0:T(8,128)(2,1)S(1)}, u32[]{:S(2)}, u32[]{:S(2)}) %collective-permute-start.7) | collective-permute-done | bytes 98336 | tf_op jit(solution)/shard_map/ppermute | solution.py:385
  58.5 3.8 %all-to-all-done.1.terms = bf16[8,112,128]{2,1,0:T(8,128)(2,1)S(1)} async-done(((bf16[8,112,128]{2,1,0:T(8,128)(2,1)}), bf16[8,112,128]{2,1,0:T(8,128)(2,1)S(1)}, u32[]{:S(2)}, u32[]{:S(2)}) %all-to-all-start.1) | async-done | bytes 229408 | tf_op jit(solution)/shard_map/all_to_all | solution.py:389
  63.2 3.8 %all-to-all-start.2 = ((bf16[16,112,128]{2,1,0:T(8,128)(2,1)}), bf16[16,112,128]{2,1,0:T(8,128)(2,1)S(1)}, u32[]{:S(2)}, u32[]{:S(2)}) async-start(bf16[16,112,128]{2,1,0:T(8,128)(2,1)} %get-tuple-element.53), calls=%async_computation.2 | async-start | bytes 917504 | tf_op jit(solution)/shard_map/all_to_all | solution.py:389
  67.0 1.4 %collective-permute-start.8 = (bf16[4,96,128]{2,1,0:T(8,128)(2,1)S(1)}, bf16[4,96,128]{2,1,0:T(8,128)(2,1)S(1)}, u32[]{:S(2)}, u32[]{:S(2)}) collective-permute-start(bf16[4,96,128]{2,1,0:T(8,128)(2,1)S(1)} %get-tuple-element.54), channel_id=1, source_target_pairs={{0,1},{1,2},{2,3},{3,4},{4,5},{5,6},{6,7},{7,0},{8,9},{9,10},{10,1... | collective-permute-start | bytes 294920 | tf_op jit(solution)/shard_map/ppermute | solution.py:381
  68.4 1.2 %collective-permute-start.10 = (bf16[96,128]{1,0:T(8,128)(2,1)S(1)}, bf16[96,128]{1,0:T(8,128)(2,1)S(1)}, u32[]{:S(2)}, u32[]{:S(2)}) collective-permute-start(bf16[96,128]{1,0:T(8,128)(2,1)S(1)} %get-tuple-element.56), channel_id=1, source_target_pairs={{0,9},{1,10},{2,11},{3,12},{4,13},{5,14},{6,15},{7,8},{8,17},{9,18... | collective-permute-start | bytes 73736 | tf_op jit(solution)/shard_map/ppermute | solution.py:381
  69.5 6.7 %collective-permute-done.10.from_both = bf16[96,128]{1,0:T(8,128)(2,1)S(1)} collective-permute-done((bf16[96,128]{1,0:T(8,128)(2,1)S(1)}, bf16[96,128]{1,0:T(8,128)(2,1)S(1)}, u32[]{:S(2)}, u32[]{:S(2)}) %collective-permute-start.10) | collective-permute-done | bytes 24608 | tf_op jit(solution)/shard_map/ppermute | solution.py:381
  76.3 4.4 %collective-permute-start.11 = (bf16[16,112,128]{2,1,0:T(8,128)(2,1)S(1)}, bf16[16,112,128]{2,1,0:T(8,128)(2,1)S(1)}, u32[]{:S(2)}, u32[]{:S(2)}) collective-permute-start(bf16[16,112,128]{2,1,0:T(8,128)(2,1)S(1)} %all-to-all-done.2.own), channel_id=1, source_target_pairs={{0,64},{64,0},{1,65},{65,1},{2,66},{66,2},{3,67},{67,3},{4,68},{68... | collective-permute-start | bytes 1376264 | tf_op jit(solution)/shard_map/ppermute | solution.py:385
  82.1 1.4 %unpack_sums.1 = (f32[192,576]{1,0:T(8,128)}, f32[192,192]{1,0:T(8,128)}, f32[192,768]{1,0:T(8,128)}, f32[192,768]{1,0:T(8,128)}, f32[1,192]{1,0:T(1,128)}, /*index=5*/f32[1,192]{1,0:T(1,128)}, f32[1,192]{1,0:T(1,128)}) custom-call(bf16[16,112,128]{2,1,0:T(8,128)(2,1)S(1)} %all-to-all-done.2.own, bf16[16,112,128]{2,1,0:T(8,128)(2,1)S(1)} %collective-permute-done.11.other), custom_call_target="tpu_custom_call" | custom-call | tf_op jit(solution)/shard_map/unpack_sums/pallas_call | solution.py:506
  (19 shorter events, 3.4 us)
Async XLA Ops:
  0.6 25.0 %copy-start.1 = (bf16[768,192]{0,1:T(8,128)(2,1)S(1)}, bf16[768,192]{0,1:T(8,128)(2,1)}, u32[]{:S(2)}) copy-start(bf16[768,192]{0,1:T(8,128)(2,1)} %param.19) | copy-start | bytes 884740
  2.1 23.5 %copy-start = (bf16[192,768]{1,0:T(8,128)(2,1)S(1)}, bf16[192,768]{1,0:T(8,128)(2,1)}, u32[]{:S(2)}) copy-start(bf16[192,768]{1,0:T(8,128)(2,1)} %wup.1) | copy-start | bytes 884740
  2.1 11.5 %collective-permute-start = (bf16[2,2,36,512]{3,2,1,0:T(8,128)(2,1)S(1)}, bf16[2,2,36,512]{3,2,1,0:T(8,128)(2,1)S(1)}, u32[]{:S(2)}, u32[]{:S(2)}) collective-permute-start(bf16[2,2,36,512]{3,2,1,0:T(8,128)(2,1)S(1)} %get-tuple-element.39), channel_id=1, source_target_pairs={{0,64},{64,0},{1,65},{65,1},{2,66},{66,2},{3,67},{67,3},{4,68},{68... | collective-permute-start | bytes 442376 | tf_op jit(solution)/shard_map/ppermute | solution.py:385
  5.4 7.0 %collective-permute-start.1 = (bf16[2,18,512]{2,1,0:T(8,128)(2,1)S(1)}, bf16[2,18,512]{2,1,0:T(8,128)(2,1)S(1)}, u32[]{:S(2)}, u32[]{:S(2)}) collective-permute-start(bf16[2,18,512]{2,1,0:T(8,128)(2,1)S(1)} %get-tuple-element.40), channel_id=1, source_target_pairs={{0,120},{1,121},{2,122},{3,123},{4,124},{5,125},{6,126},{7,127},{8... | collective-permute-start | bytes 110600 | tf_op jit(solution)/shard_map/ppermute | solution.py:381
  6.7 6.9 %collective-permute-start.2 = (bf16[2,18,512]{2,1,0:T(8,128)(2,1)S(1)}, bf16[2,18,512]{2,1,0:T(8,128)(2,1)S(1)}, u32[]{:S(2)}, u32[]{:S(2)}) collective-permute-start(bf16[2,18,512]{2,1,0:T(8,128)(2,1)S(1)} %get-tuple-element.40), channel_id=1, source_target_pairs={{64,120},{65,121},{66,122},{67,123},{68,124},{69,125},{70,126},{71... | collective-permute-start | bytes 110600 | tf_op jit(solution)/shard_map/ppermute | solution.py:381
  13.6 12.0 %copy-start.2 = (bf16[192,192]{1,0:T(8,128)(2,1)S(1)}, bf16[192,192]{1,0:T(8,128)(2,1)}, u32[]{:S(2)}) copy-start(bf16[192,192]{1,0:T(8,128)(2,1)} %wout.1) | copy-start | bytes 221188
  13.7 6.6 %collective-permute-start.3 = (bf16[2,36,512]{2,1,0:T(8,128)(2,1)S(1)}, bf16[2,36,512]{2,1,0:T(8,128)(2,1)S(1)}, u32[]{:S(2)}, u32[]{:S(2)}) collective-permute-start(bf16[2,36,512]{2,1,0:T(8,128)(2,1)S(1)} %get-tuple-element.42), channel_id=1, source_target_pairs={{0,128},{1,129},{2,130},{3,131},{4,132},{5,133},{6,134},{7,135},{8... | collective-permute-start | bytes 221192 | tf_op jit(solution)/shard_map/ppermute | solution.py:381
  16.6 4.7 %collective-permute-start.4 = (bf16[2,36,512]{2,1,0:T(8,128)(2,1)S(1)}, bf16[2,36,512]{2,1,0:T(8,128)(2,1)S(1)}, u32[]{:S(2)}, u32[]{:S(2)}) collective-permute-start(bf16[2,36,512]{2,1,0:T(8,128)(2,1)S(1)} %get-tuple-element.43), channel_id=1, source_target_pairs={{0,7},{1,0},{2,1},{3,2},{4,3},{5,4},{6,5},{7,6},{8,15},{9,8},{10,9... | collective-permute-start | bytes 221192 | tf_op jit(solution)/shard_map/ppermute | solution.py:381
  19.3 6.3 %collective-permute-start.5 = (bf16[2,36,512]{2,1,0:T(8,128)(2,1)S(1)}, bf16[2,36,512]{2,1,0:T(8,128)(2,1)S(1)}, u32[]{:S(2)}, u32[]{:S(2)}) collective-permute-start(bf16[2,36,512]{2,1,0:T(8,128)(2,1)S(1)} %get-tuple-element.44), channel_id=1, source_target_pairs={{0,135},{1,128},{2,129},{3,130},{4,131},{5,132},{6,133},{7,134},{8... | collective-permute-start | bytes 221192 | tf_op jit(solution)/shard_map/ppermute | solution.py:381
  33.5 2.7 %collective-permute-start.6 = (bf16[2176,128]{1,0:T(8,128)(2,1)S(1)}, bf16[2176,128]{1,0:T(8,128)(2,1)S(1)}, u32[]{:S(2)}, u32[]{:S(2)}) collective-permute-start(bf16[2176,128]{1,0:T(8,128)(2,1)S(1)} %get-tuple-element.48), channel_id=1, source_target_pairs={{0,64},{64,0},{1,65},{65,1},{2,66},{66,2},{3,67},{67,3},{4,68},{68... | collective-permute-start | bytes 1671176 | tf_op jit(solution)/shard_map/ppermute | solution.py:385
  50.1 12.2 %all-to-all-start.1 = ((bf16[8,112,128]{2,1,0:T(8,128)(2,1)}), bf16[8,112,128]{2,1,0:T(8,128)(2,1)S(1)}, u32[]{:S(2)}, u32[]{:S(2)}) async-start(bf16[8,112,128]{2,1,0:T(8,128)(2,1)} %sum_group.1), calls=%async_computation.1 | async-start | bytes 458752 | tf_op jit(solution)/shard_map/all_to_all | solution.py:389
  53.5 5.1 %collective-permute-start.7 = (bf16[2,192,128]{2,1,0:T(8,128)(2,1)S(1)}, bf16[2,192,128]{2,1,0:T(8,128)(2,1)S(1)}, u32[]{:S(2)}, u32[]{:S(2)}) collective-permute-start(bf16[2,192,128]{2,1,0:T(8,128)(2,1)S(1)} %get-tuple-element.51), channel_id=1, source_target_pairs={{0,128},{128,0},{1,129},{129,1},{2,130},{130,2},{3,131},{131,3},{4... | collective-permute-start | bytes 294920 | tf_op jit(solution)/shard_map/ppermute | solution.py:385
  63.2 13.1 %all-to-all-start.2 = ((bf16[16,112,128]{2,1,0:T(8,128)(2,1)}), bf16[16,112,128]{2,1,0:T(8,128)(2,1)S(1)}, u32[]{:S(2)}, u32[]{:S(2)}) async-start(bf16[16,112,128]{2,1,0:T(8,128)(2,1)} %get-tuple-element.53), calls=%async_computation.2 | async-start | bytes 917504 | tf_op jit(solution)/shard_map/all_to_all | solution.py:389
  67.0 9.2 %collective-permute-start.8 = (bf16[4,96,128]{2,1,0:T(8,128)(2,1)S(1)}, bf16[4,96,128]{2,1,0:T(8,128)(2,1)S(1)}, u32[]{:S(2)}, u32[]{:S(2)}) collective-permute-start(bf16[4,96,128]{2,1,0:T(8,128)(2,1)S(1)} %get-tuple-element.54), channel_id=1, source_target_pairs={{0,1},{1,2},{2,3},{3,4},{4,5},{5,6},{6,7},{7,0},{8,9},{9,10},{10,1... | collective-permute-start | bytes 294920 | tf_op jit(solution)/shard_map/ppermute | solution.py:381
  68.4 7.8 %collective-permute-start.10 = (bf16[96,128]{1,0:T(8,128)(2,1)S(1)}, bf16[96,128]{1,0:T(8,128)(2,1)S(1)}, u32[]{:S(2)}, u32[]{:S(2)}) collective-permute-start(bf16[96,128]{1,0:T(8,128)(2,1)S(1)} %get-tuple-element.56), channel_id=1, source_target_pairs={{0,9},{1,10},{2,11},{3,12},{4,13},{5,14},{6,15},{7,8},{8,17},{9,18... | collective-permute-start | bytes 73736 | tf_op jit(solution)/shard_map/ppermute | solution.py:381
  69.5 6.7 %collective-permute-start.9 = (bf16[96,128]{1,0:T(8,128)(2,1)S(1)}, bf16[96,128]{1,0:T(8,128)(2,1)S(1)}, u32[]{:S(2)}, u32[]{:S(2)}) collective-permute-start(bf16[96,128]{1,0:T(8,128)(2,1)S(1)} %get-tuple-element.55), channel_id=1, source_target_pairs={{0,8},{1,9},{2,10},{3,11},{4,12},{5,13},{6,14},{7,15},{8,16},{9,17... | collective-permute-start | bytes 73736 | tf_op jit(solution)/shard_map/ppermute | solution.py:381
  76.3 5.8 %collective-permute-start.11 = (bf16[16,112,128]{2,1,0:T(8,128)(2,1)S(1)}, bf16[16,112,128]{2,1,0:T(8,128)(2,1)S(1)}, u32[]{:S(2)}, u32[]{:S(2)}) collective-permute-start(bf16[16,112,128]{2,1,0:T(8,128)(2,1)S(1)} %all-to-all-done.2.own), channel_id=1, source_target_pairs={{0,64},{64,0},{1,65},{65,1},{2,66},{66,2},{3,67},{67,3},{4,68},{68... | collective-permute-start | bytes 1376264 | tf_op jit(solution)/shard_map/ppermute | solution.py:385

commit v5 on v4

--- a/solution.py
+++ b/solution.py
@@ -24,6 +24,8 @@
 BLOCK = 48
 QUARTER = 4 * BLOCK
 SENT = SUMS + 2 * QUARTER
+HALF_CH = CH // 2
+TILED = 18 * HALF_CH
 SCALE = HEAD_DIM ** (-0.5)
 EPS = 1e-05
 F32 = jnp.float32
@@ -113,7 +115,7 @@
     near_own, near_x, lon_own, lon_x, vectors, wqkv, wout, wup, wdown_t,
     send_out, keep_out,
     x, qkv, probs, qm_all, emb, xh1, r1, hid_xh, r2, gp, act, normed_s, mixed_s, nm_s,
-    cot_s, dpre_s, dproj_s, dqkv_s, dstate, small, msg, sems,
+    cot_s, dpre_s, dproj_s, dqkv_s, dstate, small, msg,
 ):
     core = lax.axis_index("core")
     here = lax.axis_index("xh")
@@ -235,45 +237,37 @@
         for half in range(2):
             piece = dstate[HALF * half : HALF * half + HALF, :]
             for tile in range(2):
-                at = SUMS + QUARTER * (s // 2) + BLOCK * (2 * half + tile)
+                at = QUARTER * (s // 2) + BLOCK * (2 * half + tile)
                 block = jnp.concatenate([piece[:, 128 * tile : 128 * tile + 128], zero_rows], axis=0)
                 msg[s % 2, at : at + BLOCK, :] = block.astype(BF16)
 
     factor = float(STEPS * 192 * 96) ** (-0.5)
 
+    def own_first(v):
+        return jnp.where(core == 0, v, jnp.concatenate([v[:, HALF_CH:], v[:, :HALF_CH]], axis=1))
+
     def put(tile, value):
+        value = (value * factor).astype(BF16)
         for j in range(value.shape[1] // 128):
-            start = (tile + j) * CH
-            done = 0
-            while done < CH:
-                part, row = divmod(start + done, SUMS)
-                n = min(CH - done, SUMS - row)
-                msg[part, row : row + n, :] = value[done : done + n, 128 * j : 128 * j + 128]
-                done += n
-
-    cot_all = cot_s[...].astype(BF16)
-    put(12, (tn(cot_all, act[...]) * factor).astype(BF16))
-    put(6, (tn(nm_s[...], dpre_s[...].astype(BF16)) * factor).astype(BF16))
-    g_qkv = tn(normed_s[...].astype(BF16), dqkv_s[...].astype(BF16)) * factor
-    g_out = tn(mixed_s[...].astype(BF16), dproj_s[...].astype(BF16)) * factor
-    put(0, jnp.concatenate([g_qkv, g_out], axis=1).astype(BF16))
+            at = (tile + j) * HALF_CH
+            piece = value[:, 128 * j : 128 * j + 128]
+            keep_out[at : at + HALF_CH, :] = piece[:HALF_CH]
+            send_out[at : at + HALF_CH, :] = piece[HALF_CH:]
+
+    put(12, tn(own_first(cot_s[...]).astype(BF16), act[...]))
+    put(6, tn(own_first(nm_s[...]), dpre_s[...].astype(BF16)))
+    g_qkv = tn(own_first(normed_s[...]).astype(BF16), dqkv_s[...].astype(BF16))
+    g_out = tn(own_first(mixed_s[...]).astype(BF16), dproj_s[...].astype(BF16))
+    put(0, jnp.concatenate([g_qkv, g_out], axis=1))
     small[...] = jnp.zeros_like(small)
     for i, total in enumerate((land_sum, gain_a_sum, gain_m_sum)):
         total = total * factor
         small[2 * i : 2 * i + 1, :] = total[:, 0:128]
         small[2 * i + 1 : 2 * i + 2, 0:64] = total[:, 128:192]
-    msg[1, 18 * CH - SUMS : SUMS, :] = small[...].astype(BF16)
-    copies = [
-        pltpu.make_async_copy(msg.at[1 - core], send_out, sems.at[0]),
-        pltpu.make_async_copy(msg.at[core], keep_out, sems.at[1]),
-    ]
-    for copy in copies:
-        copy.start()
-    for copy in copies:
-        copy.wait()
-
-
-SMALL_ROWS = 2 * SUMS - 18 * CH
+    keep_out[TILED:SUMS, :] = jnp.where(core == 1, small[...], 0.0).astype(BF16)
+    send_out[TILED:SUMS, :] = jnp.where(core == 1, 0.0, small[...]).astype(BF16)
+    keep_out[SUMS:SENT, :] = msg[core]
+    send_out[SUMS:SENT, :] = msg[1 - core]
 
 
 def pair_kernel(kept, arrived, chunks, x_send, x_keep):
@@ -318,34 +312,25 @@
         total_out[g] = total
 
 
-def unpack_kernel(
-    own, other, g_qkv, g_out, g_up, g_down, g_land, g_ga, g_gm, msg
-):
+def unpack_kernel(own, other, g_qkv, g_out, g_up, g_down, g_land, g_ga, g_gm):
     core = lax.axis_index("core")
-    for g in range(GROUP):
-        msg[core, UNIT * g : UNIT * g + UNIT, :] = own[g]
-        msg[1 - core, UNIT * g : UNIT * g + UNIT, :] = other[g]
-
-    def rows_of(start, count):
-        pieces = []
-        done = 0
-        while done < count:
-            part, row = divmod(start + done, SUMS)
-            n = min(count - done, SUMS - row)
-            pieces.append(msg[part, row : row + n, :].astype(F32))
-            done += n
-        return pieces[0] if len(pieces) == 1 else jnp.concatenate(pieces, axis=0)
-
-    for j in range(4):
-        g_qkv[:, 128 * j : 128 * j + 128] = rows_of(j * CH, CH)
-    mid = rows_of(4 * CH, CH)
-    tail = rows_of(5 * CH, CH)
-    g_qkv[:, 512:576] = mid[:, 0:64]
-    g_out[...] = jnp.concatenate([mid[:, 64:128], tail], axis=1)
-    for j in range(6):
-        g_up[:, 128 * j : 128 * j + 128] = rows_of((6 + j) * CH, CH)
-        g_down[:, 128 * j : 128 * j + 128] = rows_of((12 + j) * CH, CH)
-    little = rows_of(18 * CH, 16)
+    for rows, half in ((core, own), (1 - core, other)):
+        to = pl.ds(pl.multiple_of(HALF_CH * rows, 32), HALF_CH)
+
+        def tile(t):
+            return half[HALF_CH * t : HALF_CH * t + HALF_CH, :].astype(F32)
+
+        for j in range(4):
+            g_qkv[to, 128 * j : 128 * j + 128] = tile(j)
+        mid = tile(4)
+        g_qkv[to, 512:576] = mid[:, 0:64]
+        g_out[to, :] = jnp.concatenate([mid[:, 64:128], tile(5)], axis=1)
+        for j in range(6):
+            g_up[to, 128 * j : 128 * j + 128] = tile(6 + j)
+            g_down[to, 128 * j : 128 * j + 128] = tile(12 + j)
+    little = jnp.where(
+        core == 1, own[TILED : TILED + 16, :].astype(F32), other[TILED : TILED + 16, :].astype(F32)
+    )
     for i, out in enumerate((g_land, g_ga, g_gm)):
         out[...] = jnp.concatenate(
             [little[2 * i : 2 * i + 1, :], little[2 * i + 1 : 2 * i + 2, 0:64]], axis=1
@@ -389,10 +374,8 @@
     return lax.all_to_all(value, axis, 0, 0, tiled=True)
 
 
-def call(kernel, name, outs, scratch=(), mib=8, from_hbm=0, placed=False):
+def call(kernel, name, outs, scratch=(), mib=8, from_hbm=0):
     specs = {}
-    if placed:
-        specs["out_specs"] = tuple(pl.BlockSpec(memory_space=pl.ANY) for _ in outs)
     if from_hbm:
         specs["in_specs"] = [pl.BlockSpec(memory_space=pltpu.HBM)] * from_hbm
     return pl.pallas_call(
@@ -468,12 +451,10 @@
             ((TOK, CH), F32),
             ((TOK, 3 * CH), F32),
             ((WIN, 256), F32),
-            ((SMALL_ROWS, 128), F32),
-            ((2, SENT, 128), BF16),
-            (pltpu.SemaphoreType.DMA((2,)), None),
+            ((SUMS - TILED, 128), F32),
+            ((2, 2 * QUARTER, 128), BF16),
         ],
         mib=24,
-        placed=True,
     )(
         near_own, near_x, lon_own, lon_x, vectors, w_qkv, w_out, w_up, w_down.T
     )
@@ -500,6 +481,7 @@
     own, from_lon, from_lat, from_both = lax.optimization_barrier(
         (exchange(total, ("xh", "lon")), from_lon, from_lat, from_both)
     )
+    own = own.reshape(SUMS, 128)
     (state_grads,) = call(state_kernel, "unpack_states", [((WIN_LON, ROWS, CH), F32)])(
         near, from_lon, from_lat, from_both
     )
@@ -515,7 +497,6 @@
             ((1, CH), F32),
             ((1, CH), F32),
         ],
-        [((2, SUMS, 128), BF16)],
         mib=16,
     )(own, swap(own, "core"))
     return (

time: 83.8 us -> 83.8 us (level)
  no operation moved by 1% of the time
where the time goes in v5:
time: 83.8 us; the launch traced here: 83.5 us
  starting transfers between devices  33.2 us (40%)
  waiting for transfers between devices  23.2 us (28%)
  Pallas kernels  13.3 us (16%)
  blocking collectives  13 us (16%)
    ppermute x8, starting transfers between devices, hop(): return lax.ppermute(value, AXES, pairs)  16.2 us
    ppermute x8, waiting for transfers between devices, hop(): return lax.ppermute(value, AXES, pairs)  13.1 us
    all_to_all x1, blocking collectives, exchange(): return lax.all_to_all(value, axis, 0, 0, tiled=True)  13 us
    ppermute x4, starting transfers between devices, swap(): return lax.ppermute(value, axis, [(0, 1), (1, 0)])  9.84 us
    pallas_call x1, Pallas kernels, local(): call(main_kernel, 'window_steps', [((SENT, 128), BF16)] * 2, [((STEPS, WI...  7.96 us
    all_to_all x2, starting transfers between devices, exchange(): return lax.all_to_all(value, axis, 0, 0, tiled=True)  7.23 us
    ppermute x4, waiting for transfers between devices, swap(): return lax.ppermute(value, axis, [(0, 1), (1, 0)])  6.28 us
    all_to_all x2, waiting for transfers between devices, exchange(): return lax.all_to_all(value, axis, 0, 0, tiled=True)  3.81 us
  transfers between devices with their start and end apart: 14, of which 8 were waited for; matrix products, arithmetic and copies ran while one was open for 0% of the time, Pallas kernels for 1%

profile of v5, /device:TPU:1, one launch (start us, length us, event | category | flops | bytes accessed | tf_op | source)
XLA Modules:
  0.0 83.5 jit_solution(2985838687553205334)
XLA Ops:
  0.6 1.4 %pack_cells.1 = (bf16[2,2,36,512]{3,2,1,0:T(8,128)(2,1)S(1)}, bf16[2,2,36,512]{3,2,1,0:T(8,128)(2,1)S(1)}, bf16[2,18,512]{2,1,0:T(8,128)(2,1)S(1)}, f32[8,192]{1,0:T(8,128)S(1)}, bf16[192,576]{1,0:T(8,128)(2,1)S(1)}) custom-call(bf16[12,24,192]{2,1,0:T(8,128)(2,1)} %bitcast.23, bf16[12,24,192]{2,1,0:T(8,128)(2,1)} %bitcast.24, s32[12,24]{1,0:T(8,128)} %bitcast.25, ...), custom_call_target="tpu_custom_call" | custom-call | tf_op jit(solution)/shard_map/pack_cells/pallas_call | solution.py:394
  2.1 3.3 %collective-permute-start = (bf16[2,2,36,512]{3,2,1,0:T(8,128)(2,1)S(1)}, bf16[2,2,36,512]{3,2,1,0:T(8,128)(2,1)S(1)}, u32[]{:S(2)}, u32[]{:S(2)}) collective-permute-start(bf16[2,2,36,512]{3,2,1,0:T(8,128)(2,1)S(1)} %get-tuple-element.39), channel_id=1, source_target_pairs={{0,64},{64,0},{1,65},{65,1},{2,66},{66,2},{3,67},{67,3},{4,68},{68... | collective-permute-start | bytes 442376 | tf_op jit(solution)/shard_map/ppermute | solution.py:370
  5.4 1.3 %collective-permute-start.1 = (bf16[2,18,512]{2,1,0:T(8,128)(2,1)S(1)}, bf16[2,18,512]{2,1,0:T(8,128)(2,1)S(1)}, u32[]{:S(2)}, u32[]{:S(2)}) collective-permute-start(bf16[2,18,512]{2,1,0:T(8,128)(2,1)S(1)} %get-tuple-element.40), channel_id=1, source_target_pairs={{0,120},{1,121},{2,122},{3,123},{4,124},{5,125},{6,126},{7,127},{8... | collective-permute-start | bytes 110600 | tf_op jit(solution)/shard_map/ppermute | solution.py:366
  6.7 5.7 %collective-permute-start.2 = (bf16[2,18,512]{2,1,0:T(8,128)(2,1)S(1)}, bf16[2,18,512]{2,1,0:T(8,128)(2,1)S(1)}, u32[]{:S(2)}, u32[]{:S(2)}) collective-permute-start(bf16[2,18,512]{2,1,0:T(8,128)(2,1)S(1)} %get-tuple-element.40), channel_id=1, source_target_pairs={{64,120},{65,121},{66,122},{67,123},{68,124},{69,125},{70,126},{71... | collective-permute-start | bytes 110600 | tf_op jit(solution)/shard_map/ppermute | solution.py:366
  12.5 1.1 %collective-permute-done.2.edge1 = bf16[2,18,512]{2,1,0:T(8,128)(2,1)S(1)} collective-permute-done((bf16[2,18,512]{2,1,0:T(8,128)(2,1)S(1)}, bf16[2,18,512]{2,1,0:T(8,128)(2,1)S(1)}, u32[]{:S(2)}, u32[]{:S(2)}) %collective-permute-start.2) | collective-permute-done | bytes 36896 | tf_op jit(solution)/shard_map/ppermute | solution.py:366
  13.7 2.8 %collective-permute-start.3 = (bf16[2,36,512]{2,1,0:T(8,128)(2,1)S(1)}, bf16[2,36,512]{2,1,0:T(8,128)(2,1)S(1)}, u32[]{:S(2)}, u32[]{:S(2)}) collective-permute-start(bf16[2,36,512]{2,1,0:T(8,128)(2,1)S(1)} %get-tuple-element.42), channel_id=1, source_target_pairs={{0,128},{1,129},{2,130},{3,131},{4,132},{5,133},{6,134},{7,135},{8... | collective-permute-start | bytes 221192 | tf_op jit(solution)/shard_map/ppermute | solution.py:366
  16.6 2.8 %collective-permute-start.4 = (bf16[2,36,512]{2,1,0:T(8,128)(2,1)S(1)}, bf16[2,36,512]{2,1,0:T(8,128)(2,1)S(1)}, u32[]{:S(2)}, u32[]{:S(2)}) collective-permute-start(bf16[2,36,512]{2,1,0:T(8,128)(2,1)S(1)} %get-tuple-element.43), channel_id=1, source_target_pairs={{0,7},{1,0},{2,1},{3,2},{4,3},{5,4},{6,5},{7,6},{8,15},{9,8},{10,9... | collective-permute-start | bytes 221192 | tf_op jit(solution)/shard_map/ppermute | solution.py:366
  19.3 1.0 %collective-permute-start.5 = (bf16[2,36,512]{2,1,0:T(8,128)(2,1)S(1)}, bf16[2,36,512]{2,1,0:T(8,128)(2,1)S(1)}, u32[]{:S(2)}, u32[]{:S(2)}) collective-permute-start(bf16[2,36,512]{2,1,0:T(8,128)(2,1)S(1)} %get-tuple-element.44), channel_id=1, source_target_pairs={{0,135},{1,128},{2,129},{3,130},{4,131},{5,132},{6,133},{7,134},{8... | collective-permute-start | bytes 221192 | tf_op jit(solution)/shard_map/ppermute | solution.py:366
  20.4 1.0 %collective-permute-done.4.lon_own = bf16[2,36,512]{2,1,0:T(8,128)(2,1)S(1)} collective-permute-done((bf16[2,36,512]{2,1,0:T(8,128)(2,1)S(1)}, bf16[2,36,512]{2,1,0:T(8,128)(2,1)S(1)}, u32[]{:S(2)}, u32[]{:S(2)}) %collective-permute-start.4) | collective-permute-done | bytes 73760 | tf_op jit(solution)/shard_map/ppermute | solution.py:366
  21.3 4.3 %collective-permute-done.5.lon_x = bf16[2,36,512]{2,1,0:T(8,128)(2,1)S(1)} collective-permute-done((bf16[2,36,512]{2,1,0:T(8,128)(2,1)S(1)}, bf16[2,36,512]{2,1,0:T(8,128)(2,1)S(1)}, u32[]{:S(2)}, u32[]{:S(2)}) %collective-permute-start.5) | collective-permute-done | bytes 73760 | tf_op jit(solution)/shard_map/ppermute | solution.py:366
  25.6 8.0 %window_steps.1 = (bf16[2176,128]{1,0:T(8,128)(2,1)S(1)}, bf16[2176,128]{1,0:T(8,128)(2,1)S(1)}) custom-call(bf16[2,36,512]{2,1,0:T(8,128)(2,1)S(1)} %get-tuple-element.41.near_own, bf16[2,36,512]{2,1,0:T(8,128)(2,1)S(1)} %collective-permute-done.3.near_x, bf16[2,36,512]{2,1,0:T(8,128)(2,1)S(1)} %collective-permute-done.4.lon_own, ...), custom_call_target="tpu_custom_call" | custom-call | tf_op jit(solution)/shard_map/window_steps/pallas_call | solution.py:430
  33.6 1.1 %collective-permute-start.6 = (bf16[2176,128]{1,0:T(8,128)(2,1)S(1)}, bf16[2176,128]{1,0:T(8,128)(2,1)S(1)}, u32[]{:S(2)}, u32[]{:S(2)}) collective-permute-start(bf16[2176,128]{1,0:T(8,128)(2,1)S(1)} %get-tuple-element.48), channel_id=1, source_target_pairs={{0,64},{64,0},{1,65},{65,1},{2,66},{66,2},{3,67},{67,3},{4,68},{68... | collective-permute-start | bytes 1671176 | tf_op jit(solution)/shard_map/ppermute | solution.py:370
  34.7 1.6 %collective-permute-done.6.arrived = bf16[2176,128]{1,0:T(8,128)(2,1)S(1)} collective-permute-done((bf16[2176,128]{1,0:T(8,128)(2,1)S(1)}, bf16[2176,128]{1,0:T(8,128)(2,1)S(1)}, u32[]{:S(2)}, u32[]{:S(2)}) %collective-permute-start.6) | collective-permute-done | bytes 557088 | tf_op jit(solution)/shard_map/ppermute | solution.py:370
  36.4 13.0 %all_to_all.15.terms = bf16[16,112,128]{2,1,0:T(8,128)(2,1)S(1)} all-to-all(bf16[16,112,128]{2,1,0:T(8,128)(2,1)S(1)} %get-tuple-element.49), channel_id=1, replica_groups=mesh['xh'=2,'core'=2,'lat'=8,'lon'=8] {'xh','lon'}, dimensions={0} | all-to-all | bytes 917504 | tf_op jit(solution)/shard_map/all_to_all | solution.py:374
  50.1 3.4 %all-to-all-start.1 = ((bf16[8,112,128]{2,1,0:T(8,128)(2,1)}), bf16[8,112,128]{2,1,0:T(8,128)(2,1)S(1)}, u32[]{:S(2)}, u32[]{:S(2)}) async-start(bf16[8,112,128]{2,1,0:T(8,128)(2,1)} %sum_group.1), calls=%async_computation.1 | async-start | bytes 458752 | tf_op jit(solution)/shard_map/all_to_all | solution.py:374
  53.6 1.0 %collective-permute-start.7 = (bf16[2,192,128]{2,1,0:T(8,128)(2,1)S(1)}, bf16[2,192,128]{2,1,0:T(8,128)(2,1)S(1)}, u32[]{:S(2)}, u32[]{:S(2)}) collective-permute-start(bf16[2,192,128]{2,1,0:T(8,128)(2,1)S(1)} %get-tuple-element.51), channel_id=1, source_target_pairs={{0,128},{128,0},{1,129},{129,1},{2,130},{130,2},{3,131},{131,3},{4... | collective-permute-start | bytes 294920 | tf_op jit(solution)/shard_map/ppermute | solution.py:370
  54.6 4.0 %collective-permute-done.7.arrived = bf16[2,192,128]{2,1,0:T(8,128)(2,1)S(1)} collective-permute-done((bf16[2,192,128]{2,1,0:T(8,128)(2,1)S(1)}, bf16[2,192,128]{2,1,0:T(8,128)(2,1)S(1)}, u32[]{:S(2)}, u32[]{:S(2)}) %collective-permute-start.7) | collective-permute-done | bytes 98336 | tf_op jit(solution)/shard_map/ppermute | solution.py:370
  58.6 3.8 %all-to-all-done.1.terms = bf16[8,112,128]{2,1,0:T(8,128)(2,1)S(1)} async-done(((bf16[8,112,128]{2,1,0:T(8,128)(2,1)}), bf16[8,112,128]{2,1,0:T(8,128)(2,1)S(1)}, u32[]{:S(2)}, u32[]{:S(2)}) %all-to-all-start.1) | async-done | bytes 229408 | tf_op jit(solution)/shard_map/all_to_all | solution.py:374
  63.2 3.8 %all-to-all-start.2 = ((bf16[16,112,128]{2,1,0:T(8,128)(2,1)}), bf16[16,112,128]{2,1,0:T(8,128)(2,1)S(1)}, u32[]{:S(2)}, u32[]{:S(2)}) async-start(bf16[16,112,128]{2,1,0:T(8,128)(2,1)} %get-tuple-element.53), calls=%async_computation.2 | async-start | bytes 917504 | tf_op jit(solution)/shard_map/all_to_all | solution.py:374
  67.1 1.4 %collective-permute-start.8 = (bf16[4,96,128]{2,1,0:T(8,128)(2,1)S(1)}, bf16[4,96,128]{2,1,0:T(8,128)(2,1)S(1)}, u32[]{:S(2)}, u32[]{:S(2)}) collective-permute-start(bf16[4,96,128]{2,1,0:T(8,128)(2,1)S(1)} %get-tuple-element.54), channel_id=1, source_target_pairs={{0,1},{1,2},{2,3},{3,4},{4,5},{5,6},{6,7},{7,0},{8,9},{9,10},{10,1... | collective-permute-start | bytes 294920 | tf_op jit(solution)/shard_map/ppermute | solution.py:366
  68.4 1.2 %collective-permute-start.10 = (bf16[96,128]{1,0:T(8,128)(2,1)S(1)}, bf16[96,128]{1,0:T(8,128)(2,1)S(1)}, u32[]{:S(2)}, u32[]{:S(2)}) collective-permute-start(bf16[96,128]{1,0:T(8,128)(2,1)S(1)} %get-tuple-element.56), channel_id=1, source_target_pairs={{0,9},{1,10},{2,11},{3,12},{4,13},{5,14},{6,15},{7,8},{8,17},{9,18... | collective-permute-start | bytes 73736 | tf_op jit(solution)/shard_map/ppermute | solution.py:366
  69.6 6.6 %collective-permute-done.10.from_both = bf16[96,128]{1,0:T(8,128)(2,1)S(1)} collective-permute-done((bf16[96,128]{1,0:T(8,128)(2,1)S(1)}, bf16[96,128]{1,0:T(8,128)(2,1)S(1)}, u32[]{:S(2)}, u32[]{:S(2)}) %collective-permute-start.10) | collective-permute-done | bytes 24608 | tf_op jit(solution)/shard_map/ppermute | solution.py:366
  76.3 4.4 %collective-permute-start.11 = (bf16[1792,128]{1,0:T(8,128)(2,1)S(1)}, bf16[1792,128]{1,0:T(8,128)(2,1)S(1)}, u32[]{:S(2)}, u32[]{:S(2)}) collective-permute-start(bf16[1792,128]{1,0:T(8,128)(2,1)S(1)} %bitcast.19), channel_id=1, source_target_pairs={{0,64},{64,0},{1,65},{65,1},{2,66},{66,2},{3,67},{67,3},{4,68},{68... | collective-permute-start | bytes 1376264 | tf_op jit(solution)/shard_map/ppermute | solution.py:370
  82.2 1.3 %unpack_sums.1 = (f32[192,576]{1,0:T(8,128)}, f32[192,192]{1,0:T(8,128)}, f32[192,768]{1,0:T(8,128)}, f32[192,768]{1,0:T(8,128)}, f32[1,192]{1,0:T(1,128)}, /*index=5*/f32[1,192]{1,0:T(1,128)}, f32[1,192]{1,0:T(1,128)}) custom-call(bf16[1792,128]{1,0:T(8,128)(2,1)S(1)} %bitcast.20, bf16[1792,128]{1,0:T(8,128)(2,1)S(1)} %collective-permute-done.11.other), custom_call_target="tpu_custom_call" | custom-call | tf_op jit(solution)/shard_map/unpack_sums/pallas_call | solution.py:488
  (19 shorter events, 3.4 us)
Async XLA Ops:
  0.6 25.0 %copy-start.1 = (bf16[768,192]{0,1:T(8,128)(2,1)S(1)}, bf16[768,192]{0,1:T(8,128)(2,1)}, u32[]{:S(2)}) copy-start(bf16[768,192]{0,1:T(8,128)(2,1)} %param.19) | copy-start | bytes 884740
  2.1 23.5 %copy-start = (bf16[192,768]{1,0:T(8,128)(2,1)S(1)}, bf16[192,768]{1,0:T(8,128)(2,1)}, u32[]{:S(2)}) copy-start(bf16[192,768]{1,0:T(8,128)(2,1)} %wup.1) | copy-start | bytes 884740
  2.1 11.5 %collective-permute-start = (bf16[2,2,36,512]{3,2,1,0:T(8,128)(2,1)S(1)}, bf16[2,2,36,512]{3,2,1,0:T(8,128)(2,1)S(1)}, u32[]{:S(2)}, u32[]{:S(2)}) collective-permute-start(bf16[2,2,36,512]{3,2,1,0:T(8,128)(2,1)S(1)} %get-tuple-element.39), channel_id=1, source_target_pairs={{0,64},{64,0},{1,65},{65,1},{2,66},{66,2},{3,67},{67,3},{4,68},{68... | collective-permute-start | bytes 442376 | tf_op jit(solution)/shard_map/ppermute | solution.py:370
  5.4 7.0 %collective-permute-start.1 = (bf16[2,18,512]{2,1,0:T(8,128)(2,1)S(1)}, bf16[2,18,512]{2,1,0:T(8,128)(2,1)S(1)}, u32[]{:S(2)}, u32[]{:S(2)}) collective-permute-start(bf16[2,18,512]{2,1,0:T(8,128)(2,1)S(1)} %get-tuple-element.40), channel_id=1, source_target_pairs={{0,120},{1,121},{2,122},{3,123},{4,124},{5,125},{6,126},{7,127},{8... | collective-permute-start | bytes 110600 | tf_op jit(solution)/shard_map/ppermute | solution.py:366
  6.7 6.9 %collective-permute-start.2 = (bf16[2,18,512]{2,1,0:T(8,128)(2,1)S(1)}, bf16[2,18,512]{2,1,0:T(8,128)(2,1)S(1)}, u32[]{:S(2)}, u32[]{:S(2)}) collective-permute-start(bf16[2,18,512]{2,1,0:T(8,128)(2,1)S(1)} %get-tuple-element.40), channel_id=1, source_target_pairs={{64,120},{65,121},{66,122},{67,123},{68,124},{69,125},{70,126},{71... | collective-permute-start | bytes 110600 | tf_op jit(solution)/shard_map/ppermute | solution.py:366
  13.6 12.0 %copy-start.2 = (bf16[192,192]{1,0:T(8,128)(2,1)S(1)}, bf16[192,192]{1,0:T(8,128)(2,1)}, u32[]{:S(2)}) copy-start(bf16[192,192]{1,0:T(8,128)(2,1)} %wout.1) | copy-start | bytes 221188
  13.7 6.6 %collective-permute-start.3 = (bf16[2,36,512]{2,1,0:T(8,128)(2,1)S(1)}, bf16[2,36,512]{2,1,0:T(8,128)(2,1)S(1)}, u32[]{:S(2)}, u32[]{:S(2)}) collective-permute-start(bf16[2,36,512]{2,1,0:T(8,128)(2,1)S(1)} %get-tuple-element.42), channel_id=1, source_target_pairs={{0,128},{1,129},{2,130},{3,131},{4,132},{5,133},{6,134},{7,135},{8... | collective-permute-start | bytes 221192 | tf_op jit(solution)/shard_map/ppermute | solution.py:366
  16.6 4.7 %collective-permute-start.4 = (bf16[2,36,512]{2,1,0:T(8,128)(2,1)S(1)}, bf16[2,36,512]{2,1,0:T(8,128)(2,1)S(1)}, u32[]{:S(2)}, u32[]{:S(2)}) collective-permute-start(bf16[2,36,512]{2,1,0:T(8,128)(2,1)S(1)} %get-tuple-element.43), channel_id=1, source_target_pairs={{0,7},{1,0},{2,1},{3,2},{4,3},{5,4},{6,5},{7,6},{8,15},{9,8},{10,9... | collective-permute-start | bytes 221192 | tf_op jit(solution)/shard_map/ppermute | solution.py:366
  19.3 6.3 %collective-permute-start.5 = (bf16[2,36,512]{2,1,0:T(8,128)(2,1)S(1)}, bf16[2,36,512]{2,1,0:T(8,128)(2,1)S(1)}, u32[]{:S(2)}, u32[]{:S(2)}) collective-permute-start(bf16[2,36,512]{2,1,0:T(8,128)(2,1)S(1)} %get-tuple-element.44), channel_id=1, source_target_pairs={{0,135},{1,128},{2,129},{3,130},{4,131},{5,132},{6,133},{7,134},{8... | collective-permute-start | bytes 221192 | tf_op jit(solution)/shard_map/ppermute | solution.py:366
  33.6 2.7 %collective-permute-start.6 = (bf16[2176,128]{1,0:T(8,128)(2,1)S(1)}, bf16[2176,128]{1,0:T(8,128)(2,1)S(1)}, u32[]{:S(2)}, u32[]{:S(2)}) collective-permute-start(bf16[2176,128]{1,0:T(8,128)(2,1)S(1)} %get-tuple-element.48), channel_id=1, source_target_pairs={{0,64},{64,0},{1,65},{65,1},{2,66},{66,2},{3,67},{67,3},{4,68},{68... | collective-permute-start | bytes 1671176 | tf_op jit(solution)/shard_map/ppermute | solution.py:370
  50.1 12.2 %all-to-all-start.1 = ((bf16[8,112,128]{2,1,0:T(8,128)(2,1)}), bf16[8,112,128]{2,1,0:T(8,128)(2,1)S(1)}, u32[]{:S(2)}, u32[]{:S(2)}) async-start(bf16[8,112,128]{2,1,0:T(8,128)(2,1)} %sum_group.1), calls=%async_computation.1 | async-start | bytes 458752 | tf_op jit(solution)/shard_map/all_to_all | solution.py:374
  53.6 5.1 %collective-permute-start.7 = (bf16[2,192,128]{2,1,0:T(8,128)(2,1)S(1)}, bf16[2,192,128]{2,1,0:T(8,128)(2,1)S(1)}, u32[]{:S(2)}, u32[]{:S(2)}) collective-permute-start(bf16[2,192,128]{2,1,0:T(8,128)(2,1)S(1)} %get-tuple-element.51), channel_id=1, source_target_pairs={{0,128},{128,0},{1,129},{129,1},{2,130},{130,2},{3,131},{131,3},{4... | collective-permute-start | bytes 294920 | tf_op jit(solution)/shard_map/ppermute | solution.py:370
  63.2 13.1 %all-to-all-start.2 = ((bf16[16,112,128]{2,1,0:T(8,128)(2,1)}), bf16[16,112,128]{2,1,0:T(8,128)(2,1)S(1)}, u32[]{:S(2)}, u32[]{:S(2)}) async-start(bf16[16,112,128]{2,1,0:T(8,128)(2,1)} %get-tuple-element.53), calls=%async_computation.2 | async-start | bytes 917504 | tf_op jit(solution)/shard_map/all_to_all | solution.py:374
  67.1 9.2 %collective-permute-start.8 = (bf16[4,96,128]{2,1,0:T(8,128)(2,1)S(1)}, bf16[4,96,128]{2,1,0:T(8,128)(2,1)S(1)}, u32[]{:S(2)}, u32[]{:S(2)}) collective-permute-start(bf16[4,96,128]{2,1,0:T(8,128)(2,1)S(1)} %get-tuple-element.54), channel_id=1, source_target_pairs={{0,1},{1,2},{2,3},{3,4},{4,5},{5,6},{6,7},{7,0},{8,9},{9,10},{10,1... | collective-permute-start | bytes 294920 | tf_op jit(solution)/shard_map/ppermute | solution.py:366
  68.4 7.8 %collective-permute-start.10 = (bf16[96,128]{1,0:T(8,128)(2,1)S(1)}, bf16[96,128]{1,0:T(8,128)(2,1)S(1)}, u32[]{:S(2)}, u32[]{:S(2)}) collective-permute-start(bf16[96,128]{1,0:T(8,128)(2,1)S(1)} %get-tuple-element.56), channel_id=1, source_target_pairs={{0,9},{1,10},{2,11},{3,12},{4,13},{5,14},{6,15},{7,8},{8,17},{9,18... | collective-permute-start | bytes 73736 | tf_op jit(solution)/shard_map/ppermute | solution.py:366
  69.6 6.7 %collective-permute-start.9 = (bf16[96,128]{1,0:T(8,128)(2,1)S(1)}, bf16[96,128]{1,0:T(8,128)(2,1)S(1)}, u32[]{:S(2)}, u32[]{:S(2)}) collective-permute-start(bf16[96,128]{1,0:T(8,128)(2,1)S(1)} %get-tuple-element.55), channel_id=1, source_target_pairs={{0,8},{1,9},{2,10},{3,11},{4,12},{5,13},{6,14},{7,15},{8,16},{9,17... | collective-permute-start | bytes 73736 | tf_op jit(solution)/shard_map/ppermute | solution.py:366
  76.3 5.8 %collective-permute-start.11 = (bf16[1792,128]{1,0:T(8,128)(2,1)S(1)}, bf16[1792,128]{1,0:T(8,128)(2,1)S(1)}, u32[]{:S(2)}, u32[]{:S(2)}) collective-permute-start(bf16[1792,128]{1,0:T(8,128)(2,1)S(1)} %bitcast.19), channel_id=1, source_target_pairs={{0,64},{64,0},{1,65},{65,1},{2,66},{66,2},{3,67},{67,3},{4,68},{68... | collective-permute-start | bytes 1376264 | tf_op jit(solution)/shard_map/ppermute | solution.py:370

commit v6 on v5

--- a/solution.py
+++ b/solution.py
@@ -23,6 +23,7 @@
 SUMS = GROUP * UNIT
 BLOCK = 48
 QUARTER = 4 * BLOCK
+COLUMNS = QUARTER // 2
 SENT = SUMS + 2 * QUARTER
 HALF_CH = CH // 2
 TILED = 18 * HALF_CH
@@ -270,19 +271,20 @@
     send_out[SUMS:SENT, :] = msg[1 - core]
 
 
-def pair_kernel(kept, arrived, chunks, x_send, x_keep):
+def pair_kernel(kept, arrived, chunks, near_own, near_x, lon_own, lon_x):
     core = lax.axis_index("core")
     here = lax.axis_index("xh")
     for g in range(GROUP):
         at = UNIT * g
         total = kept[at : at + UNIT, :].astype(F32) + arrived[at : at + UNIT, :].astype(F32)
         chunks[g] = total.astype(BF16)
-    own = pl.ds(pl.multiple_of(SUMS + QUARTER * here, 64), QUARTER)
-    other = pl.ds(pl.multiple_of(SUMS + QUARTER * (1 - here), 64), QUARTER)
-    x_send[core] = kept[other, :]
-    x_send[1 - core] = arrived[other, :]
-    x_keep[core] = kept[own, :]
-    x_keep[1 - core] = arrived[own, :]
+    for half, near, lon in ((here, near_own, lon_own), (1 - here, near_x, lon_x)):
+        first = pl.ds(pl.multiple_of(SUMS + QUARTER * half, 64), COLUMNS)
+        second = pl.ds(pl.multiple_of(SUMS + QUARTER * half + COLUMNS, 32), COLUMNS)
+        near[core] = kept[first, :]
+        near[1 - core] = arrived[first, :]
+        lon[core] = kept[second, :]
+        lon[1 - core] = arrived[second, :]
 
 
 def group_kernel(terms, total_out):
@@ -294,16 +296,15 @@
         total_out[g] = total
 
 
-def column_kernel(terms, kept, arrived, total_out, near, to_lon, to_lat, to_both):
+def column_kernel(terms, near_own, near_x, lon_own, lon_x, total_out, near, lon, to_lat):
     here = lax.axis_index("xh")
-    half = QUARTER // 2
     for c in range(2):
-        near[2 * here + c] = kept[c, 0:half, :]
-        near[2 * (1 - here) + c] = arrived[c, 0:half, :]
-        to_lon[2 * here + c] = kept[c, half:QUARTER, :]
-        to_lon[2 * (1 - here) + c] = arrived[c, half:QUARTER, :]
-    to_lat[...] = near[3]
-    to_both[...] = to_lon[3]
+        near[2 * here + c] = near_own[c]
+        near[2 * (1 - here) + c] = near_x[c]
+        lon[2 * here + c] = lon_own[c]
+        lon[2 * (1 - here) + c] = lon_x[c]
+    to_lat[0] = near[3]
+    to_lat[1] = lon[3]
     total = terms[0].astype(F32)
     for g in range(1, 8):
         total = total + terms[g].astype(F32)
@@ -337,12 +338,12 @@
         )
 
 
-def state_kernel(near, from_lon, from_lat, from_both, state_out):
-    for first, wide, edge in ((6, near, from_lat), (0, from_lon, from_both)):
+def state_kernel(near, lon, edges, state_out):
+    for part, first, wide in ((0, 6, near), (1, 0, lon)):
         for tile, lanes in ((0, slice(0, 128)), (1, slice(128, 192))):
             n = lanes.stop - lanes.start
             at = slice(BLOCK * tile, BLOCK * tile + BLOCK)
-            before = edge[at, :].astype(F32)
+            before = edges[part, at, :].astype(F32)
             for c in range(6):
                 state_out[first + c, 0:3, lanes] = before[6 * c + 3 : 6 * c + 6, 0:n]
             for k in range(4):
@@ -459,31 +460,28 @@
         near_own, near_x, lon_own, lon_x, vectors, w_qkv, w_out, w_up, w_down.T
     )
 
-    chunks, x_send, x_keep = call(
+    chunks, near_own, near_x, lon_own, lon_x = call(
         pair_kernel,
         "sum_cores",
-        [((GROUP, UNIT, 128), BF16)] + [((2, QUARTER, 128), BF16)] * 2,
+        [((GROUP, UNIT, 128), BF16)] + [((2, COLUMNS, 128), BF16)] * 4,
     )(keep, swap(send, "core"))
-    x_arrived = swap(x_send, "xh")
+    near_x = hop(near_x, 0, 0, 1)
+    lon_own = hop(lon_own, 0, 1)
+    lon_x = hop(lon_x, 0, 1, 1)
     (partial,) = call(group_kernel, "sum_group", [((8, UNIT, 128), BF16)])(
         exchange(chunks, ("xh", "lon"))
     )
-    total, near, to_lon, to_lat, to_both = call(
+    total, near, lon, to_lat = call(
         column_kernel,
         "sum_column",
         [((GROUP, UNIT, 128), BF16)]
-        + [((4, QUARTER // 2, 128), BF16)] * 2
-        + [((QUARTER // 2, 128), BF16)] * 2,
-    )(exchange(partial, "lat"), x_keep, x_arrived)
-    from_lon = hop(to_lon, 0, 1)
-    from_lat = hop(to_lat, 1, 0)
-    from_both = hop(to_both, 1, 1)
-    own, from_lon, from_lat, from_both = lax.optimization_barrier(
-        (exchange(total, ("xh", "lon")), from_lon, from_lat, from_both)
-    )
+        + [((4, COLUMNS, 128), BF16)] * 2
+        + [((2, COLUMNS, 128), BF16)],
+    )(exchange(partial, "lat"), near_own, near_x, lon_own, lon_x)
+    own, edges = lax.optimization_barrier((exchange(total, ("xh", "lon")), hop(to_lat, 1, 0)))
     own = own.reshape(SUMS, 128)
     (state_grads,) = call(state_kernel, "unpack_states", [((WIN_LON, ROWS, CH), F32)])(
-        near, from_lon, from_lat, from_both
+        near, lon, edges
     )
     outs = call(
         unpack_kernel,

time: 83.8 us -> 83.4 us (level)
  waiting for transfers between devices: 23.2 us -> 21.6 us
  starting transfers between devices: 33.2 us -> 34.3 us
    ppermute x4 -> x3, waiting for transfers between devices: 6.28 us -> 2.26 us  [swap(): return lax.ppermute(value, axis, [(0, 1), (1, 0)])]
    ppermute x8 -> x9, starting transfers between devices: 16.2 us -> 18.2 us  [hop(): return lax.ppermute(value, AXES, pairs)]
    all_to_all x2, waiting for transfers between devices: 3.81 us -> 5.55 us  [exchange(): return lax.all_to_all(value, axis, 0, 0, tiled=True)]
    ppermute x4 -> x3, starting transfers between devices: 9.84 us -> 8.9 us  [swap(): return lax.ppermute(value, axis, [(0, 1), (1, 0)])]
    ppermute x8 -> x9, waiting for transfers between devices: 13.1 us -> 13.8 us  [hop(): return lax.ppermute(value, AXES, pairs)]
  transfers between devices with their start and end apart: 14 -> 14, of which waited for: 8 -> 11; matrix products, arithmetic and copies ran while one was open for 0% -> 0% of each run, Pallas kernels for 1% -> 1%
where the time goes in v6:
time: 83.4 us; the launch traced here: 83 us
  starting transfers between devices  34.3 us (41%)
  waiting for transfers between devices  21.6 us (26%)
  Pallas kernels  13.3 us (16%)
  blocking collectives  13 us (16%)
    ppermute x9, starting transfers between devices, hop(): return lax.ppermute(value, AXES, pairs)  18.2 us
    ppermute x9, waiting for transfers between devices, hop(): return lax.ppermute(value, AXES, pairs)  13.8 us
    all_to_all x1, blocking collectives, exchange(): return lax.all_to_all(value, axis, 0, 0, tiled=True)  13 us
    ppermute x3, starting transfers between devices, swap(): return lax.ppermute(value, axis, [(0, 1), (1, 0)])  8.9 us
    pallas_call x1, Pallas kernels, local(): call(main_kernel, 'window_steps', [((SENT, 128), BF16)] * 2, [((STEPS, WI...  7.96 us
    all_to_all x2, starting transfers between devices, exchange(): return lax.all_to_all(value, axis, 0, 0, tiled=True)  7.23 us
    all_to_all x2, waiting for transfers between devices, exchange(): return lax.all_to_all(value, axis, 0, 0, tiled=True)  5.55 us
    ppermute x3, waiting for transfers between devices, swap(): return lax.ppermute(value, axis, [(0, 1), (1, 0)])  2.26 us
  transfers between devices with their start and end apart: 14, of which 11 were waited for; matrix products, arithmetic and copies ran while one was open for 0% of the time, Pallas kernels for 1%

profile of v6, /device:TPU:1, one launch (start us, length us, event | category | flops | bytes accessed | tf_op | source)
XLA Modules:
  0.0 83.0 jit_solution(9137129191835126725)
XLA Ops:
  0.6 1.4 %pack_cells.1 = (bf16[2,2,36,512]{3,2,1,0:T(8,128)(2,1)S(1)}, bf16[2,2,36,512]{3,2,1,0:T(8,128)(2,1)S(1)}, bf16[2,18,512]{2,1,0:T(8,128)(2,1)S(1)}, f32[8,192]{1,0:T(8,128)S(1)}, bf16[192,576]{1,0:T(8,128)(2,1)S(1)}) custom-call(bf16[12,24,192]{2,1,0:T(8,128)(2,1)} %bitcast.23, bf16[12,24,192]{2,1,0:T(8,128)(2,1)} %bitcast.24, s32[12,24]{1,0:T(8,128)} %bitcast.25, ...), custom_call_target="tpu_custom_call" | custom-call | tf_op jit(solution)/shard_map/pack_cells/pallas_call | solution.py:395
  2.1 3.3 %collective-permute-start = (bf16[2,2,36,512]{3,2,1,0:T(8,128)(2,1)S(1)}, bf16[2,2,36,512]{3,2,1,0:T(8,128)(2,1)S(1)}, u32[]{:S(2)}, u32[]{:S(2)}) collective-permute-start(bf16[2,2,36,512]{3,2,1,0:T(8,128)(2,1)S(1)} %get-tuple-element.38), channel_id=1, source_target_pairs={{0,64},{64,0},{1,65},{65,1},{2,66},{66,2},{3,67},{67,3},{4,68},{68... | collective-permute-start | bytes 442376 | tf_op jit(solution)/shard_map/ppermute | solution.py:371
  5.4 1.3 %collective-permute-start.1 = (bf16[2,18,512]{2,1,0:T(8,128)(2,1)S(1)}, bf16[2,18,512]{2,1,0:T(8,128)(2,1)S(1)}, u32[]{:S(2)}, u32[]{:S(2)}) collective-permute-start(bf16[2,18,512]{2,1,0:T(8,128)(2,1)S(1)} %get-tuple-element.39), channel_id=1, source_target_pairs={{0,120},{1,121},{2,122},{3,123},{4,124},{5,125},{6,126},{7,127},{8... | collective-permute-start | bytes 110600 | tf_op jit(solution)/shard_map/ppermute | solution.py:367
  6.7 5.7 %collective-permute-start.2 = (bf16[2,18,512]{2,1,0:T(8,128)(2,1)S(1)}, bf16[2,18,512]{2,1,0:T(8,128)(2,1)S(1)}, u32[]{:S(2)}, u32[]{:S(2)}) collective-permute-start(bf16[2,18,512]{2,1,0:T(8,128)(2,1)S(1)} %get-tuple-element.39), channel_id=1, source_target_pairs={{64,120},{65,121},{66,122},{67,123},{68,124},{69,125},{70,126},{71... | collective-permute-start | bytes 110600 | tf_op jit(solution)/shard_map/ppermute | solution.py:367
  12.5 1.1 %collective-permute-done.2.edge1 = bf16[2,18,512]{2,1,0:T(8,128)(2,1)S(1)} collective-permute-done((bf16[2,18,512]{2,1,0:T(8,128)(2,1)S(1)}, bf16[2,18,512]{2,1,0:T(8,128)(2,1)S(1)}, u32[]{:S(2)}, u32[]{:S(2)}) %collective-permute-start.2) | collective-permute-done | bytes 36896 | tf_op jit(solution)/shard_map/ppermute | solution.py:367
  13.7 2.8 %collective-permute-start.3 = (bf16[2,36,512]{2,1,0:T(8,128)(2,1)S(1)}, bf16[2,36,512]{2,1,0:T(8,128)(2,1)S(1)}, u32[]{:S(2)}, u32[]{:S(2)}) collective-permute-start(bf16[2,36,512]{2,1,0:T(8,128)(2,1)S(1)} %get-tuple-element.41), channel_id=1, source_target_pairs={{0,128},{1,129},{2,130},{3,131},{4,132},{5,133},{6,134},{7,135},{8... | collective-permute-start | bytes 221192 | tf_op jit(solution)/shard_map/ppermute | solution.py:367
  16.6 2.8 %collective-permute-start.4 = (bf16[2,36,512]{2,1,0:T(8,128)(2,1)S(1)}, bf16[2,36,512]{2,1,0:T(8,128)(2,1)S(1)}, u32[]{:S(2)}, u32[]{:S(2)}) collective-permute-start(bf16[2,36,512]{2,1,0:T(8,128)(2,1)S(1)} %get-tuple-element.42), channel_id=1, source_target_pairs={{0,7},{1,0},{2,1},{3,2},{4,3},{5,4},{6,5},{7,6},{8,15},{9,8},{10,9... | collective-permute-start | bytes 221192 | tf_op jit(solution)/shard_map/ppermute | solution.py:367
  21.3 4.3 %collective-permute-done.5.lon_x = bf16[2,36,512]{2,1,0:T(8,128)(2,1)S(1)} collective-permute-done((bf16[2,36,512]{2,1,0:T(8,128)(2,1)S(1)}, bf16[2,36,512]{2,1,0:T(8,128)(2,1)S(1)}, u32[]{:S(2)}, u32[]{:S(2)}) %collective-permute-start.5) | collective-permute-done | bytes 73760 | tf_op jit(solution)/shard_map/ppermute | solution.py:367
  25.6 8.0 %window_steps.1 = (bf16[2176,128]{1,0:T(8,128)(2,1)S(1)}, bf16[2176,128]{1,0:T(8,128)(2,1)S(1)}) custom-call(bf16[2,36,512]{2,1,0:T(8,128)(2,1)S(1)} %get-tuple-element.40.near_own, bf16[2,36,512]{2,1,0:T(8,128)(2,1)S(1)} %collective-permute-done.3.near_x, bf16[2,36,512]{2,1,0:T(8,128)(2,1)S(1)} %collective-permute-done.4.lon_own, ...), custom_call_target="tpu_custom_call" | custom-call | tf_op jit(solution)/shard_map/window_steps/pallas_call | solution.py:431
  33.6 1.1 %collective-permute-start.6 = (bf16[2176,128]{1,0:T(8,128)(2,1)S(1)}, bf16[2176,128]{1,0:T(8,128)(2,1)S(1)}, u32[]{:S(2)}, u32[]{:S(2)}) collective-permute-start(bf16[2176,128]{1,0:T(8,128)(2,1)S(1)} %get-tuple-element.47), channel_id=1, source_target_pairs={{0,64},{64,0},{1,65},{65,1},{2,66},{66,2},{3,67},{67,3},{4,68},{68... | collective-permute-start | bytes 1671176 | tf_op jit(solution)/shard_map/ppermute | solution.py:371
  34.7 1.6 %collective-permute-done.6.arrived = bf16[2176,128]{1,0:T(8,128)(2,1)S(1)} collective-permute-done((bf16[2176,128]{1,0:T(8,128)(2,1)S(1)}, bf16[2176,128]{1,0:T(8,128)(2,1)S(1)}, u32[]{:S(2)}, u32[]{:S(2)}) %collective-permute-start.6) | collective-permute-done | bytes 557088 | tf_op jit(solution)/shard_map/ppermute | solution.py:371
  36.4 13.0 %all_to_all.15.terms = bf16[16,112,128]{2,1,0:T(8,128)(2,1)S(1)} all-to-all(bf16[16,112,128]{2,1,0:T(8,128)(2,1)S(1)} %get-tuple-element.48), channel_id=1, replica_groups=mesh['xh'=2,'core'=2,'lat'=8,'lon'=8] {'xh','lon'}, dimensions={0} | all-to-all | bytes 917504 | tf_op jit(solution)/shard_map/all_to_all | solution.py:375
  50.2 3.4 %all-to-all-start.1 = ((bf16[8,112,128]{2,1,0:T(8,128)(2,1)}), bf16[8,112,128]{2,1,0:T(8,128)(2,1)S(1)}, u32[]{:S(2)}, u32[]{:S(2)}) async-start(bf16[8,112,128]{2,1,0:T(8,128)(2,1)} %sum_group.1), calls=%async_computation.1 | async-start | bytes 458752 | tf_op jit(solution)/shard_map/all_to_all | solution.py:375
  54.8 2.1 %collective-permute-start.9 = (bf16[2,96,128]{2,1,0:T(8,128)(2,1)S(1)}, bf16[2,96,128]{2,1,0:T(8,128)(2,1)S(1)}, u32[]{:S(2)}, u32[]{:S(2)}) collective-permute-start(bf16[2,96,128]{2,1,0:T(8,128)(2,1)S(1)} %get-tuple-element.52), channel_id=1, source_target_pairs={{0,129},{1,130},{2,131},{3,132},{4,133},{5,134},{6,135},{7,128},{8... | collective-permute-start | bytes 147464 | tf_op jit(solution)/shard_map/ppermute | solution.py:367
  57.0 1.1 %collective-permute-done.7.near_x = bf16[2,96,128]{2,1,0:T(8,128)(2,1)S(1)} collective-permute-done((bf16[2,96,128]{2,1,0:T(8,128)(2,1)S(1)}, bf16[2,96,128]{2,1,0:T(8,128)(2,1)S(1)}, u32[]{:S(2)}, u32[]{:S(2)}) %collective-permute-start.7) | collective-permute-done | bytes 49184 | tf_op jit(solution)/shard_map/ppermute | solution.py:367
  58.1 1.6 %collective-permute-done.8.lon_own = bf16[2,96,128]{2,1,0:T(8,128)(2,1)S(1)} collective-permute-done((bf16[2,96,128]{2,1,0:T(8,128)(2,1)S(1)}, bf16[2,96,128]{2,1,0:T(8,128)(2,1)S(1)}, u32[]{:S(2)}, u32[]{:S(2)}) %collective-permute-start.8) | collective-permute-done | bytes 49184 | tf_op jit(solution)/shard_map/ppermute | solution.py:367
  59.7 1.7 %collective-permute-done.9.lon_x = bf16[2,96,128]{2,1,0:T(8,128)(2,1)S(1)} collective-permute-done((bf16[2,96,128]{2,1,0:T(8,128)(2,1)S(1)}, bf16[2,96,128]{2,1,0:T(8,128)(2,1)S(1)}, u32[]{:S(2)}, u32[]{:S(2)}) %collective-permute-start.9) | collective-permute-done | bytes 49184 | tf_op jit(solution)/shard_map/ppermute | solution.py:367
  61.3 1.1 %all-to-all-done.1.terms = bf16[8,112,128]{2,1,0:T(8,128)(2,1)S(1)} async-done(((bf16[8,112,128]{2,1,0:T(8,128)(2,1)}), bf16[8,112,128]{2,1,0:T(8,128)(2,1)S(1)}, u32[]{:S(2)}, u32[]{:S(2)}) %all-to-all-start.1) | async-done | bytes 229408 | tf_op jit(solution)/shard_map/all_to_all | solution.py:375
  63.2 3.8 %all-to-all-start.2 = ((bf16[16,112,128]{2,1,0:T(8,128)(2,1)}), bf16[16,112,128]{2,1,0:T(8,128)(2,1)S(1)}, u32[]{:S(2)}, u32[]{:S(2)}) async-start(bf16[16,112,128]{2,1,0:T(8,128)(2,1)} %get-tuple-element.55), calls=%async_computation.2 | async-start | bytes 917504 | tf_op jit(solution)/shard_map/all_to_all | solution.py:375
  67.1 1.2 %collective-permute-start.10 = (bf16[2,96,128]{2,1,0:T(8,128)(2,1)S(1)}, bf16[2,96,128]{2,1,0:T(8,128)(2,1)S(1)}, u32[]{:S(2)}, u32[]{:S(2)}) collective-permute-start(bf16[2,96,128]{2,1,0:T(8,128)(2,1)S(1)} %get-tuple-element.56), channel_id=1, source_target_pairs={{0,8},{1,9},{2,10},{3,11},{4,12},{5,13},{6,14},{7,15},{8,16},{9,17... | collective-permute-start | bytes 147464 | tf_op jit(solution)/shard_map/ppermute | solution.py:367
  68.2 3.1 %collective-permute-done.10.edges = bf16[2,96,128]{2,1,0:T(8,128)(2,1)S(1)} collective-permute-done((bf16[2,96,128]{2,1,0:T(8,128)(2,1)S(1)}, bf16[2,96,128]{2,1,0:T(8,128)(2,1)S(1)}, u32[]{:S(2)}, u32[]{:S(2)}) %collective-permute-start.10) | collective-permute-done | bytes 49184 | tf_op jit(solution)/shard_map/ppermute | solution.py:367
  71.3 4.5 %all-to-all-done.2 = bf16[16,112,128]{2,1,0:T(8,128)(2,1)S(1)} async-done(((bf16[16,112,128]{2,1,0:T(8,128)(2,1)}), bf16[16,112,128]{2,1,0:T(8,128)(2,1)S(1)}, u32[]{:S(2)}, u32[]{:S(2)}) %all-to-all-start.2) | async-done | bytes 458784 | tf_op jit(solution)/shard_map/all_to_all | solution.py:375
  75.8 4.5 %collective-permute-start.11 = (bf16[1792,128]{1,0:T(8,128)(2,1)S(1)}, bf16[1792,128]{1,0:T(8,128)(2,1)S(1)}, u32[]{:S(2)}, u32[]{:S(2)}) collective-permute-start(bf16[1792,128]{1,0:T(8,128)(2,1)S(1)} %bitcast.19), channel_id=1, source_target_pairs={{0,64},{64,0},{1,65},{65,1},{2,66},{66,2},{3,67},{67,3},{4,68},{68... | collective-permute-start | bytes 1376264 | tf_op jit(solution)/shard_map/ppermute | solution.py:371
  81.7 1.3 %unpack_sums.1 = (f32[192,576]{1,0:T(8,128)}, f32[192,192]{1,0:T(8,128)}, f32[192,768]{1,0:T(8,128)}, f32[192,768]{1,0:T(8,128)}, f32[1,192]{1,0:T(1,128)}, /*index=5*/f32[1,192]{1,0:T(1,128)}, f32[1,192]{1,0:T(1,128)}) custom-call(bf16[1792,128]{1,0:T(8,128)(2,1)S(1)} %bitcast.20, bf16[1792,128]{1,0:T(8,128)(2,1)S(1)} %collective-permute-done.11.other), custom_call_target="tpu_custom_call" | custom-call | tf_op jit(solution)/shard_map/unpack_sums/pallas_call | solution.py:486
  (19 shorter events, 6.5 us)
Async XLA Ops:
  0.6 25.0 %copy-start.1 = (bf16[768,192]{0,1:T(8,128)(2,1)S(1)}, bf16[768,192]{0,1:T(8,128)(2,1)}, u32[]{:S(2)}) copy-start(bf16[768,192]{0,1:T(8,128)(2,1)} %param.19) | copy-start | bytes 884740
  2.1 23.5 %copy-start = (bf16[192,768]{1,0:T(8,128)(2,1)S(1)}, bf16[192,768]{1,0:T(8,128)(2,1)}, u32[]{:S(2)}) copy-start(bf16[192,768]{1,0:T(8,128)(2,1)} %wup.1) | copy-start | bytes 884740
  2.1 11.5 %collective-permute-start = (bf16[2,2,36,512]{3,2,1,0:T(8,128)(2,1)S(1)}, bf16[2,2,36,512]{3,2,1,0:T(8,128)(2,1)S(1)}, u32[]{:S(2)}, u32[]{:S(2)}) collective-permute-start(bf16[2,2,36,512]{3,2,1,0:T(8,128)(2,1)S(1)} %get-tuple-element.38), channel_id=1, source_target_pairs={{0,64},{64,0},{1,65},{65,1},{2,66},{66,2},{3,67},{67,3},{4,68},{68... | collective-permute-start | bytes 442376 | tf_op jit(solution)/shard_map/ppermute | solution.py:371
  5.4 7.0 %collective-permute-start.1 = (bf16[2,18,512]{2,1,0:T(8,128)(2,1)S(1)}, bf16[2,18,512]{2,1,0:T(8,128)(2,1)S(1)}, u32[]{:S(2)}, u32[]{:S(2)}) collective-permute-start(bf16[2,18,512]{2,1,0:T(8,128)(2,1)S(1)} %get-tuple-element.39), channel_id=1, source_target_pairs={{0,120},{1,121},{2,122},{3,123},{4,124},{5,125},{6,126},{7,127},{8... | collective-permute-start | bytes 110600 | tf_op jit(solution)/shard_map/ppermute | solution.py:367
  6.7 6.9 %collective-permute-start.2 = (bf16[2,18,512]{2,1,0:T(8,128)(2,1)S(1)}, bf16[2,18,512]{2,1,0:T(8,128)(2,1)S(1)}, u32[]{:S(2)}, u32[]{:S(2)}) collective-permute-start(bf16[2,18,512]{2,1,0:T(8,128)(2,1)S(1)} %get-tuple-element.39), channel_id=1, source_target_pairs={{64,120},{65,121},{66,122},{67,123},{68,124},{69,125},{70,126},{71... | collective-permute-start | bytes 110600 | tf_op jit(solution)/shard_map/ppermute | solution.py:367
  13.6 12.0 %copy-start.2 = (bf16[192,192]{1,0:T(8,128)(2,1)S(1)}, bf16[192,192]{1,0:T(8,128)(2,1)}, u32[]{:S(2)}) copy-start(bf16[192,192]{1,0:T(8,128)(2,1)} %wout.1) | copy-start | bytes 221188
  13.7 6.6 %collective-permute-start.3 = (bf16[2,36,512]{2,1,0:T(8,128)(2,1)S(1)}, bf16[2,36,512]{2,1,0:T(8,128)(2,1)S(1)}, u32[]{:S(2)}, u32[]{:S(2)}) collective-permute-start(bf16[2,36,512]{2,1,0:T(8,128)(2,1)S(1)} %get-tuple-element.41), channel_id=1, source_target_pairs={{0,128},{1,129},{2,130},{3,131},{4,132},{5,133},{6,134},{7,135},{8... | collective-permute-start | bytes 221192 | tf_op jit(solution)/shard_map/ppermute | solution.py:367
  16.6 4.7 %collective-permute-start.4 = (bf16[2,36,512]{2,1,0:T(8,128)(2,1)S(1)}, bf16[2,36,512]{2,1,0:T(8,128)(2,1)S(1)}, u32[]{:S(2)}, u32[]{:S(2)}) collective-permute-start(bf16[2,36,512]{2,1,0:T(8,128)(2,1)S(1)} %get-tuple-element.42), channel_id=1, source_target_pairs={{0,7},{1,0},{2,1},{3,2},{4,3},{5,4},{6,5},{7,6},{8,15},{9,8},{10,9... | collective-permute-start | bytes 221192 | tf_op jit(solution)/shard_map/ppermute | solution.py:367
  19.3 6.3 %collective-permute-start.5 = (bf16[2,36,512]{2,1,0:T(8,128)(2,1)S(1)}, bf16[2,36,512]{2,1,0:T(8,128)(2,1)S(1)}, u32[]{:S(2)}, u32[]{:S(2)}) collective-permute-start(bf16[2,36,512]{2,1,0:T(8,128)(2,1)S(1)} %get-tuple-element.43), channel_id=1, source_target_pairs={{0,135},{1,128},{2,129},{3,130},{4,131},{5,132},{6,133},{7,134},{8... | collective-permute-start | bytes 221192 | tf_op jit(solution)/shard_map/ppermute | solution.py:367
  33.6 2.7 %collective-permute-start.6 = (bf16[2176,128]{1,0:T(8,128)(2,1)S(1)}, bf16[2176,128]{1,0:T(8,128)(2,1)S(1)}, u32[]{:S(2)}, u32[]{:S(2)}) collective-permute-start(bf16[2176,128]{1,0:T(8,128)(2,1)S(1)} %get-tuple-element.47), channel_id=1, source_target_pairs={{0,64},{64,0},{1,65},{65,1},{2,66},{66,2},{3,67},{67,3},{4,68},{68... | collective-permute-start | bytes 1671176 | tf_op jit(solution)/shard_map/ppermute | solution.py:371
  50.2 12.2 %all-to-all-start.1 = ((bf16[8,112,128]{2,1,0:T(8,128)(2,1)}), bf16[8,112,128]{2,1,0:T(8,128)(2,1)S(1)}, u32[]{:S(2)}, u32[]{:S(2)}) async-start(bf16[8,112,128]{2,1,0:T(8,128)(2,1)} %sum_group.1), calls=%async_computation.1 | async-start | bytes 458752 | tf_op jit(solution)/shard_map/all_to_all | solution.py:375
  53.6 4.5 %collective-permute-start.7 = (bf16[2,96,128]{2,1,0:T(8,128)(2,1)S(1)}, bf16[2,96,128]{2,1,0:T(8,128)(2,1)S(1)}, u32[]{:S(2)}, u32[]{:S(2)}) collective-permute-start(bf16[2,96,128]{2,1,0:T(8,128)(2,1)S(1)} %get-tuple-element.50), channel_id=1, source_target_pairs={{0,128},{1,129},{2,130},{3,131},{4,132},{5,133},{6,134},{7,135},{8... | collective-permute-start | bytes 147464 | tf_op jit(solution)/shard_map/ppermute | solution.py:367
  54.6 5.0 %collective-permute-start.8 = (bf16[2,96,128]{2,1,0:T(8,128)(2,1)S(1)}, bf16[2,96,128]{2,1,0:T(8,128)(2,1)S(1)}, u32[]{:S(2)}, u32[]{:S(2)}) collective-permute-start(bf16[2,96,128]{2,1,0:T(8,128)(2,1)S(1)} %get-tuple-element.51), channel_id=1, source_target_pairs={{0,1},{1,2},{2,3},{3,4},{4,5},{5,6},{6,7},{7,0},{8,9},{9,10},{10,1... | collective-permute-start | bytes 147464 | tf_op jit(solution)/shard_map/ppermute | solution.py:367
  54.8 6.5 %collective-permute-start.9 = (bf16[2,96,128]{2,1,0:T(8,128)(2,1)S(1)}, bf16[2,96,128]{2,1,0:T(8,128)(2,1)S(1)}, u32[]{:S(2)}, u32[]{:S(2)}) collective-permute-start(bf16[2,96,128]{2,1,0:T(8,128)(2,1)S(1)} %get-tuple-element.52), channel_id=1, source_target_pairs={{0,129},{1,130},{2,131},{3,132},{4,133},{5,134},{6,135},{7,128},{8... | collective-permute-start | bytes 147464 | tf_op jit(solution)/shard_map/ppermute | solution.py:367
  63.2 12.5 %all-to-all-start.2 = ((bf16[16,112,128]{2,1,0:T(8,128)(2,1)}), bf16[16,112,128]{2,1,0:T(8,128)(2,1)S(1)}, u32[]{:S(2)}, u32[]{:S(2)}) async-start(bf16[16,112,128]{2,1,0:T(8,128)(2,1)} %get-tuple-element.55), calls=%async_computation.2 | async-start | bytes 917504 | tf_op jit(solution)/shard_map/all_to_all | solution.py:375
  67.1 4.2 %collective-permute-start.10 = (bf16[2,96,128]{2,1,0:T(8,128)(2,1)S(1)}, bf16[2,96,128]{2,1,0:T(8,128)(2,1)S(1)}, u32[]{:S(2)}, u32[]{:S(2)}) collective-permute-start(bf16[2,96,128]{2,1,0:T(8,128)(2,1)S(1)} %get-tuple-element.56), channel_id=1, source_target_pairs={{0,8},{1,9},{2,10},{3,11},{4,12},{5,13},{6,14},{7,15},{8,16},{9,17... | collective-permute-start | bytes 147464 | tf_op jit(solution)/shard_map/ppermute | solution.py:367
  75.8 5.9 %collective-permute-start.11 = (bf16[1792,128]{1,0:T(8,128)(2,1)S(1)}, bf16[1792,128]{1,0:T(8,128)(2,1)S(1)}, u32[]{:S(2)}, u32[]{:S(2)}) collective-permute-start(bf16[1792,128]{1,0:T(8,128)(2,1)S(1)} %bitcast.19), channel_id=1, source_target_pairs={{0,64},{64,0},{1,65},{65,1},{2,66},{66,2},{3,67},{67,3},{4,68},{68... | collective-permute-start | bytes 1376264 | tf_op jit(solution)/shard_map/ppermute | solution.py:371

commit v7 on v6

--- a/solution.py
+++ b/solution.py
@@ -17,7 +17,8 @@
 HALF = WIN // 2
 STEPS = 4
 TOK = STEPS * WIN
-MSG = 512
+MSG = 384
+TALL = 40
 GROUP = 16
 UNIT = 112
 SUMS = GROUP * UNIT
@@ -71,19 +72,32 @@
     for copy in copies:
         copy.wait()
     core = lax.axis_index("core")
-    mask = land[...].astype(F32)
     nothing = jnp.zeros((3, MSG), F32)
+    cells[:, :, :, HALF:TALL, :] = jnp.zeros((2, 2, 2, TALL - HALF, MSG), F32)
+    edges[:, HALF // 2 : 24, :] = jnp.zeros((2, 24 - HALF // 2, MSG), F32)
     for c in range(WIN_LON):
-        column = jnp.broadcast_to(mask[c : c + 1, :], (64, ROWS)).T
-        cell = jnp.concatenate(
-            [states[c].astype(F32), column, loss[c].astype(F32), column], axis=1
-        )
+        cell = jnp.concatenate([states[c].astype(F32), loss[c].astype(F32)], axis=1)
         part, at = (1, 6 * c) if c < 6 else (0, 6 * (c - 6))
         for k in range(3):
             cells[k % 2, k // 2, part, at : at + 6, :] = cell[6 * k + 3 : 6 * k + 9]
         cells[1, 1, part, at : at + 3, :] = cell[21:24]
         cells[1, 1, part, at + 3 : at + 6, :] = nothing
         edges[part, at // 2 : at // 2 + 3, :] = cell[0:3]
+    lanes = lax.broadcasted_iota(jnp.int32, (ROWS, 640), 1)
+    row = lax.broadcasted_iota(jnp.int32, (ROWS, 640), 0)
+    window = lanes // 128
+    inner = lax.rem(lax.rem(lanes, 128), WIN_LAT)
+    wanted = jnp.where(window == 4, inner - 3, 6 * window + 3 + inner)
+    picked = nn(land[...].astype(BF16), (row == wanted).astype(BF16))
+    token = lax.rem(lax.broadcasted_iota(jnp.int32, (6, 640), 1), 128)
+    column = lax.broadcasted_iota(jnp.int32, (6, 640), 0)
+    here = (token // WIN_LAT == column).astype(F32)
+    for part in range(2):
+        first = 6 - 6 * part
+        line = jnp.sum(picked[first : first + 6] * here, axis=0, keepdims=True)
+        for k in range(4):
+            cells[k % 2, k // 2, part, HALF : HALF + 1, 0:128] = line[:, 128 * k : 128 * k + 128]
+        edges[part, HALF // 2 : HALF // 2 + 1, 0:128] = line[:, 512:640]
     keep_out[...] = cells[core].astype(BF16)
     send_out[...] = cells[1 - core].astype(BF16)
     edge_out[...] = edges[...].astype(BF16)
@@ -104,6 +118,10 @@
                 rows = edge[part].astype(F32)
                 for c in range(6):
                     cells[step, 1, part, 6 * c + 3 : 6 * c + 6, :] = rows[3 * c : 3 * c + 3]
+                line = rows[HALF // 2 : HALF // 2 + 1]
+                cells[step, 1, part, HALF : HALF + 1, :] = (
+                    cells[step, 1, part, HALF : HALF + 1, :] + line
+                )
 
     for step in range(2):
         near_own[step] = cells[step, here, 0].astype(BF16)
@@ -115,7 +133,7 @@
 def main_kernel(
     near_own, near_x, lon_own, lon_x, vectors, wqkv, wout, wup, wdown_t,
     send_out, keep_out,
-    x, qkv, probs, qm_all, emb, xh1, r1, hid_xh, r2, gp, act, normed_s, mixed_s, nm_s,
+    x, land_s, qkv, probs, qm_all, emb, xh1, r1, hid_xh, r2, gp, act, normed_s, mixed_s, nm_s,
     cot_s, dpre_s, dproj_s, dqkv_s, dstate, small, msg,
 ):
     core = lax.axis_index("core")
@@ -123,10 +141,14 @@
     last = jnp.logical_and(lax.axis_index("lat") == 7, jnp.logical_and(here == 1, core == 1))
     closed = jnp.where(last, 0.0, 1.0).astype(F32)
     for step in range(2):
-        x[2 * here + step, 0:HALF, :] = near_own[step].astype(F32)
-        x[2 * here + step, HALF:WIN, :] = lon_own[step].astype(F32)
-        x[2 * (1 - here) + step, 0:HALF, :] = near_x[step].astype(F32)
-        x[2 * (1 - here) + step, HALF:WIN, :] = lon_x[step].astype(F32)
+        x[2 * here + step, 0:HALF, :] = near_own[step].astype(F32)[0:HALF]
+        x[2 * here + step, HALF:WIN, :] = lon_own[step].astype(F32)[0:HALF]
+        x[2 * (1 - here) + step, 0:HALF, :] = near_x[step].astype(F32)[0:HALF]
+        x[2 * (1 - here) + step, HALF:WIN, :] = lon_x[step].astype(F32)[0:HALF]
+    for part, cells in ((0, near_own), (1, lon_own)):
+        line = cells[0].astype(F32)[HALF : HALF + 1, 0:128]
+        column = jnp.broadcast_to(line, (8, 128)).T
+        land_s[HALF * part : HALF * part + HALF, :] = column[0:HALF, 0:1]
     le = vectors[0:1, :]
     ga = vectors[1:2, :]
     gm = vectors[2:3, :]
@@ -148,7 +170,7 @@
 
     for s in range(STEPS):
         rows = slice(WIN * s, WIN * s + WIN)
-        land = x[s, :, 192:256][:, 0:1]
+        land = land_s[...]
         e = x[s, :, 0:CH] + land * le
         emb[rows, :] = e
         off = e - mean_of(e)
@@ -197,7 +219,7 @@
     dstate[...] = jnp.zeros_like(dstate)
     for s in range(STEPS - 1, -1, -1):
         rows = slice(WIN * s, WIN * s + WIN)
-        cot = x[s, :, 256:448]
+        cot = x[s, :, CH:MSG]
         if incoming is not None:
             cot = cot + incoming
         cotb = cot.astype(BF16)
@@ -231,7 +253,7 @@
         gain_a_sum = gain_a_sum + jnp.sum(dy * xh, axis=0, keepdims=True)
         dxh = dy * ga
         d_state = d_hid + r1[rows, :] * (dxh - mean_of(dxh) - xh * mean_of(dxh * xh))
-        land = x[s, :, 192:256][:, 0:1]
+        land = land_s[...]
         land_sum = land_sum + jnp.sum(d_state * land, axis=0, keepdims=True)
         incoming = d_state.astype(BF16).astype(F32)
         dstate[:, 0:CH] = incoming
@@ -395,15 +417,15 @@
     keep, send, edge, vectors, w_qkv = call(
         pack_kernel,
         "pack_cells",
-        [((2, 2, HALF, MSG), BF16)] * 2 + [((2, HALF // 2, MSG), BF16), ((8, CH), F32)]
+        [((2, 2, TALL, MSG), BF16)] * 2 + [((2, 24, MSG), BF16), ((8, CH), F32)]
         + [((CH, 3 * CH), BF16)],
         [
             ((WIN_LON, ROWS, CH), BF16),
             ((WIN_LON, ROWS, CH), BF16),
             ((WIN_LON, ROWS), jnp.int32),
             ((8, CH), F32),
-            ((2, 2, 2, HALF, MSG), F32),
-            ((2, HALF // 2, MSG), F32),
+            ((2, 2, 2, TALL, MSG), F32),
+            ((2, 24, MSG), F32),
             (pltpu.SemaphoreType.DMA((7,)), None),
         ],
         from_hbm=7,
@@ -419,8 +441,8 @@
     near_own, near_x, lon_own, lon_x = call(
         sort_kernel,
         "sort_windows",
-        [((2, HALF, MSG), BF16)] * 4,
-        [((2, 2, 2, HALF, MSG), F32)],
+        [((2, TALL, MSG), BF16)] * 4,
+        [((2, 2, 2, TALL, MSG), F32)],
     )(
         keep, swap(send, "core"),
         hop(edge, -1, 0, cores=((0, 1),)), hop(edge, -1, 0, cores=((1, 1),)),
@@ -434,6 +456,7 @@
         [((SENT, 128), BF16)] * 2,
         [
             ((STEPS, WIN, MSG), F32),
+            ((WIN, 1), F32),
             ((TOK, 3 * CH), F32),
             ((STEPS, WIN, HEADS * WIN), F32),
             ((STEPS, HEADS * WIN, CH), BF16),

time: 83.4 us -> 84 us (level)
  Pallas kernels: 13.3 us -> 14.4 us
    pallas_call x1, Pallas kernels: 7.96 us -> 9.19 us  [local(): call(main_kernel, 'window_steps', [((SENT, 128), BF16)] * 2, [((STEPS, WI...]
where the time goes in v7:
time: 84 us; the launch traced here: 83.6 us
  starting transfers between devices  34.5 us (41%)
  waiting for transfers between devices  21 us (25%)
  Pallas kernels  14.4 us (17%)
  blocking collectives  13 us (15%)
    ppermute x9, starting transfers between devices, hop(): return lax.ppermute(value, AXES, pairs)  18.1 us
    ppermute x9, waiting for transfers between devices, hop(): return lax.ppermute(value, AXES, pairs)  13.1 us
    all_to_all x1, blocking collectives, exchange(): return lax.all_to_all(value, axis, 0, 0, tiled=True)  13 us
    pallas_call x1, Pallas kernels, local(): call(main_kernel, 'window_steps', [((SENT, 128), BF16)] * 2, [((STEPS, WI...  9.19 us
    ppermute x3, starting transfers between devices, swap(): return lax.ppermute(value, axis, [(0, 1), (1, 0)])  9.16 us
    all_to_all x2, starting transfers between devices, exchange(): return lax.all_to_all(value, axis, 0, 0, tiled=True)  7.27 us
    all_to_all x2, waiting for transfers between devices, exchange(): return lax.all_to_all(value, axis, 0, 0, tiled=True)  5.65 us
    ppermute x3, waiting for transfers between devices, swap(): return lax.ppermute(value, axis, [(0, 1), (1, 0)])  2.26 us
  transfers between devices with their start and end apart: 14, of which 11 were waited for; matrix products, arithmetic and copies ran while one was open for 0% of the time, Pallas kernels for 1%

profile of v7, /device:TPU:1, one launch (start us, length us, event | category | flops | bytes accessed | tf_op | source)
XLA Modules:
  0.0 83.6 jit_solution(12634370119870865874)
XLA Ops:
  0.7 1.3 %pack_cells.1 = (bf16[2,2,40,384]{3,2,1,0:T(8,128)(2,1)S(1)}, bf16[2,2,40,384]{3,2,1,0:T(8,128)(2,1)S(1)}, bf16[2,24,384]{2,1,0:T(8,128)(2,1)S(1)}, f32[8,192]{1,0:T(8,128)S(1)}, bf16[192,576]{1,0:T(8,128)(2,1)S(1)}) custom-call(bf16[12,24,192]{2,1,0:T(8,128)(2,1)} %bitcast.23, bf16[12,24,192]{2,1,0:T(8,128)(2,1)} %bitcast.24, s32[12,24]{1,0:T(8,128)} %bitcast.25, ...), custom_call_target="tpu_custom_call" | custom-call | tf_op jit(solution)/shard_map/pack_cells/pallas_call | solution.py:417
  2.0 3.3 %collective-permute-start = (bf16[2,2,40,384]{3,2,1,0:T(8,128)(2,1)S(1)}, bf16[2,2,40,384]{3,2,1,0:T(8,128)(2,1)S(1)}, u32[]{:S(2)}, u32[]{:S(2)}) collective-permute-start(bf16[2,2,40,384]{3,2,1,0:T(8,128)(2,1)S(1)} %get-tuple-element.38), channel_id=1, source_target_pairs={{0,64},{64,0},{1,65},{65,1},{2,66},{66,2},{3,67},{67,3},{4,68},{68... | collective-permute-start | bytes 368648 | tf_op jit(solution)/shard_map/ppermute | solution.py:393
  5.3 1.3 %collective-permute-start.1 = (bf16[2,24,384]{2,1,0:T(8,128)(2,1)S(1)}, bf16[2,24,384]{2,1,0:T(8,128)(2,1)S(1)}, u32[]{:S(2)}, u32[]{:S(2)}) collective-permute-start(bf16[2,24,384]{2,1,0:T(8,128)(2,1)S(1)} %get-tuple-element.39), channel_id=1, source_target_pairs={{0,120},{1,121},{2,122},{3,123},{4,124},{5,125},{6,126},{7,127},{8... | collective-permute-start | bytes 110600 | tf_op jit(solution)/shard_map/ppermute | solution.py:389
  6.6 5.7 %collective-permute-start.2 = (bf16[2,24,384]{2,1,0:T(8,128)(2,1)S(1)}, bf16[2,24,384]{2,1,0:T(8,128)(2,1)S(1)}, u32[]{:S(2)}, u32[]{:S(2)}) collective-permute-start(bf16[2,24,384]{2,1,0:T(8,128)(2,1)S(1)} %get-tuple-element.39), channel_id=1, source_target_pairs={{64,120},{65,121},{66,122},{67,123},{68,124},{69,125},{70,126},{71... | collective-permute-start | bytes 110600 | tf_op jit(solution)/shard_map/ppermute | solution.py:389
  12.4 1.0 %collective-permute-done.2.edge1 = bf16[2,24,384]{2,1,0:T(8,128)(2,1)S(1)} collective-permute-done((bf16[2,24,384]{2,1,0:T(8,128)(2,1)S(1)}, bf16[2,24,384]{2,1,0:T(8,128)(2,1)S(1)}, u32[]{:S(2)}, u32[]{:S(2)}) %collective-permute-start.2) | collective-permute-done | bytes 36896 | tf_op jit(solution)/shard_map/ppermute | solution.py:389
  13.5 2.8 %collective-permute-start.3 = (bf16[2,40,384]{2,1,0:T(8,128)(2,1)S(1)}, bf16[2,40,384]{2,1,0:T(8,128)(2,1)S(1)}, u32[]{:S(2)}, u32[]{:S(2)}) collective-permute-start(bf16[2,40,384]{2,1,0:T(8,128)(2,1)S(1)} %get-tuple-element.41), channel_id=1, source_target_pairs={{0,128},{1,129},{2,130},{3,131},{4,132},{5,133},{6,134},{7,135},{8... | collective-permute-start | bytes 184328 | tf_op jit(solution)/shard_map/ppermute | solution.py:389
  16.4 2.8 %collective-permute-start.4 = (bf16[2,40,384]{2,1,0:T(8,128)(2,1)S(1)}, bf16[2,40,384]{2,1,0:T(8,128)(2,1)S(1)}, u32[]{:S(2)}, u32[]{:S(2)}) collective-permute-start(bf16[2,40,384]{2,1,0:T(8,128)(2,1)S(1)} %get-tuple-element.42), channel_id=1, source_target_pairs={{0,7},{1,0},{2,1},{3,2},{4,3},{5,4},{6,5},{7,6},{8,15},{9,8},{10,9... | collective-permute-start | bytes 184328 | tf_op jit(solution)/shard_map/ppermute | solution.py:389
  20.6 4.0 %collective-permute-done.5.lon_x = bf16[2,40,384]{2,1,0:T(8,128)(2,1)S(1)} collective-permute-done((bf16[2,40,384]{2,1,0:T(8,128)(2,1)S(1)}, bf16[2,40,384]{2,1,0:T(8,128)(2,1)S(1)}, u32[]{:S(2)}, u32[]{:S(2)}) %collective-permute-start.5) | collective-permute-done | bytes 61472 | tf_op jit(solution)/shard_map/ppermute | solution.py:389
  24.6 9.2 %window_steps.1 = (bf16[2176,128]{1,0:T(8,128)(2,1)S(1)}, bf16[2176,128]{1,0:T(8,128)(2,1)S(1)}) custom-call(bf16[2,40,384]{2,1,0:T(8,128)(2,1)S(1)} %get-tuple-element.40.near_own, bf16[2,40,384]{2,1,0:T(8,128)(2,1)S(1)} %collective-permute-done.3.near_x, bf16[2,40,384]{2,1,0:T(8,128)(2,1)S(1)} %collective-permute-done.4.lon_own, ...), custom_call_target="tpu_custom_call" | custom-call | tf_op jit(solution)/shard_map/window_steps/pallas_call | solution.py:453
  33.8 1.4 %collective-permute-start.6 = (bf16[2176,128]{1,0:T(8,128)(2,1)S(1)}, bf16[2176,128]{1,0:T(8,128)(2,1)S(1)}, u32[]{:S(2)}, u32[]{:S(2)}) collective-permute-start(bf16[2176,128]{1,0:T(8,128)(2,1)S(1)} %get-tuple-element.47), channel_id=1, source_target_pairs={{0,64},{64,0},{1,65},{65,1},{2,66},{66,2},{3,67},{67,3},{4,68},{68... | collective-permute-start | bytes 1671176 | tf_op jit(solution)/shard_map/ppermute | solution.py:393
  35.2 1.6 %collective-permute-done.6.arrived = bf16[2176,128]{1,0:T(8,128)(2,1)S(1)} collective-permute-done((bf16[2176,128]{1,0:T(8,128)(2,1)S(1)}, bf16[2176,128]{1,0:T(8,128)(2,1)S(1)}, u32[]{:S(2)}, u32[]{:S(2)}) %collective-permute-start.6) | collective-permute-done | bytes 557088 | tf_op jit(solution)/shard_map/ppermute | solution.py:393
  36.9 13.0 %all_to_all.15.terms = bf16[16,112,128]{2,1,0:T(8,128)(2,1)S(1)} all-to-all(bf16[16,112,128]{2,1,0:T(8,128)(2,1)S(1)} %get-tuple-element.48), channel_id=1, replica_groups=mesh['xh'=2,'core'=2,'lat'=8,'lon'=8] {'xh','lon'}, dimensions={0} | all-to-all | bytes 917504 | tf_op jit(solution)/shard_map/all_to_all | solution.py:397
  50.7 3.4 %all-to-all-start.1 = ((bf16[8,112,128]{2,1,0:T(8,128)(2,1)}), bf16[8,112,128]{2,1,0:T(8,128)(2,1)S(1)}, u32[]{:S(2)}, u32[]{:S(2)}) async-start(bf16[8,112,128]{2,1,0:T(8,128)(2,1)} %sum_group.1), calls=%async_computation.1 | async-start | bytes 458752 | tf_op jit(solution)/shard_map/all_to_all | solution.py:397
  54.1 1.1 %collective-permute-start.7 = (bf16[2,96,128]{2,1,0:T(8,128)(2,1)S(1)}, bf16[2,96,128]{2,1,0:T(8,128)(2,1)S(1)}, u32[]{:S(2)}, u32[]{:S(2)}) collective-permute-start(bf16[2,96,128]{2,1,0:T(8,128)(2,1)S(1)} %get-tuple-element.50), channel_id=1, source_target_pairs={{0,128},{1,129},{2,130},{3,131},{4,132},{5,133},{6,134},{7,135},{8... | collective-permute-start | bytes 147464 | tf_op jit(solution)/shard_map/ppermute | solution.py:389
  55.4 2.2 %collective-permute-start.9 = (bf16[2,96,128]{2,1,0:T(8,128)(2,1)S(1)}, bf16[2,96,128]{2,1,0:T(8,128)(2,1)S(1)}, u32[]{:S(2)}, u32[]{:S(2)}) collective-permute-start(bf16[2,96,128]{2,1,0:T(8,128)(2,1)S(1)} %get-tuple-element.52), channel_id=1, source_target_pairs={{0,129},{1,130},{2,131},{3,132},{4,133},{5,134},{6,135},{7,128},{8... | collective-permute-start | bytes 147464 | tf_op jit(solution)/shard_map/ppermute | solution.py:389
  57.5 1.1 %collective-permute-done.7.near_x = bf16[2,96,128]{2,1,0:T(8,128)(2,1)S(1)} collective-permute-done((bf16[2,96,128]{2,1,0:T(8,128)(2,1)S(1)}, bf16[2,96,128]{2,1,0:T(8,128)(2,1)S(1)}, u32[]{:S(2)}, u32[]{:S(2)}) %collective-permute-start.7) | collective-permute-done | bytes 49184 | tf_op jit(solution)/shard_map/ppermute | solution.py:389
  58.6 1.6 %collective-permute-done.8.lon_own = bf16[2,96,128]{2,1,0:T(8,128)(2,1)S(1)} collective-permute-done((bf16[2,96,128]{2,1,0:T(8,128)(2,1)S(1)}, bf16[2,96,128]{2,1,0:T(8,128)(2,1)S(1)}, u32[]{:S(2)}, u32[]{:S(2)}) %collective-permute-start.8) | collective-permute-done | bytes 49184 | tf_op jit(solution)/shard_map/ppermute | solution.py:389
  60.2 1.7 %collective-permute-done.9.lon_x = bf16[2,96,128]{2,1,0:T(8,128)(2,1)S(1)} collective-permute-done((bf16[2,96,128]{2,1,0:T(8,128)(2,1)S(1)}, bf16[2,96,128]{2,1,0:T(8,128)(2,1)S(1)}, u32[]{:S(2)}, u32[]{:S(2)}) %collective-permute-start.9) | collective-permute-done | bytes 49184 | tf_op jit(solution)/shard_map/ppermute | solution.py:389
  61.9 1.2 %all-to-all-done.1.terms = bf16[8,112,128]{2,1,0:T(8,128)(2,1)S(1)} async-done(((bf16[8,112,128]{2,1,0:T(8,128)(2,1)}), bf16[8,112,128]{2,1,0:T(8,128)(2,1)S(1)}, u32[]{:S(2)}, u32[]{:S(2)}) %all-to-all-start.1) | async-done | bytes 229408 | tf_op jit(solution)/shard_map/all_to_all | solution.py:397
  63.9 3.9 %all-to-all-start.2 = ((bf16[16,112,128]{2,1,0:T(8,128)(2,1)}), bf16[16,112,128]{2,1,0:T(8,128)(2,1)S(1)}, u32[]{:S(2)}, u32[]{:S(2)}) async-start(bf16[16,112,128]{2,1,0:T(8,128)(2,1)} %get-tuple-element.55), calls=%async_computation.2 | async-start | bytes 917504 | tf_op jit(solution)/shard_map/all_to_all | solution.py:397
  68.8 3.2 %collective-permute-done.10.edges = bf16[2,96,128]{2,1,0:T(8,128)(2,1)S(1)} collective-permute-done((bf16[2,96,128]{2,1,0:T(8,128)(2,1)S(1)}, bf16[2,96,128]{2,1,0:T(8,128)(2,1)S(1)}, u32[]{:S(2)}, u32[]{:S(2)}) %collective-permute-start.10) | collective-permute-done | bytes 49184 | tf_op jit(solution)/shard_map/ppermute | solution.py:389
  72.0 4.5 %all-to-all-done.2 = bf16[16,112,128]{2,1,0:T(8,128)(2,1)S(1)} async-done(((bf16[16,112,128]{2,1,0:T(8,128)(2,1)}), bf16[16,112,128]{2,1,0:T(8,128)(2,1)S(1)}, u32[]{:S(2)}, u32[]{:S(2)}) %all-to-all-start.2) | async-done | bytes 458784 | tf_op jit(solution)/shard_map/all_to_all | solution.py:397
  76.5 4.4 %collective-permute-start.11 = (bf16[1792,128]{1,0:T(8,128)(2,1)S(1)}, bf16[1792,128]{1,0:T(8,128)(2,1)S(1)}, u32[]{:S(2)}, u32[]{:S(2)}) collective-permute-start(bf16[1792,128]{1,0:T(8,128)(2,1)S(1)} %bitcast.19), channel_id=1, source_target_pairs={{0,64},{64,0},{1,65},{65,1},{2,66},{66,2},{3,67},{67,3},{4,68},{68... | collective-permute-start | bytes 1376264 | tf_op jit(solution)/shard_map/ppermute | solution.py:393
  82.3 1.3 %unpack_sums.1 = (f32[192,576]{1,0:T(8,128)}, f32[192,192]{1,0:T(8,128)}, f32[192,768]{1,0:T(8,128)}, f32[192,768]{1,0:T(8,128)}, f32[1,192]{1,0:T(1,128)}, /*index=5*/f32[1,192]{1,0:T(1,128)}, f32[1,192]{1,0:T(1,128)}) custom-call(bf16[1792,128]{1,0:T(8,128)(2,1)S(1)} %bitcast.20, bf16[1792,128]{1,0:T(8,128)(2,1)S(1)} %collective-permute-done.11.other), custom_call_target="tpu_custom_call" | custom-call | tf_op jit(solution)/shard_map/unpack_sums/pallas_call | solution.py:509
  (19 shorter events, 6.0 us)
Async XLA Ops:
  0.6 24.0 %copy-start.1 = (bf16[768,192]{0,1:T(8,128)(2,1)S(1)}, bf16[768,192]{0,1:T(8,128)(2,1)}, u32[]{:S(2)}) copy-start(bf16[768,192]{0,1:T(8,128)(2,1)} %param.19) | copy-start | bytes 884740
  0.6 24.0 %copy-start.2 = (bf16[192,192]{1,0:T(8,128)(2,1)S(1)}, bf16[192,192]{1,0:T(8,128)(2,1)}, u32[]{:S(2)}) copy-start(bf16[192,192]{1,0:T(8,128)(2,1)} %wout.1) | copy-start | bytes 221188
  2.0 22.6 %copy-start = (bf16[192,768]{1,0:T(8,128)(2,1)S(1)}, bf16[192,768]{1,0:T(8,128)(2,1)}, u32[]{:S(2)}) copy-start(bf16[192,768]{1,0:T(8,128)(2,1)} %wup.1) | copy-start | bytes 884740
  2.0 11.4 %collective-permute-start = (bf16[2,2,40,384]{3,2,1,0:T(8,128)(2,1)S(1)}, bf16[2,2,40,384]{3,2,1,0:T(8,128)(2,1)S(1)}, u32[]{:S(2)}, u32[]{:S(2)}) collective-permute-start(bf16[2,2,40,384]{3,2,1,0:T(8,128)(2,1)S(1)} %get-tuple-element.38), channel_id=1, source_target_pairs={{0,64},{64,0},{1,65},{65,1},{2,66},{66,2},{3,67},{67,3},{4,68},{68... | collective-permute-start | bytes 368648 | tf_op jit(solution)/shard_map/ppermute | solution.py:393
  5.3 7.0 %collective-permute-start.1 = (bf16[2,24,384]{2,1,0:T(8,128)(2,1)S(1)}, bf16[2,24,384]{2,1,0:T(8,128)(2,1)S(1)}, u32[]{:S(2)}, u32[]{:S(2)}) collective-permute-start(bf16[2,24,384]{2,1,0:T(8,128)(2,1)S(1)} %get-tuple-element.39), channel_id=1, source_target_pairs={{0,120},{1,121},{2,122},{3,123},{4,124},{5,125},{6,126},{7,127},{8... | collective-permute-start | bytes 110600 | tf_op jit(solution)/shard_map/ppermute | solution.py:389
  6.6 6.8 %collective-permute-start.2 = (bf16[2,24,384]{2,1,0:T(8,128)(2,1)S(1)}, bf16[2,24,384]{2,1,0:T(8,128)(2,1)S(1)}, u32[]{:S(2)}, u32[]{:S(2)}) collective-permute-start(bf16[2,24,384]{2,1,0:T(8,128)(2,1)S(1)} %get-tuple-element.39), channel_id=1, source_target_pairs={{64,120},{65,121},{66,122},{67,123},{68,124},{69,125},{70,126},{71... | collective-permute-start | bytes 110600 | tf_op jit(solution)/shard_map/ppermute | solution.py:389
  13.5 6.6 %collective-permute-start.3 = (bf16[2,40,384]{2,1,0:T(8,128)(2,1)S(1)}, bf16[2,40,384]{2,1,0:T(8,128)(2,1)S(1)}, u32[]{:S(2)}, u32[]{:S(2)}) collective-permute-start(bf16[2,40,384]{2,1,0:T(8,128)(2,1)S(1)} %get-tuple-element.41), channel_id=1, source_target_pairs={{0,128},{1,129},{2,130},{3,131},{4,132},{5,133},{6,134},{7,135},{8... | collective-permute-start | bytes 184328 | tf_op jit(solution)/shard_map/ppermute | solution.py:389
  16.4 4.3 %collective-permute-start.4 = (bf16[2,40,384]{2,1,0:T(8,128)(2,1)S(1)}, bf16[2,40,384]{2,1,0:T(8,128)(2,1)S(1)}, u32[]{:S(2)}, u32[]{:S(2)}) collective-permute-start(bf16[2,40,384]{2,1,0:T(8,128)(2,1)S(1)} %get-tuple-element.42), channel_id=1, source_target_pairs={{0,7},{1,0},{2,1},{3,2},{4,3},{5,4},{6,5},{7,6},{8,15},{9,8},{10,9... | collective-permute-start | bytes 184328 | tf_op jit(solution)/shard_map/ppermute | solution.py:389
  19.1 5.5 %collective-permute-start.5 = (bf16[2,40,384]{2,1,0:T(8,128)(2,1)S(1)}, bf16[2,40,384]{2,1,0:T(8,128)(2,1)S(1)}, u32[]{:S(2)}, u32[]{:S(2)}) collective-permute-start(bf16[2,40,384]{2,1,0:T(8,128)(2,1)S(1)} %get-tuple-element.43), channel_id=1, source_target_pairs={{0,135},{1,128},{2,129},{3,130},{4,131},{5,132},{6,133},{7,134},{8... | collective-permute-start | bytes 184328 | tf_op jit(solution)/shard_map/ppermute | solution.py:389
  33.8 3.0 %collective-permute-start.6 = (bf16[2176,128]{1,0:T(8,128)(2,1)S(1)}, bf16[2176,128]{1,0:T(8,128)(2,1)S(1)}, u32[]{:S(2)}, u32[]{:S(2)}) collective-permute-start(bf16[2176,128]{1,0:T(8,128)(2,1)S(1)} %get-tuple-element.47), channel_id=1, source_target_pairs={{0,64},{64,0},{1,65},{65,1},{2,66},{66,2},{3,67},{67,3},{4,68},{68... | collective-permute-start | bytes 1671176 | tf_op jit(solution)/shard_map/ppermute | solution.py:393
  50.7 12.4 %all-to-all-start.1 = ((bf16[8,112,128]{2,1,0:T(8,128)(2,1)}), bf16[8,112,128]{2,1,0:T(8,128)(2,1)S(1)}, u32[]{:S(2)}, u32[]{:S(2)}) async-start(bf16[8,112,128]{2,1,0:T(8,128)(2,1)} %sum_group.1), calls=%async_computation.1 | async-start | bytes 458752 | tf_op jit(solution)/shard_map/all_to_all | solution.py:397
  54.1 4.5 %collective-permute-start.7 = (bf16[2,96,128]{2,1,0:T(8,128)(2,1)S(1)}, bf16[2,96,128]{2,1,0:T(8,128)(2,1)S(1)}, u32[]{:S(2)}, u32[]{:S(2)}) collective-permute-start(bf16[2,96,128]{2,1,0:T(8,128)(2,1)S(1)} %get-tuple-element.50), channel_id=1, source_target_pairs={{0,128},{1,129},{2,130},{3,131},{4,132},{5,133},{6,134},{7,135},{8... | collective-permute-start | bytes 147464 | tf_op jit(solution)/shard_map/ppermute | solution.py:389
  55.1 5.0 %collective-permute-start.8 = (bf16[2,96,128]{2,1,0:T(8,128)(2,1)S(1)}, bf16[2,96,128]{2,1,0:T(8,128)(2,1)S(1)}, u32[]{:S(2)}, u32[]{:S(2)}) collective-permute-start(bf16[2,96,128]{2,1,0:T(8,128)(2,1)S(1)} %get-tuple-element.51), channel_id=1, source_target_pairs={{0,1},{1,2},{2,3},{3,4},{4,5},{5,6},{6,7},{7,0},{8,9},{9,10},{10,1... | collective-permute-start | bytes 147464 | tf_op jit(solution)/shard_map/ppermute | solution.py:389
  55.4 6.5 %collective-permute-start.9 = (bf16[2,96,128]{2,1,0:T(8,128)(2,1)S(1)}, bf16[2,96,128]{2,1,0:T(8,128)(2,1)S(1)}, u32[]{:S(2)}, u32[]{:S(2)}) collective-permute-start(bf16[2,96,128]{2,1,0:T(8,128)(2,1)S(1)} %get-tuple-element.52), channel_id=1, source_target_pairs={{0,129},{1,130},{2,131},{3,132},{4,133},{5,134},{6,135},{7,128},{8... | collective-permute-start | bytes 147464 | tf_op jit(solution)/shard_map/ppermute | solution.py:389
  63.9 12.6 %all-to-all-start.2 = ((bf16[16,112,128]{2,1,0:T(8,128)(2,1)}), bf16[16,112,128]{2,1,0:T(8,128)(2,1)S(1)}, u32[]{:S(2)}, u32[]{:S(2)}) async-start(bf16[16,112,128]{2,1,0:T(8,128)(2,1)} %get-tuple-element.55), calls=%async_computation.2 | async-start | bytes 917504 | tf_op jit(solution)/shard_map/all_to_all | solution.py:397
  67.8 4.2 %collective-permute-start.10 = (bf16[2,96,128]{2,1,0:T(8,128)(2,1)S(1)}, bf16[2,96,128]{2,1,0:T(8,128)(2,1)S(1)}, u32[]{:S(2)}, u32[]{:S(2)}) collective-permute-start(bf16[2,96,128]{2,1,0:T(8,128)(2,1)S(1)} %get-tuple-element.56), channel_id=1, source_target_pairs={{0,8},{1,9},{2,10},{3,11},{4,12},{5,13},{6,14},{7,15},{8,16},{9,17... | collective-permute-start | bytes 147464 | tf_op jit(solution)/shard_map/ppermute | solution.py:389
  76.5 5.8 %collective-permute-start.11 = (bf16[1792,128]{1,0:T(8,128)(2,1)S(1)}, bf16[1792,128]{1,0:T(8,128)(2,1)S(1)}, u32[]{:S(2)}, u32[]{:S(2)}) collective-permute-start(bf16[1792,128]{1,0:T(8,128)(2,1)S(1)} %bitcast.19), channel_id=1, source_target_pairs={{0,64},{64,0},{1,65},{65,1},{2,66},{66,2},{3,67},{67,3},{4,68},{68... | collective-permute-start | bytes 1376264 | tf_op jit(solution)/shard_map/ppermute | solution.py:393

commit v8 on v7

--- a/solution.py
+++ b/solution.py
@@ -133,7 +133,7 @@
 def main_kernel(
     near_own, near_x, lon_own, lon_x, vectors, wqkv, wout, wup, wdown_t,
     send_out, keep_out,
-    x, land_s, qkv, probs, qm_all, emb, xh1, r1, hid_xh, r2, gp, act, normed_s, mixed_s, nm_s,
+    x, loss, land_s, qkv, probs, qm_all, emb, xh1, r1, hid_xh, r2, gp, act, normed_s, mixed_s, nm_s,
     cot_s, dpre_s, dproj_s, dqkv_s, dstate, small, msg,
 ):
     core = lax.axis_index("core")
@@ -141,14 +141,18 @@
     last = jnp.logical_and(lax.axis_index("lat") == 7, jnp.logical_and(here == 1, core == 1))
     closed = jnp.where(last, 0.0, 1.0).astype(F32)
     for step in range(2):
-        x[2 * here + step, 0:HALF, :] = near_own[step].astype(F32)[0:HALF]
-        x[2 * here + step, HALF:WIN, :] = lon_own[step].astype(F32)[0:HALF]
-        x[2 * (1 - here) + step, 0:HALF, :] = near_x[step].astype(F32)[0:HALF]
-        x[2 * (1 - here) + step, HALF:WIN, :] = lon_x[step].astype(F32)[0:HALF]
+        for half, part, cells in (
+            (here, 0, near_own), (here, 1, lon_own), (1 - here, 0, near_x), (1 - here, 1, lon_x)
+        ):
+            rows = slice(HALF * part, HALF * part + HALF)
+            block = cells[step].astype(F32)[0:HALF]
+            x[2 * half + step, rows, :] = block[:, 0:CH]
+            loss[2 * half + step, rows, :] = block[:, CH:MSG]
     for part, cells in ((0, near_own), (1, lon_own)):
         line = cells[0].astype(F32)[HALF : HALF + 1, 0:128]
-        column = jnp.broadcast_to(line, (8, 128)).T
-        land_s[HALF * part : HALF * part + HALF, :] = column[0:HALF, 0:1]
+        column = jnp.broadcast_to(line, (128, 128)).T[0:HALF]
+        land_s[HALF * part : HALF * part + HALF, 0:128] = column
+        land_s[HALF * part : HALF * part + HALF, 128:CH] = column[:, 0 : CH - 128]
     le = vectors[0:1, :]
     ga = vectors[1:2, :]
     gm = vectors[2:3, :]
@@ -171,7 +175,7 @@
     for s in range(STEPS):
         rows = slice(WIN * s, WIN * s + WIN)
         land = land_s[...]
-        e = x[s, :, 0:CH] + land * le
+        e = x[s] + land * le
         emb[rows, :] = e
         off = e - mean_of(e)
         r = lax.rsqrt(mean_of(off * off) + EPS)
@@ -219,7 +223,7 @@
     dstate[...] = jnp.zeros_like(dstate)
     for s in range(STEPS - 1, -1, -1):
         rows = slice(WIN * s, WIN * s + WIN)
-        cot = x[s, :, CH:MSG]
+        cot = loss[s]
         if incoming is not None:
             cot = cot + incoming
         cotb = cot.astype(BF16)
@@ -455,8 +459,9 @@
         "window_steps",
         [((SENT, 128), BF16)] * 2,
         [
-            ((STEPS, WIN, MSG), F32),
-            ((WIN, 1), F32),
+            ((STEPS, WIN, CH), F32),
+            ((STEPS, WIN, CH), F32),
+            ((WIN, CH), F32),
             ((TOK, 3 * CH), F32),
             ((STEPS, WIN, HEADS * WIN), F32),
             ((STEPS, HEADS * WIN, CH), BF16),

time: 84 us -> 82.8 us (0.986)
  Pallas kernels: 14.4 us -> 13.1 us
    pallas_call x1, Pallas kernels: 9.19 us -> 7.94 us  [local(): call(main_kernel, 'window_steps', [((SENT, 128), BF16)] * 2, [((STEPS, WI...]
where the time goes in v8:
time: 82.8 us; the launch traced here: 82.4 us
  starting transfers between devices  34.5 us (42%)
  waiting for transfers between devices  21 us (25%)
  Pallas kernels  13.1 us (16%)
  blocking collectives  13 us (16%)
    ppermute x9, starting transfers between devices, hop(): return lax.ppermute(value, AXES, pairs)  18.1 us
    ppermute x9, waiting for transfers between devices, hop(): return lax.ppermute(value, AXES, pairs)  13.1 us
    all_to_all x1, blocking collectives, exchange(): return lax.all_to_all(value, axis, 0, 0, tiled=True)  13 us
    ppermute x3, starting transfers between devices, swap(): return lax.ppermute(value, axis, [(0, 1), (1, 0)])  9.16 us
    pallas_call x1, Pallas kernels, local(): call(main_kernel, 'window_steps', [((SENT, 128), BF16)] * 2, [((STEPS, WI...  7.94 us
    all_to_all x2, starting transfers between devices, exchange(): return lax.all_to_all(value, axis, 0, 0, tiled=True)  7.28 us
    all_to_all x2, waiting for transfers between devices, exchange(): return lax.all_to_all(value, axis, 0, 0, tiled=True)  5.65 us
    ppermute x3, waiting for transfers between devices, swap(): return lax.ppermute(value, axis, [(0, 1), (1, 0)])  2.26 us
  transfers between devices with their start and end apart: 14, of which 11 were waited for; matrix products, arithmetic and copies ran while one was open for 0% of the time, Pallas kernels for 1%

profile of v8, /device:TPU:1, one launch (start us, length us, event | category | flops | bytes accessed | tf_op | source)
XLA Modules:
  0.0 82.4 jit_solution(12522723554486030202)
XLA Ops:
  0.7 1.3 %pack_cells.1 = (bf16[2,2,40,384]{3,2,1,0:T(8,128)(2,1)S(1)}, bf16[2,2,40,384]{3,2,1,0:T(8,128)(2,1)S(1)}, bf16[2,24,384]{2,1,0:T(8,128)(2,1)S(1)}, f32[8,192]{1,0:T(8,128)S(1)}, bf16[192,576]{1,0:T(8,128)(2,1)S(1)}) custom-call(bf16[12,24,192]{2,1,0:T(8,128)(2,1)} %bitcast.23, bf16[12,24,192]{2,1,0:T(8,128)(2,1)} %bitcast.24, s32[12,24]{1,0:T(8,128)} %bitcast.25, ...), custom_call_target="tpu_custom_call" | custom-call | tf_op jit(solution)/shard_map/pack_cells/pallas_call | solution.py:421
  2.0 3.3 %collective-permute-start = (bf16[2,2,40,384]{3,2,1,0:T(8,128)(2,1)S(1)}, bf16[2,2,40,384]{3,2,1,0:T(8,128)(2,1)S(1)}, u32[]{:S(2)}, u32[]{:S(2)}) collective-permute-start(bf16[2,2,40,384]{3,2,1,0:T(8,128)(2,1)S(1)} %get-tuple-element.38), channel_id=1, source_target_pairs={{0,64},{64,0},{1,65},{65,1},{2,66},{66,2},{3,67},{67,3},{4,68},{68... | collective-permute-start | bytes 368648 | tf_op jit(solution)/shard_map/ppermute | solution.py:397
  5.3 1.3 %collective-permute-start.1 = (bf16[2,24,384]{2,1,0:T(8,128)(2,1)S(1)}, bf16[2,24,384]{2,1,0:T(8,128)(2,1)S(1)}, u32[]{:S(2)}, u32[]{:S(2)}) collective-permute-start(bf16[2,24,384]{2,1,0:T(8,128)(2,1)S(1)} %get-tuple-element.39), channel_id=1, source_target_pairs={{0,120},{1,121},{2,122},{3,123},{4,124},{5,125},{6,126},{7,127},{8... | collective-permute-start | bytes 110600 | tf_op jit(solution)/shard_map/ppermute | solution.py:393
  6.6 5.7 %collective-permute-start.2 = (bf16[2,24,384]{2,1,0:T(8,128)(2,1)S(1)}, bf16[2,24,384]{2,1,0:T(8,128)(2,1)S(1)}, u32[]{:S(2)}, u32[]{:S(2)}) collective-permute-start(bf16[2,24,384]{2,1,0:T(8,128)(2,1)S(1)} %get-tuple-element.39), channel_id=1, source_target_pairs={{64,120},{65,121},{66,122},{67,123},{68,124},{69,125},{70,126},{71... | collective-permute-start | bytes 110600 | tf_op jit(solution)/shard_map/ppermute | solution.py:393
  12.4 1.0 %collective-permute-done.2.edge1 = bf16[2,24,384]{2,1,0:T(8,128)(2,1)S(1)} collective-permute-done((bf16[2,24,384]{2,1,0:T(8,128)(2,1)S(1)}, bf16[2,24,384]{2,1,0:T(8,128)(2,1)S(1)}, u32[]{:S(2)}, u32[]{:S(2)}) %collective-permute-start.2) | collective-permute-done | bytes 36896 | tf_op jit(solution)/shard_map/ppermute | solution.py:393
  13.5 2.8 %collective-permute-start.3 = (bf16[2,40,384]{2,1,0:T(8,128)(2,1)S(1)}, bf16[2,40,384]{2,1,0:T(8,128)(2,1)S(1)}, u32[]{:S(2)}, u32[]{:S(2)}) collective-permute-start(bf16[2,40,384]{2,1,0:T(8,128)(2,1)S(1)} %get-tuple-element.41), channel_id=1, source_target_pairs={{0,128},{1,129},{2,130},{3,131},{4,132},{5,133},{6,134},{7,135},{8... | collective-permute-start | bytes 184328 | tf_op jit(solution)/shard_map/ppermute | solution.py:393
  16.4 2.8 %collective-permute-start.4 = (bf16[2,40,384]{2,1,0:T(8,128)(2,1)S(1)}, bf16[2,40,384]{2,1,0:T(8,128)(2,1)S(1)}, u32[]{:S(2)}, u32[]{:S(2)}) collective-permute-start(bf16[2,40,384]{2,1,0:T(8,128)(2,1)S(1)} %get-tuple-element.42), channel_id=1, source_target_pairs={{0,7},{1,0},{2,1},{3,2},{4,3},{5,4},{6,5},{7,6},{8,15},{9,8},{10,9... | collective-permute-start | bytes 184328 | tf_op jit(solution)/shard_map/ppermute | solution.py:393
  20.6 4.0 %collective-permute-done.5.lon_x = bf16[2,40,384]{2,1,0:T(8,128)(2,1)S(1)} collective-permute-done((bf16[2,40,384]{2,1,0:T(8,128)(2,1)S(1)}, bf16[2,40,384]{2,1,0:T(8,128)(2,1)S(1)}, u32[]{:S(2)}, u32[]{:S(2)}) %collective-permute-start.5) | collective-permute-done | bytes 61472 | tf_op jit(solution)/shard_map/ppermute | solution.py:393
  24.6 7.9 %window_steps.1 = (bf16[2176,128]{1,0:T(8,128)(2,1)S(1)}, bf16[2176,128]{1,0:T(8,128)(2,1)S(1)}) custom-call(bf16[2,40,384]{2,1,0:T(8,128)(2,1)S(1)} %get-tuple-element.40.near_own, bf16[2,40,384]{2,1,0:T(8,128)(2,1)S(1)} %collective-permute-done.3.near_x, bf16[2,40,384]{2,1,0:T(8,128)(2,1)S(1)} %collective-permute-done.4.lon_own, ...), custom_call_target="tpu_custom_call" | custom-call | tf_op jit(solution)/shard_map/window_steps/pallas_call | solution.py:457
  32.6 1.4 %collective-permute-start.6 = (bf16[2176,128]{1,0:T(8,128)(2,1)S(1)}, bf16[2176,128]{1,0:T(8,128)(2,1)S(1)}, u32[]{:S(2)}, u32[]{:S(2)}) collective-permute-start(bf16[2176,128]{1,0:T(8,128)(2,1)S(1)} %get-tuple-element.47), channel_id=1, source_target_pairs={{0,64},{64,0},{1,65},{65,1},{2,66},{66,2},{3,67},{67,3},{4,68},{68... | collective-permute-start | bytes 1671176 | tf_op jit(solution)/shard_map/ppermute | solution.py:397
  34.0 1.6 %collective-permute-done.6.arrived = bf16[2176,128]{1,0:T(8,128)(2,1)S(1)} collective-permute-done((bf16[2176,128]{1,0:T(8,128)(2,1)S(1)}, bf16[2176,128]{1,0:T(8,128)(2,1)S(1)}, u32[]{:S(2)}, u32[]{:S(2)}) %collective-permute-start.6) | collective-permute-done | bytes 557088 | tf_op jit(solution)/shard_map/ppermute | solution.py:397
  35.7 13.0 %all_to_all.15.terms = bf16[16,112,128]{2,1,0:T(8,128)(2,1)S(1)} all-to-all(bf16[16,112,128]{2,1,0:T(8,128)(2,1)S(1)} %get-tuple-element.48), channel_id=1, replica_groups=mesh['xh'=2,'core'=2,'lat'=8,'lon'=8] {'xh','lon'}, dimensions={0} | all-to-all | bytes 917504 | tf_op jit(solution)/shard_map/all_to_all | solution.py:401
  49.4 3.4 %all-to-all-start.1 = ((bf16[8,112,128]{2,1,0:T(8,128)(2,1)}), bf16[8,112,128]{2,1,0:T(8,128)(2,1)S(1)}, u32[]{:S(2)}, u32[]{:S(2)}) async-start(bf16[8,112,128]{2,1,0:T(8,128)(2,1)} %sum_group.1), calls=%async_computation.1 | async-start | bytes 458752 | tf_op jit(solution)/shard_map/all_to_all | solution.py:401
  52.8 1.1 %collective-permute-start.7 = (bf16[2,96,128]{2,1,0:T(8,128)(2,1)S(1)}, bf16[2,96,128]{2,1,0:T(8,128)(2,1)S(1)}, u32[]{:S(2)}, u32[]{:S(2)}) collective-permute-start(bf16[2,96,128]{2,1,0:T(8,128)(2,1)S(1)} %get-tuple-element.50), channel_id=1, source_target_pairs={{0,128},{1,129},{2,130},{3,131},{4,132},{5,133},{6,134},{7,135},{8... | collective-permute-start | bytes 147464 | tf_op jit(solution)/shard_map/ppermute | solution.py:393
  54.1 2.2 %collective-permute-start.9 = (bf16[2,96,128]{2,1,0:T(8,128)(2,1)S(1)}, bf16[2,96,128]{2,1,0:T(8,128)(2,1)S(1)}, u32[]{:S(2)}, u32[]{:S(2)}) collective-permute-start(bf16[2,96,128]{2,1,0:T(8,128)(2,1)S(1)} %get-tuple-element.52), channel_id=1, source_target_pairs={{0,129},{1,130},{2,131},{3,132},{4,133},{5,134},{6,135},{7,128},{8... | collective-permute-start | bytes 147464 | tf_op jit(solution)/shard_map/ppermute | solution.py:393
  56.3 1.1 %collective-permute-done.7.near_x = bf16[2,96,128]{2,1,0:T(8,128)(2,1)S(1)} collective-permute-done((bf16[2,96,128]{2,1,0:T(8,128)(2,1)S(1)}, bf16[2,96,128]{2,1,0:T(8,128)(2,1)S(1)}, u32[]{:S(2)}, u32[]{:S(2)}) %collective-permute-start.7) | collective-permute-done | bytes 49184 | tf_op jit(solution)/shard_map/ppermute | solution.py:393
  57.4 1.6 %collective-permute-done.8.lon_own = bf16[2,96,128]{2,1,0:T(8,128)(2,1)S(1)} collective-permute-done((bf16[2,96,128]{2,1,0:T(8,128)(2,1)S(1)}, bf16[2,96,128]{2,1,0:T(8,128)(2,1)S(1)}, u32[]{:S(2)}, u32[]{:S(2)}) %collective-permute-start.8) | collective-permute-done | bytes 49184 | tf_op jit(solution)/shard_map/ppermute | solution.py:393
  58.9 1.7 %collective-permute-done.9.lon_x = bf16[2,96,128]{2,1,0:T(8,128)(2,1)S(1)} collective-permute-done((bf16[2,96,128]{2,1,0:T(8,128)(2,1)S(1)}, bf16[2,96,128]{2,1,0:T(8,128)(2,1)S(1)}, u32[]{:S(2)}, u32[]{:S(2)}) %collective-permute-start.9) | collective-permute-done | bytes 49184 | tf_op jit(solution)/shard_map/ppermute | solution.py:393
  60.6 1.2 %all-to-all-done.1.terms = bf16[8,112,128]{2,1,0:T(8,128)(2,1)S(1)} async-done(((bf16[8,112,128]{2,1,0:T(8,128)(2,1)}), bf16[8,112,128]{2,1,0:T(8,128)(2,1)S(1)}, u32[]{:S(2)}, u32[]{:S(2)}) %all-to-all-start.1) | async-done | bytes 229408 | tf_op jit(solution)/shard_map/all_to_all | solution.py:401
  62.7 3.9 %all-to-all-start.2 = ((bf16[16,112,128]{2,1,0:T(8,128)(2,1)}), bf16[16,112,128]{2,1,0:T(8,128)(2,1)S(1)}, u32[]{:S(2)}, u32[]{:S(2)}) async-start(bf16[16,112,128]{2,1,0:T(8,128)(2,1)} %get-tuple-element.55), calls=%async_computation.2 | async-start | bytes 917504 | tf_op jit(solution)/shard_map/all_to_all | solution.py:401
  67.5 3.2 %collective-permute-done.10.edges = bf16[2,96,128]{2,1,0:T(8,128)(2,1)S(1)} collective-permute-done((bf16[2,96,128]{2,1,0:T(8,128)(2,1)S(1)}, bf16[2,96,128]{2,1,0:T(8,128)(2,1)S(1)}, u32[]{:S(2)}, u32[]{:S(2)}) %collective-permute-start.10) | collective-permute-done | bytes 49184 | tf_op jit(solution)/shard_map/ppermute | solution.py:393
  70.8 4.5 %all-to-all-done.2 = bf16[16,112,128]{2,1,0:T(8,128)(2,1)S(1)} async-done(((bf16[16,112,128]{2,1,0:T(8,128)(2,1)}), bf16[16,112,128]{2,1,0:T(8,128)(2,1)S(1)}, u32[]{:S(2)}, u32[]{:S(2)}) %all-to-all-start.2) | async-done | bytes 458784 | tf_op jit(solution)/shard_map/all_to_all | solution.py:401
  75.2 4.4 %collective-permute-start.11 = (bf16[1792,128]{1,0:T(8,128)(2,1)S(1)}, bf16[1792,128]{1,0:T(8,128)(2,1)S(1)}, u32[]{:S(2)}, u32[]{:S(2)}) collective-permute-start(bf16[1792,128]{1,0:T(8,128)(2,1)S(1)} %bitcast.19), channel_id=1, source_target_pairs={{0,64},{64,0},{1,65},{65,1},{2,66},{66,2},{3,67},{67,3},{4,68},{68... | collective-permute-start | bytes 1376264 | tf_op jit(solution)/shard_map/ppermute | solution.py:397
  81.1 1.3 %unpack_sums.1 = (f32[192,576]{1,0:T(8,128)}, f32[192,192]{1,0:T(8,128)}, f32[192,768]{1,0:T(8,128)}, f32[192,768]{1,0:T(8,128)}, f32[1,192]{1,0:T(1,128)}, /*index=5*/f32[1,192]{1,0:T(1,128)}, f32[1,192]{1,0:T(1,128)}) custom-call(bf16[1792,128]{1,0:T(8,128)(2,1)S(1)} %bitcast.20, bf16[1792,128]{1,0:T(8,128)(2,1)S(1)} %collective-permute-done.11.other), custom_call_target="tpu_custom_call" | custom-call | tf_op jit(solution)/shard_map/unpack_sums/pallas_call | solution.py:514
  (19 shorter events, 6.0 us)
Async XLA Ops:
  0.6 24.0 %copy-start.1 = (bf16[768,192]{0,1:T(8,128)(2,1)S(1)}, bf16[768,192]{0,1:T(8,128)(2,1)}, u32[]{:S(2)}) copy-start(bf16[768,192]{0,1:T(8,128)(2,1)} %param.19) | copy-start | bytes 884740
  0.6 24.0 %copy-start.2 = (bf16[192,192]{1,0:T(8,128)(2,1)S(1)}, bf16[192,192]{1,0:T(8,128)(2,1)}, u32[]{:S(2)}) copy-start(bf16[192,192]{1,0:T(8,128)(2,1)} %wout.1) | copy-start | bytes 221188
  2.0 22.6 %copy-start = (bf16[192,768]{1,0:T(8,128)(2,1)S(1)}, bf16[192,768]{1,0:T(8,128)(2,1)}, u32[]{:S(2)}) copy-start(bf16[192,768]{1,0:T(8,128)(2,1)} %wup.1) | copy-start | bytes 884740
  2.0 11.4 %collective-permute-start = (bf16[2,2,40,384]{3,2,1,0:T(8,128)(2,1)S(1)}, bf16[2,2,40,384]{3,2,1,0:T(8,128)(2,1)S(1)}, u32[]{:S(2)}, u32[]{:S(2)}) collective-permute-start(bf16[2,2,40,384]{3,2,1,0:T(8,128)(2,1)S(1)} %get-tuple-element.38), channel_id=1, source_target_pairs={{0,64},{64,0},{1,65},{65,1},{2,66},{66,2},{3,67},{67,3},{4,68},{68... | collective-permute-start | bytes 368648 | tf_op jit(solution)/shard_map/ppermute | solution.py:397
  5.3 7.0 %collective-permute-start.1 = (bf16[2,24,384]{2,1,0:T(8,128)(2,1)S(1)}, bf16[2,24,384]{2,1,0:T(8,128)(2,1)S(1)}, u32[]{:S(2)}, u32[]{:S(2)}) collective-permute-start(bf16[2,24,384]{2,1,0:T(8,128)(2,1)S(1)} %get-tuple-element.39), channel_id=1, source_target_pairs={{0,120},{1,121},{2,122},{3,123},{4,124},{5,125},{6,126},{7,127},{8... | collective-permute-start | bytes 110600 | tf_op jit(solution)/shard_map/ppermute | solution.py:393
  6.6 6.8 %collective-permute-start.2 = (bf16[2,24,384]{2,1,0:T(8,128)(2,1)S(1)}, bf16[2,24,384]{2,1,0:T(8,128)(2,1)S(1)}, u32[]{:S(2)}, u32[]{:S(2)}) collective-permute-start(bf16[2,24,384]{2,1,0:T(8,128)(2,1)S(1)} %get-tuple-element.39), channel_id=1, source_target_pairs={{64,120},{65,121},{66,122},{67,123},{68,124},{69,125},{70,126},{71... | collective-permute-start | bytes 110600 | tf_op jit(solution)/shard_map/ppermute | solution.py:393
  13.5 6.6 %collective-permute-start.3 = (bf16[2,40,384]{2,1,0:T(8,128)(2,1)S(1)}, bf16[2,40,384]{2,1,0:T(8,128)(2,1)S(1)}, u32[]{:S(2)}, u32[]{:S(2)}) collective-permute-start(bf16[2,40,384]{2,1,0:T(8,128)(2,1)S(1)} %get-tuple-element.41), channel_id=1, source_target_pairs={{0,128},{1,129},{2,130},{3,131},{4,132},{5,133},{6,134},{7,135},{8... | collective-permute-start | bytes 184328 | tf_op jit(solution)/shard_map/ppermute | solution.py:393
  16.4 4.3 %collective-permute-start.4 = (bf16[2,40,384]{2,1,0:T(8,128)(2,1)S(1)}, bf16[2,40,384]{2,1,0:T(8,128)(2,1)S(1)}, u32[]{:S(2)}, u32[]{:S(2)}) collective-permute-start(bf16[2,40,384]{2,1,0:T(8,128)(2,1)S(1)} %get-tuple-element.42), channel_id=1, source_target_pairs={{0,7},{1,0},{2,1},{3,2},{4,3},{5,4},{6,5},{7,6},{8,15},{9,8},{10,9... | collective-permute-start | bytes 184328 | tf_op jit(solution)/shard_map/ppermute | solution.py:393
  19.1 5.5 %collective-permute-start.5 = (bf16[2,40,384]{2,1,0:T(8,128)(2,1)S(1)}, bf16[2,40,384]{2,1,0:T(8,128)(2,1)S(1)}, u32[]{:S(2)}, u32[]{:S(2)}) collective-permute-start(bf16[2,40,384]{2,1,0:T(8,128)(2,1)S(1)} %get-tuple-element.43), channel_id=1, source_target_pairs={{0,135},{1,128},{2,129},{3,130},{4,131},{5,132},{6,133},{7,134},{8... | collective-permute-start | bytes 184328 | tf_op jit(solution)/shard_map/ppermute | solution.py:393
  32.6 3.0 %collective-permute-start.6 = (bf16[2176,128]{1,0:T(8,128)(2,1)S(1)}, bf16[2176,128]{1,0:T(8,128)(2,1)S(1)}, u32[]{:S(2)}, u32[]{:S(2)}) collective-permute-start(bf16[2176,128]{1,0:T(8,128)(2,1)S(1)} %get-tuple-element.47), channel_id=1, source_target_pairs={{0,64},{64,0},{1,65},{65,1},{2,66},{66,2},{3,67},{67,3},{4,68},{68... | collective-permute-start | bytes 1671176 | tf_op jit(solution)/shard_map/ppermute | solution.py:397
  49.4 12.4 %all-to-all-start.1 = ((bf16[8,112,128]{2,1,0:T(8,128)(2,1)}), bf16[8,112,128]{2,1,0:T(8,128)(2,1)S(1)}, u32[]{:S(2)}, u32[]{:S(2)}) async-start(bf16[8,112,128]{2,1,0:T(8,128)(2,1)} %sum_group.1), calls=%async_computation.1 | async-start | bytes 458752 | tf_op jit(solution)/shard_map/all_to_all | solution.py:401
  52.8 4.5 %collective-permute-start.7 = (bf16[2,96,128]{2,1,0:T(8,128)(2,1)S(1)}, bf16[2,96,128]{2,1,0:T(8,128)(2,1)S(1)}, u32[]{:S(2)}, u32[]{:S(2)}) collective-permute-start(bf16[2,96,128]{2,1,0:T(8,128)(2,1)S(1)} %get-tuple-element.50), channel_id=1, source_target_pairs={{0,128},{1,129},{2,130},{3,131},{4,132},{5,133},{6,134},{7,135},{8... | collective-permute-start | bytes 147464 | tf_op jit(solution)/shard_map/ppermute | solution.py:393
  53.9 5.0 %collective-permute-start.8 = (bf16[2,96,128]{2,1,0:T(8,128)(2,1)S(1)}, bf16[2,96,128]{2,1,0:T(8,128)(2,1)S(1)}, u32[]{:S(2)}, u32[]{:S(2)}) collective-permute-start(bf16[2,96,128]{2,1,0:T(8,128)(2,1)S(1)} %get-tuple-element.51), channel_id=1, source_target_pairs={{0,1},{1,2},{2,3},{3,4},{4,5},{5,6},{6,7},{7,0},{8,9},{9,10},{10,1... | collective-permute-start | bytes 147464 | tf_op jit(solution)/shard_map/ppermute | solution.py:393
  54.1 6.5 %collective-permute-start.9 = (bf16[2,96,128]{2,1,0:T(8,128)(2,1)S(1)}, bf16[2,96,128]{2,1,0:T(8,128)(2,1)S(1)}, u32[]{:S(2)}, u32[]{:S(2)}) collective-permute-start(bf16[2,96,128]{2,1,0:T(8,128)(2,1)S(1)} %get-tuple-element.52), channel_id=1, source_target_pairs={{0,129},{1,130},{2,131},{3,132},{4,133},{5,134},{6,135},{7,128},{8... | collective-permute-start | bytes 147464 | tf_op jit(solution)/shard_map/ppermute | solution.py:393
  62.7 12.6 %all-to-all-start.2 = ((bf16[16,112,128]{2,1,0:T(8,128)(2,1)}), bf16[16,112,128]{2,1,0:T(8,128)(2,1)S(1)}, u32[]{:S(2)}, u32[]{:S(2)}) async-start(bf16[16,112,128]{2,1,0:T(8,128)(2,1)} %get-tuple-element.55), calls=%async_computation.2 | async-start | bytes 917504 | tf_op jit(solution)/shard_map/all_to_all | solution.py:401
  66.5 4.2 %collective-permute-start.10 = (bf16[2,96,128]{2,1,0:T(8,128)(2,1)S(1)}, bf16[2,96,128]{2,1,0:T(8,128)(2,1)S(1)}, u32[]{:S(2)}, u32[]{:S(2)}) collective-permute-start(bf16[2,96,128]{2,1,0:T(8,128)(2,1)S(1)} %get-tuple-element.56), channel_id=1, source_target_pairs={{0,8},{1,9},{2,10},{3,11},{4,12},{5,13},{6,14},{7,15},{8,16},{9,17... | collective-permute-start | bytes 147464 | tf_op jit(solution)/shard_map/ppermute | solution.py:393
  75.2 5.8 %collective-permute-start.11 = (bf16[1792,128]{1,0:T(8,128)(2,1)S(1)}, bf16[1792,128]{1,0:T(8,128)(2,1)S(1)}, u32[]{:S(2)}, u32[]{:S(2)}) collective-permute-start(bf16[1792,128]{1,0:T(8,128)(2,1)S(1)} %bitcast.19), channel_id=1, source_target_pairs={{0,64},{64,0},{1,65},{65,1},{2,66},{66,2},{3,67},{67,3},{4,68},{68... | collective-permute-start | bytes 1376264 | tf_op jit(solution)/shard_map/ppermute | solution.py:397

commit v9 on v8

--- a/solution.py
+++ b/solution.py
@@ -131,7 +131,7 @@
 
 
 def main_kernel(
-    near_own, near_x, lon_own, lon_x, vectors, wqkv, wout, wup, wdown_t,
+    lon_x, near_x, lon_own, near_own, vectors, wqkv, wout, wup, wdown_t,
     send_out, keep_out,
     x, loss, land_s, qkv, probs, qm_all, emb, xh1, r1, hid_xh, r2, gp, act, normed_s, mixed_s, nm_s,
     cot_s, dpre_s, dproj_s, dqkv_s, dstate, small, msg,
@@ -322,7 +322,7 @@
         total_out[g] = total
 
 
-def column_kernel(terms, near_own, near_x, lon_own, lon_x, total_out, near, lon, to_lat):
+def column_kernel(terms, lon_x, near_x, lon_own, near_own, total_out, near, lon, to_lat):
     here = lax.axis_index("xh")
     for c in range(2):
         near[2 * here + c] = near_own[c]
@@ -451,9 +451,9 @@
         keep, swap(send, "core"),
         hop(edge, -1, 0, cores=((0, 1),)), hop(edge, -1, 0, cores=((1, 1),)),
     )
+    lon_x = hop(lon_x, 0, -1, 1)
     near_x = hop(near_x, 0, 0, 1)
     lon_own = hop(lon_own, 0, -1)
-    lon_x = hop(lon_x, 0, -1, 1)
     send, keep = call(
         main_kernel,
         "window_steps",
@@ -485,7 +485,7 @@
         ],
         mib=24,
     )(
-        near_own, near_x, lon_own, lon_x, vectors, w_qkv, w_out, w_up, w_down.T
+        lon_x, near_x, lon_own, near_own, vectors, w_qkv, w_out, w_up, w_down.T
     )
 
     chunks, near_own, near_x, lon_own, lon_x = call(
@@ -493,9 +493,9 @@
         "sum_cores",
         [((GROUP, UNIT, 128), BF16)] + [((2, COLUMNS, 128), BF16)] * 4,
     )(keep, swap(send, "core"))
+    lon_x = hop(lon_x, 0, 1, 1)
     near_x = hop(near_x, 0, 0, 1)
     lon_own = hop(lon_own, 0, 1)
-    lon_x = hop(lon_x, 0, 1, 1)
     (partial,) = call(group_kernel, "sum_group", [((8, UNIT, 128), BF16)])(
         exchange(chunks, ("xh", "lon"))
     )
@@ -505,7 +505,7 @@
         [((GROUP, UNIT, 128), BF16)]
         + [((4, COLUMNS, 128), BF16)] * 2
         + [((2, COLUMNS, 128), BF16)],
-    )(exchange(partial, "lat"), near_own, near_x, lon_own, lon_x)
+    )(exchange(partial, "lat"), lon_x, near_x, lon_own, near_own)
     own, edges = lax.optimization_barrier((exchange(total, ("xh", "lon")), hop(to_lat, 1, 0)))
     own = own.reshape(SUMS, 128)
     (state_grads,) = call(state_kernel, "unpack_states", [((WIN_LON, ROWS, CH), F32)])(

time: 82.8 us -> 83.4 us (level)
  blocking collectives: 13 us -> 15.5 us
  waiting for transfers between devices: 21 us -> 20 us
    all_to_all x1, blocking collectives: 13 us -> 15.5 us  [exchange(): return lax.all_to_all(value, axis, 0, 0, tiled=True)]
  transfers between devices with their start and end apart: 14 -> 14, of which waited for: 11 -> 10; matrix products, arithmetic and copies ran while one was open for 0% -> 0% of each run, Pallas kernels for 1% -> 1%
where the time goes in v9:
time: 83.4 us; the launch traced here: 83.1 us
  starting transfers between devices  33.7 us (40%)
  waiting for transfers between devices  20 us (24%)
  blocking collectives  15.5 us (19%)
  Pallas kernels  13.2 us (16%)
    ppermute x9, starting transfers between devices, hop(): return lax.ppermute(value, AXES, pairs)  18 us
    all_to_all x1, blocking collectives, exchange(): return lax.all_to_all(value, axis, 0, 0, tiled=True)  15.5 us
    ppermute x9, waiting for transfers between devices, hop(): return lax.ppermute(value, AXES, pairs)  12.9 us
    ppermute x3, starting transfers between devices, swap(): return lax.ppermute(value, axis, [(0, 1), (1, 0)])  8.43 us
    pallas_call x1, Pallas kernels, local(): call(main_kernel, 'window_steps', [((SENT, 128), BF16)] * 2, [((STEPS, WI...  7.95 us
    all_to_all x2, starting transfers between devices, exchange(): return lax.all_to_all(value, axis, 0, 0, tiled=True)  7.23 us
    all_to_all x2, waiting for transfers between devices, exchange(): return lax.all_to_all(value, axis, 0, 0, tiled=True)  4.84 us
    ppermute x3, waiting for transfers between devices, swap(): return lax.ppermute(value, axis, [(0, 1), (1, 0)])  2.26 us
  transfers between devices with their start and end apart: 14, of which 10 were waited for; matrix products, arithmetic and copies ran while one was open for 0% of the time, Pallas kernels for 1%

profile of v9, /device:TPU:1, one launch (start us, length us, event | category | flops | bytes accessed | tf_op | source)
XLA Modules:
  0.0 83.1 jit_solution(4743560411176697392)
XLA Ops:
  0.7 1.3 %pack_cells.1 = (bf16[2,2,40,384]{3,2,1,0:T(8,128)(2,1)S(1)}, bf16[2,2,40,384]{3,2,1,0:T(8,128)(2,1)S(1)}, bf16[2,24,384]{2,1,0:T(8,128)(2,1)S(1)}, f32[8,192]{1,0:T(8,128)S(1)}, bf16[192,576]{1,0:T(8,128)(2,1)S(1)}) custom-call(bf16[12,24,192]{2,1,0:T(8,128)(2,1)} %bitcast.23, bf16[12,24,192]{2,1,0:T(8,128)(2,1)} %bitcast.24, s32[12,24]{1,0:T(8,128)} %bitcast.25, ...), custom_call_target="tpu_custom_call" | custom-call | tf_op jit(solution)/shard_map/pack_cells/pallas_call | solution.py:421
  2.0 3.3 %collective-permute-start = (bf16[2,2,40,384]{3,2,1,0:T(8,128)(2,1)S(1)}, bf16[2,2,40,384]{3,2,1,0:T(8,128)(2,1)S(1)}, u32[]{:S(2)}, u32[]{:S(2)}) collective-permute-start(bf16[2,2,40,384]{3,2,1,0:T(8,128)(2,1)S(1)} %get-tuple-element.38), channel_id=1, source_target_pairs={{0,64},{64,0},{1,65},{65,1},{2,66},{66,2},{3,67},{67,3},{4,68},{68... | collective-permute-start | bytes 368648 | tf_op jit(solution)/shard_map/ppermute | solution.py:397
  5.3 1.3 %collective-permute-start.1 = (bf16[2,24,384]{2,1,0:T(8,128)(2,1)S(1)}, bf16[2,24,384]{2,1,0:T(8,128)(2,1)S(1)}, u32[]{:S(2)}, u32[]{:S(2)}) collective-permute-start(bf16[2,24,384]{2,1,0:T(8,128)(2,1)S(1)} %get-tuple-element.39), channel_id=1, source_target_pairs={{0,120},{1,121},{2,122},{3,123},{4,124},{5,125},{6,126},{7,127},{8... | collective-permute-start | bytes 110600 | tf_op jit(solution)/shard_map/ppermute | solution.py:393
  6.6 5.7 %collective-permute-start.2 = (bf16[2,24,384]{2,1,0:T(8,128)(2,1)S(1)}, bf16[2,24,384]{2,1,0:T(8,128)(2,1)S(1)}, u32[]{:S(2)}, u32[]{:S(2)}) collective-permute-start(bf16[2,24,384]{2,1,0:T(8,128)(2,1)S(1)} %get-tuple-element.39), channel_id=1, source_target_pairs={{64,120},{65,121},{66,122},{67,123},{68,124},{69,125},{70,126},{71... | collective-permute-start | bytes 110600 | tf_op jit(solution)/shard_map/ppermute | solution.py:393
  12.4 1.0 %collective-permute-done.2.edge1 = bf16[2,24,384]{2,1,0:T(8,128)(2,1)S(1)} collective-permute-done((bf16[2,24,384]{2,1,0:T(8,128)(2,1)S(1)}, bf16[2,24,384]{2,1,0:T(8,128)(2,1)S(1)}, u32[]{:S(2)}, u32[]{:S(2)}) %collective-permute-start.2) | collective-permute-done | bytes 36896 | tf_op jit(solution)/shard_map/ppermute | solution.py:393
  13.5 5.0 %collective-permute-start.3 = (bf16[2,40,384]{2,1,0:T(8,128)(2,1)S(1)}, bf16[2,40,384]{2,1,0:T(8,128)(2,1)S(1)}, u32[]{:S(2)}, u32[]{:S(2)}) collective-permute-start(bf16[2,40,384]{2,1,0:T(8,128)(2,1)S(1)} %get-tuple-element.40), channel_id=1, source_target_pairs={{0,135},{1,128},{2,129},{3,130},{4,131},{5,132},{6,133},{7,134},{8... | collective-permute-start | bytes 184328 | tf_op jit(solution)/shard_map/ppermute | solution.py:393
  19.1 1.4 %collective-permute-start.5 = (bf16[2,40,384]{2,1,0:T(8,128)(2,1)S(1)}, bf16[2,40,384]{2,1,0:T(8,128)(2,1)S(1)}, u32[]{:S(2)}, u32[]{:S(2)}) collective-permute-start(bf16[2,40,384]{2,1,0:T(8,128)(2,1)S(1)} %get-tuple-element.42), channel_id=1, source_target_pairs={{0,7},{1,0},{2,1},{3,2},{4,3},{5,4},{6,5},{7,6},{8,15},{9,8},{10,9... | collective-permute-start | bytes 184328 | tf_op jit(solution)/shard_map/ppermute | solution.py:393
  20.4 1.0 %collective-permute-done.3.lon_x = bf16[2,40,384]{2,1,0:T(8,128)(2,1)S(1)} collective-permute-done((bf16[2,40,384]{2,1,0:T(8,128)(2,1)S(1)}, bf16[2,40,384]{2,1,0:T(8,128)(2,1)S(1)}, u32[]{:S(2)}, u32[]{:S(2)}) %collective-permute-start.3) | collective-permute-done | bytes 61472 | tf_op jit(solution)/shard_map/ppermute | solution.py:393
  21.4 2.3 %collective-permute-done.4.near_x = bf16[2,40,384]{2,1,0:T(8,128)(2,1)S(1)} collective-permute-done((bf16[2,40,384]{2,1,0:T(8,128)(2,1)S(1)}, bf16[2,40,384]{2,1,0:T(8,128)(2,1)S(1)}, u32[]{:S(2)}, u32[]{:S(2)}) %collective-permute-start.4) | collective-permute-done | bytes 61472 | tf_op jit(solution)/shard_map/ppermute | solution.py:393
  23.8 8.0 %window_steps.1 = (bf16[2176,128]{1,0:T(8,128)(2,1)S(1)}, bf16[2176,128]{1,0:T(8,128)(2,1)S(1)}) custom-call(bf16[2,40,384]{2,1,0:T(8,128)(2,1)S(1)} %collective-permute-done.3.lon_x, bf16[2,40,384]{2,1,0:T(8,128)(2,1)S(1)} %collective-permute-done.4.near_x, bf16[2,40,384]{2,1,0:T(8,128)(2,1)S(1)} %collective-permute-done.5.lon_own, ...), custom_call_target="tpu_custom_call" | custom-call | tf_op jit(solution)/shard_map/window_steps/pallas_call | solution.py:457
  31.7 0.8 collective-permute-start.6
  32.5 1.6 %collective-permute-done.6.arrived = bf16[2176,128]{1,0:T(8,128)(2,1)S(1)} collective-permute-done((bf16[2176,128]{1,0:T(8,128)(2,1)S(1)}, bf16[2176,128]{1,0:T(8,128)(2,1)S(1)}, u32[]{:S(2)}, u32[]{:S(2)}) %collective-permute-start.6) | collective-permute-done | bytes 557088 | tf_op jit(solution)/shard_map/ppermute | solution.py:397
  34.2 15.5 %all_to_all.15.terms = bf16[16,112,128]{2,1,0:T(8,128)(2,1)S(1)} all-to-all(bf16[16,112,128]{2,1,0:T(8,128)(2,1)S(1)} %get-tuple-element.48), channel_id=1, replica_groups=mesh['xh'=2,'core'=2,'lat'=8,'lon'=8] {'xh','lon'}, dimensions={0} | all-to-all | bytes 917504 | tf_op jit(solution)/shard_map/all_to_all | solution.py:401
  50.4 3.4 %all-to-all-start.1 = ((bf16[8,112,128]{2,1,0:T(8,128)(2,1)}), bf16[8,112,128]{2,1,0:T(8,128)(2,1)S(1)}, u32[]{:S(2)}, u32[]{:S(2)}) async-start(bf16[8,112,128]{2,1,0:T(8,128)(2,1)} %sum_group.1), calls=%async_computation.1 | async-start | bytes 458752 | tf_op jit(solution)/shard_map/all_to_all | solution.py:401
  53.9 1.0 %collective-permute-start.7 = (bf16[2,96,128]{2,1,0:T(8,128)(2,1)S(1)}, bf16[2,96,128]{2,1,0:T(8,128)(2,1)S(1)}, u32[]{:S(2)}, u32[]{:S(2)}) collective-permute-start(bf16[2,96,128]{2,1,0:T(8,128)(2,1)S(1)} %get-tuple-element.49), channel_id=1, source_target_pairs={{0,129},{1,130},{2,131},{3,132},{4,133},{5,134},{6,135},{7,128},{8... | collective-permute-start | bytes 147464 | tf_op jit(solution)/shard_map/ppermute | solution.py:393
  54.8 2.1 %collective-permute-start.8 = (bf16[2,96,128]{2,1,0:T(8,128)(2,1)S(1)}, bf16[2,96,128]{2,1,0:T(8,128)(2,1)S(1)}, u32[]{:S(2)}, u32[]{:S(2)}) collective-permute-start(bf16[2,96,128]{2,1,0:T(8,128)(2,1)S(1)} %get-tuple-element.50), channel_id=1, source_target_pairs={{0,128},{1,129},{2,130},{3,131},{4,132},{5,133},{6,134},{7,135},{8... | collective-permute-start | bytes 147464 | tf_op jit(solution)/shard_map/ppermute | solution.py:393
  57.3 2.9 %collective-permute-done.7.lon_x = bf16[2,96,128]{2,1,0:T(8,128)(2,1)S(1)} collective-permute-done((bf16[2,96,128]{2,1,0:T(8,128)(2,1)S(1)}, bf16[2,96,128]{2,1,0:T(8,128)(2,1)S(1)}, u32[]{:S(2)}, u32[]{:S(2)}) %collective-permute-start.7) | collective-permute-done | bytes 49184 | tf_op jit(solution)/shard_map/ppermute | solution.py:393
  60.2 2.1 %collective-permute-done.9.lon_own = bf16[2,96,128]{2,1,0:T(8,128)(2,1)S(1)} collective-permute-done((bf16[2,96,128]{2,1,0:T(8,128)(2,1)S(1)}, bf16[2,96,128]{2,1,0:T(8,128)(2,1)S(1)}, u32[]{:S(2)}, u32[]{:S(2)}) %collective-permute-start.9) | collective-permute-done | bytes 49184 | tf_op jit(solution)/shard_map/ppermute | solution.py:393
  62.7 0.8 %sum_column.1 = (bf16[16,112,128]{2,1,0:T(8,128)(2,1)}, bf16[4,96,128]{2,1,0:T(8,128)(2,1)S(1)}, bf16[4,96,128]{2,1,0:T(8,128)(2,1)S(1)}, bf16[2,96,128]{2,1,0:T(8,128)(2,1)S(1)}) custom-call(bf16[8,112,128]{2,1,0:T(8,128)(2,1)S(1)} %all-to-all-done.1.terms, bf16[2,96,128]{2,1,0:T(8,128)(2,1)S(1)} %collective-permute-done.7.lon_x, ...), custom_call_target="tpu_custom_call" | custom-call | tf_op jit(solution)/shard_map/sum_column/pallas_call | solution.py:502
  63.5 3.8 %all-to-all-start.2 = ((bf16[16,112,128]{2,1,0:T(8,128)(2,1)}), bf16[16,112,128]{2,1,0:T(8,128)(2,1)S(1)}, u32[]{:S(2)}, u32[]{:S(2)}) async-start(bf16[16,112,128]{2,1,0:T(8,128)(2,1)} %get-tuple-element.55), calls=%async_computation.2 | async-start | bytes 917504 | tf_op jit(solution)/shard_map/all_to_all | solution.py:401
  68.0 3.6 %collective-permute-done.10.edges = bf16[2,96,128]{2,1,0:T(8,128)(2,1)S(1)} collective-permute-done((bf16[2,96,128]{2,1,0:T(8,128)(2,1)S(1)}, bf16[2,96,128]{2,1,0:T(8,128)(2,1)S(1)}, u32[]{:S(2)}, u32[]{:S(2)}) %collective-permute-start.10) | collective-permute-done | bytes 49184 | tf_op jit(solution)/shard_map/ppermute | solution.py:393
  71.6 4.4 %all-to-all-done.2 = bf16[16,112,128]{2,1,0:T(8,128)(2,1)S(1)} async-done(((bf16[16,112,128]{2,1,0:T(8,128)(2,1)}), bf16[16,112,128]{2,1,0:T(8,128)(2,1)S(1)}, u32[]{:S(2)}, u32[]{:S(2)}) %all-to-all-start.2) | async-done | bytes 458784 | tf_op jit(solution)/shard_map/all_to_all | solution.py:401
  76.0 4.3 %collective-permute-start.11 = (bf16[1792,128]{1,0:T(8,128)(2,1)S(1)}, bf16[1792,128]{1,0:T(8,128)(2,1)S(1)}, u32[]{:S(2)}, u32[]{:S(2)}) collective-permute-start(bf16[1792,128]{1,0:T(8,128)(2,1)S(1)} %bitcast.19), channel_id=1, source_target_pairs={{0,64},{64,0},{1,65},{65,1},{2,66},{66,2},{3,67},{67,3},{4,68},{68... | collective-permute-start | bytes 1376264 | tf_op jit(solution)/shard_map/ppermute | solution.py:397
  81.8 1.3 %unpack_sums.1 = (f32[192,576]{1,0:T(8,128)}, f32[192,192]{1,0:T(8,128)}, f32[192,768]{1,0:T(8,128)}, f32[192,768]{1,0:T(8,128)}, f32[1,192]{1,0:T(1,128)}, /*index=5*/f32[1,192]{1,0:T(1,128)}, f32[1,192]{1,0:T(1,128)}) custom-call(bf16[1792,128]{1,0:T(8,128)(2,1)S(1)} %bitcast.20, bf16[1792,128]{1,0:T(8,128)(2,1)S(1)} %collective-permute-done.11.other), custom_call_target="tpu_custom_call" | custom-call | tf_op jit(solution)/shard_map/unpack_sums/pallas_call | solution.py:514
  (19 shorter events, 4.4 us)
Async XLA Ops:
  0.6 23.1 %copy-start.1 = (bf16[768,192]{0,1:T(8,128)(2,1)S(1)}, bf16[768,192]{0,1:T(8,128)(2,1)}, u32[]{:S(2)}) copy-start(bf16[768,192]{0,1:T(8,128)(2,1)} %param.19) | copy-start | bytes 884740
  0.6 23.1 %copy-start.2 = (bf16[192,192]{1,0:T(8,128)(2,1)S(1)}, bf16[192,192]{1,0:T(8,128)(2,1)}, u32[]{:S(2)}) copy-start(bf16[192,192]{1,0:T(8,128)(2,1)} %wout.1) | copy-start | bytes 221188
  2.0 21.8 %copy-start = (bf16[192,768]{1,0:T(8,128)(2,1)S(1)}, bf16[192,768]{1,0:T(8,128)(2,1)}, u32[]{:S(2)}) copy-start(bf16[192,768]{1,0:T(8,128)(2,1)} %wup.1) | copy-start | bytes 884740
  2.0 11.4 %collective-permute-start = (bf16[2,2,40,384]{3,2,1,0:T(8,128)(2,1)S(1)}, bf16[2,2,40,384]{3,2,1,0:T(8,128)(2,1)S(1)}, u32[]{:S(2)}, u32[]{:S(2)}) collective-permute-start(bf16[2,2,40,384]{3,2,1,0:T(8,128)(2,1)S(1)} %get-tuple-element.38), channel_id=1, source_target_pairs={{0,64},{64,0},{1,65},{65,1},{2,66},{66,2},{3,67},{67,3},{4,68},{68... | collective-permute-start | bytes 368648 | tf_op jit(solution)/shard_map/ppermute | solution.py:397
  5.3 7.0 %collective-permute-start.1 = (bf16[2,24,384]{2,1,0:T(8,128)(2,1)S(1)}, bf16[2,24,384]{2,1,0:T(8,128)(2,1)S(1)}, u32[]{:S(2)}, u32[]{:S(2)}) collective-permute-start(bf16[2,24,384]{2,1,0:T(8,128)(2,1)S(1)} %get-tuple-element.39), channel_id=1, source_target_pairs={{0,120},{1,121},{2,122},{3,123},{4,124},{5,125},{6,126},{7,127},{8... | collective-permute-start | bytes 110600 | tf_op jit(solution)/shard_map/ppermute | solution.py:393
  6.6 6.8 %collective-permute-start.2 = (bf16[2,24,384]{2,1,0:T(8,128)(2,1)S(1)}, bf16[2,24,384]{2,1,0:T(8,128)(2,1)S(1)}, u32[]{:S(2)}, u32[]{:S(2)}) collective-permute-start(bf16[2,24,384]{2,1,0:T(8,128)(2,1)S(1)} %get-tuple-element.39), channel_id=1, source_target_pairs={{64,120},{65,121},{66,122},{67,123},{68,124},{69,125},{70,126},{71... | collective-permute-start | bytes 110600 | tf_op jit(solution)/shard_map/ppermute | solution.py:393
  13.5 7.9 %collective-permute-start.3 = (bf16[2,40,384]{2,1,0:T(8,128)(2,1)S(1)}, bf16[2,40,384]{2,1,0:T(8,128)(2,1)S(1)}, u32[]{:S(2)}, u32[]{:S(2)}) collective-permute-start(bf16[2,40,384]{2,1,0:T(8,128)(2,1)S(1)} %get-tuple-element.40), channel_id=1, source_target_pairs={{0,135},{1,128},{2,129},{3,130},{4,131},{5,132},{6,133},{7,134},{8... | collective-permute-start | bytes 184328 | tf_op jit(solution)/shard_map/ppermute | solution.py:393
  18.5 5.2 %collective-permute-start.4 = (bf16[2,40,384]{2,1,0:T(8,128)(2,1)S(1)}, bf16[2,40,384]{2,1,0:T(8,128)(2,1)S(1)}, u32[]{:S(2)}, u32[]{:S(2)}) collective-permute-start(bf16[2,40,384]{2,1,0:T(8,128)(2,1)S(1)} %get-tuple-element.41), channel_id=1, source_target_pairs={{0,128},{1,129},{2,130},{3,131},{4,132},{5,133},{6,134},{7,135},{8... | collective-permute-start | bytes 184328 | tf_op jit(solution)/shard_map/ppermute | solution.py:393
  19.1 4.7 %collective-permute-start.5 = (bf16[2,40,384]{2,1,0:T(8,128)(2,1)S(1)}, bf16[2,40,384]{2,1,0:T(8,128)(2,1)S(1)}, u32[]{:S(2)}, u32[]{:S(2)}) collective-permute-start(bf16[2,40,384]{2,1,0:T(8,128)(2,1)S(1)} %get-tuple-element.42), channel_id=1, source_target_pairs={{0,7},{1,0},{2,1},{3,2},{4,3},{5,4},{6,5},{7,6},{8,15},{9,8},{10,9... | collective-permute-start | bytes 184328 | tf_op jit(solution)/shard_map/ppermute | solution.py:393
  31.7 2.4 %collective-permute-start.6 = (bf16[2176,128]{1,0:T(8,128)(2,1)S(1)}, bf16[2176,128]{1,0:T(8,128)(2,1)S(1)}, u32[]{:S(2)}, u32[]{:S(2)}) collective-permute-start(bf16[2176,128]{1,0:T(8,128)(2,1)S(1)} %get-tuple-element.47), channel_id=1, source_target_pairs={{0,64},{64,0},{1,65},{65,1},{2,66},{66,2},{3,67},{67,3},{4,68},{68... | collective-permute-start | bytes 1671176 | tf_op jit(solution)/shard_map/ppermute | solution.py:397
  50.4 12.2 %all-to-all-start.1 = ((bf16[8,112,128]{2,1,0:T(8,128)(2,1)}), bf16[8,112,128]{2,1,0:T(8,128)(2,1)S(1)}, u32[]{:S(2)}, u32[]{:S(2)}) async-start(bf16[8,112,128]{2,1,0:T(8,128)(2,1)} %sum_group.1), calls=%async_computation.1 | async-start | bytes 458752 | tf_op jit(solution)/shard_map/all_to_all | solution.py:401
  53.9 6.3 %collective-permute-start.7 = (bf16[2,96,128]{2,1,0:T(8,128)(2,1)S(1)}, bf16[2,96,128]{2,1,0:T(8,128)(2,1)S(1)}, u32[]{:S(2)}, u32[]{:S(2)}) collective-permute-start(bf16[2,96,128]{2,1,0:T(8,128)(2,1)S(1)} %get-tuple-element.49), channel_id=1, source_target_pairs={{0,129},{1,130},{2,131},{3,132},{4,133},{5,134},{6,135},{7,128},{8... | collective-permute-start | bytes 147464 | tf_op jit(solution)/shard_map/ppermute | solution.py:393
  54.8 5.3 %collective-permute-start.8 = (bf16[2,96,128]{2,1,0:T(8,128)(2,1)S(1)}, bf16[2,96,128]{2,1,0:T(8,128)(2,1)S(1)}, u32[]{:S(2)}, u32[]{:S(2)}) collective-permute-start(bf16[2,96,128]{2,1,0:T(8,128)(2,1)S(1)} %get-tuple-element.50), channel_id=1, source_target_pairs={{0,128},{1,129},{2,130},{3,131},{4,132},{5,133},{6,134},{7,135},{8... | collective-permute-start | bytes 147464 | tf_op jit(solution)/shard_map/ppermute | solution.py:393
  56.9 5.3 %collective-permute-start.9 = (bf16[2,96,128]{2,1,0:T(8,128)(2,1)S(1)}, bf16[2,96,128]{2,1,0:T(8,128)(2,1)S(1)}, u32[]{:S(2)}, u32[]{:S(2)}) collective-permute-start(bf16[2,96,128]{2,1,0:T(8,128)(2,1)S(1)} %get-tuple-element.51), channel_id=1, source_target_pairs={{0,1},{1,2},{2,3},{3,4},{4,5},{5,6},{6,7},{7,0},{8,9},{9,10},{10,1... | collective-permute-start | bytes 147464 | tf_op jit(solution)/shard_map/ppermute | solution.py:393
  63.5 12.5 %all-to-all-start.2 = ((bf16[16,112,128]{2,1,0:T(8,128)(2,1)}), bf16[16,112,128]{2,1,0:T(8,128)(2,1)S(1)}, u32[]{:S(2)}, u32[]{:S(2)}) async-start(bf16[16,112,128]{2,1,0:T(8,128)(2,1)} %get-tuple-element.55), calls=%async_computation.2 | async-start | bytes 917504 | tf_op jit(solution)/shard_map/all_to_all | solution.py:401
  67.3 4.2 %collective-permute-start.10 = (bf16[2,96,128]{2,1,0:T(8,128)(2,1)S(1)}, bf16[2,96,128]{2,1,0:T(8,128)(2,1)S(1)}, u32[]{:S(2)}, u32[]{:S(2)}) collective-permute-start(bf16[2,96,128]{2,1,0:T(8,128)(2,1)S(1)} %get-tuple-element.56), channel_id=1, source_target_pairs={{0,8},{1,9},{2,10},{3,11},{4,12},{5,13},{6,14},{7,15},{8,16},{9,17... | collective-permute-start | bytes 147464 | tf_op jit(solution)/shard_map/ppermute | solution.py:393
  76.0 5.8 %collective-permute-start.11 = (bf16[1792,128]{1,0:T(8,128)(2,1)S(1)}, bf16[1792,128]{1,0:T(8,128)(2,1)S(1)}, u32[]{:S(2)}, u32[]{:S(2)}) collective-permute-start(bf16[1792,128]{1,0:T(8,128)(2,1)S(1)} %bitcast.19), channel_id=1, source_target_pairs={{0,64},{64,0},{1,65},{65,1},{2,66},{66,2},{3,67},{67,3},{4,68},{68... | collective-permute-start | bytes 1376264 | tf_op jit(solution)/shard_map/ppermute | solution.py:397

commit v10 on v9

--- a/solution.py
+++ b/solution.py
@@ -24,7 +24,6 @@
 SUMS = GROUP * UNIT
 BLOCK = 48
 QUARTER = 4 * BLOCK
-COLUMNS = QUARTER // 2
 SENT = SUMS + 2 * QUARTER
 HALF_CH = CH // 2
 TILED = 18 * HALF_CH
@@ -297,20 +296,19 @@
     send_out[SUMS:SENT, :] = msg[1 - core]
 
 
-def pair_kernel(kept, arrived, chunks, near_own, near_x, lon_own, lon_x):
+def pair_kernel(kept, arrived, chunks, x_send, x_keep):
     core = lax.axis_index("core")
     here = lax.axis_index("xh")
     for g in range(GROUP):
         at = UNIT * g
         total = kept[at : at + UNIT, :].astype(F32) + arrived[at : at + UNIT, :].astype(F32)
         chunks[g] = total.astype(BF16)
-    for half, near, lon in ((here, near_own, lon_own), (1 - here, near_x, lon_x)):
-        first = pl.ds(pl.multiple_of(SUMS + QUARTER * half, 64), COLUMNS)
-        second = pl.ds(pl.multiple_of(SUMS + QUARTER * half + COLUMNS, 32), COLUMNS)
-        near[core] = kept[first, :]
-        near[1 - core] = arrived[first, :]
-        lon[core] = kept[second, :]
-        lon[1 - core] = arrived[second, :]
+    own = pl.ds(pl.multiple_of(SUMS + QUARTER * here, 64), QUARTER)
+    other = pl.ds(pl.multiple_of(SUMS + QUARTER * (1 - here), 64), QUARTER)
+    x_send[core] = kept[other, :]
+    x_send[1 - core] = arrived[other, :]
+    x_keep[core] = kept[own, :]
+    x_keep[1 - core] = arrived[own, :]
 
 
 def group_kernel(terms, total_out):
@@ -322,15 +320,16 @@
         total_out[g] = total
 
 
-def column_kernel(terms, lon_x, near_x, lon_own, near_own, total_out, near, lon, to_lat):
+def column_kernel(terms, kept, arrived, total_out, near, to_lon, to_lat, to_both):
     here = lax.axis_index("xh")
+    half = QUARTER // 2
     for c in range(2):
-        near[2 * here + c] = near_own[c]
-        near[2 * (1 - here) + c] = near_x[c]
-        lon[2 * here + c] = lon_own[c]
-        lon[2 * (1 - here) + c] = lon_x[c]
-    to_lat[0] = near[3]
-    to_lat[1] = lon[3]
+        near[2 * here + c] = kept[c, 0:half, :]
+        near[2 * (1 - here) + c] = arrived[c, 0:half, :]
+        to_lon[2 * here + c] = kept[c, half:QUARTER, :]
+        to_lon[2 * (1 - here) + c] = arrived[c, half:QUARTER, :]
+    to_lat[...] = near[3]
+    to_both[...] = to_lon[3]
     total = terms[0].astype(F32)
     for g in range(1, 8):
         total = total + terms[g].astype(F32)
@@ -364,12 +363,12 @@
         )
 
 
-def state_kernel(near, lon, edges, state_out):
-    for part, first, wide in ((0, 6, near), (1, 0, lon)):
+def state_kernel(near, from_lon, from_lat, from_both, state_out):
+    for first, wide, edge in ((6, near, from_lat), (0, from_lon, from_both)):
         for tile, lanes in ((0, slice(0, 128)), (1, slice(128, 192))):
             n = lanes.stop - lanes.start
             at = slice(BLOCK * tile, BLOCK * tile + BLOCK)
-            before = edges[part, at, :].astype(F32)
+            before = edge[at, :].astype(F32)
             for c in range(6):
                 state_out[first + c, 0:3, lanes] = before[6 * c + 3 : 6 * c + 6, 0:n]
             for k in range(4):
@@ -488,28 +487,31 @@
         lon_x, near_x, lon_own, near_own, vectors, w_qkv, w_out, w_up, w_down.T
     )
 
-    chunks, near_own, near_x, lon_own, lon_x = call(
+    chunks, x_send, x_keep = call(
         pair_kernel,
         "sum_cores",
-        [((GROUP, UNIT, 128), BF16)] + [((2, COLUMNS, 128), BF16)] * 4,
+        [((GROUP, UNIT, 128), BF16)] + [((2, QUARTER, 128), BF16)] * 2,
     )(keep, swap(send, "core"))
-    lon_x = hop(lon_x, 0, 1, 1)
-    near_x = hop(near_x, 0, 0, 1)
-    lon_own = hop(lon_own, 0, 1)
+    x_arrived = swap(x_send, "xh")
     (partial,) = call(group_kernel, "sum_group", [((8, UNIT, 128), BF16)])(
         exchange(chunks, ("xh", "lon"))
     )
-    total, near, lon, to_lat = call(
+    total, near, to_lon, to_lat, to_both = call(
         column_kernel,
         "sum_column",
         [((GROUP, UNIT, 128), BF16)]
-        + [((4, COLUMNS, 128), BF16)] * 2
-        + [((2, COLUMNS, 128), BF16)],
-    )(exchange(partial, "lat"), lon_x, near_x, lon_own, near_own)
-    own, edges = lax.optimization_barrier((exchange(total, ("xh", "lon")), hop(to_lat, 1, 0)))
+        + [((4, QUARTER // 2, 128), BF16)] * 2
+        + [((QUARTER // 2, 128), BF16)] * 2,
+    )(exchange(partial, "lat"), x_keep, x_arrived)
+    from_lon = hop(to_lon, 0, 1)
+    from_lat = hop(to_lat, 1, 0)
+    from_both = hop(to_both, 1, 1)
+    own, from_lon, from_lat, from_both = lax.optimization_barrier(
+        (exchange(total, ("xh", "lon")), from_lon, from_lat, from_both)
+    )
     own = own.reshape(SUMS, 128)
     (state_grads,) = call(state_kernel, "unpack_states", [((WIN_LON, ROWS, CH), F32)])(
-        near, lon, edges
+        near, from_lon, from_lat, from_both
     )
     outs = call(
         unpack_kernel,

time: 83.4 us -> 84.1 us (level)
  waiting for transfers between devices: 20 us -> 21.2 us
    ppermute x3 -> x4, waiting for transfers between devices: 2.26 us -> 6.28 us  [swap(): return lax.ppermute(value, axis, [(0, 1), (1, 0)])]
    ppermute x9 -> x8, waiting for transfers between devices: 12.9 us -> 11.2 us  [hop(): return lax.ppermute(value, AXES, pairs)]
    ppermute x9 -> x8, starting transfers between devices: 18 us -> 16.3 us  [hop(): return lax.ppermute(value, AXES, pairs)]
    ppermute x3 -> x4, starting transfers between devices: 8.43 us -> 9.52 us  [swap(): return lax.ppermute(value, axis, [(0, 1), (1, 0)])]
    all_to_all x2, waiting for transfers between devices: 4.84 us -> 3.77 us  [exchange(): return lax.all_to_all(value, axis, 0, 0, tiled=True)]
  transfers between devices with their start and end apart: 14 -> 14, of which waited for: 10 -> 8; matrix products, arithmetic and copies ran while one was open for 0% -> 0% of each run, Pallas kernels for 1% -> 1%
where the time goes in v10:
time: 84.1 us; the launch traced here: 83.7 us
  starting transfers between devices  33.1 us (39%)
  waiting for transfers between devices  21.2 us (25%)
  blocking collectives  15.5 us (18%)
  Pallas kernels  13.2 us (16%)
    ppermute x8, starting transfers between devices, hop(): return lax.ppermute(value, AXES, pairs)  16.3 us
    all_to_all x1, blocking collectives, exchange(): return lax.all_to_all(value, axis, 0, 0, tiled=True)  15.5 us
    ppermute x8, waiting for transfers between devices, hop(): return lax.ppermute(value, AXES, pairs)  11.2 us
    ppermute x4, starting transfers between devices, swap(): return lax.ppermute(value, axis, [(0, 1), (1, 0)])  9.52 us
    pallas_call x1, Pallas kernels, local(): call(main_kernel, 'window_steps', [((SENT, 128), BF16)] * 2, [((STEPS, WI...  7.95 us
    all_to_all x2, starting transfers between devices, exchange(): return lax.all_to_all(value, axis, 0, 0, tiled=True)  7.23 us
    ppermute x4, waiting for transfers between devices, swap(): return lax.ppermute(value, axis, [(0, 1), (1, 0)])  6.28 us
    all_to_all x2, waiting for transfers between devices, exchange(): return lax.all_to_all(value, axis, 0, 0, tiled=True)  3.77 us
  transfers between devices with their start and end apart: 14, of which 8 were waited for; matrix products, arithmetic and copies ran while one was open for 0% of the time, Pallas kernels for 1%

profile of v10, /device:TPU:1, one launch (start us, length us, event | category | flops | bytes accessed | tf_op | source)
XLA Modules:
  0.0 83.7 jit_solution(14234474081581134679)
XLA Ops:
  0.7 1.3 %pack_cells.1 = (bf16[2,2,40,384]{3,2,1,0:T(8,128)(2,1)S(1)}, bf16[2,2,40,384]{3,2,1,0:T(8,128)(2,1)S(1)}, bf16[2,24,384]{2,1,0:T(8,128)(2,1)S(1)}, f32[8,192]{1,0:T(8,128)S(1)}, bf16[192,576]{1,0:T(8,128)(2,1)S(1)}) custom-call(bf16[12,24,192]{2,1,0:T(8,128)(2,1)} %bitcast.23, bf16[12,24,192]{2,1,0:T(8,128)(2,1)} %bitcast.24, s32[12,24]{1,0:T(8,128)} %bitcast.25, ...), custom_call_target="tpu_custom_call" | custom-call | tf_op jit(solution)/shard_map/pack_cells/pallas_call | solution.py:420
  2.0 3.3 %collective-permute-start = (bf16[2,2,40,384]{3,2,1,0:T(8,128)(2,1)S(1)}, bf16[2,2,40,384]{3,2,1,0:T(8,128)(2,1)S(1)}, u32[]{:S(2)}, u32[]{:S(2)}) collective-permute-start(bf16[2,2,40,384]{3,2,1,0:T(8,128)(2,1)S(1)} %get-tuple-element.39), channel_id=1, source_target_pairs={{0,64},{64,0},{1,65},{65,1},{2,66},{66,2},{3,67},{67,3},{4,68},{68... | collective-permute-start | bytes 368648 | tf_op jit(solution)/shard_map/ppermute | solution.py:396
  5.3 1.3 %collective-permute-start.1 = (bf16[2,24,384]{2,1,0:T(8,128)(2,1)S(1)}, bf16[2,24,384]{2,1,0:T(8,128)(2,1)S(1)}, u32[]{:S(2)}, u32[]{:S(2)}) collective-permute-start(bf16[2,24,384]{2,1,0:T(8,128)(2,1)S(1)} %get-tuple-element.40), channel_id=1, source_target_pairs={{0,120},{1,121},{2,122},{3,123},{4,124},{5,125},{6,126},{7,127},{8... | collective-permute-start | bytes 110600 | tf_op jit(solution)/shard_map/ppermute | solution.py:392
  6.6 5.7 %collective-permute-start.2 = (bf16[2,24,384]{2,1,0:T(8,128)(2,1)S(1)}, bf16[2,24,384]{2,1,0:T(8,128)(2,1)S(1)}, u32[]{:S(2)}, u32[]{:S(2)}) collective-permute-start(bf16[2,24,384]{2,1,0:T(8,128)(2,1)S(1)} %get-tuple-element.40), channel_id=1, source_target_pairs={{64,120},{65,121},{66,122},{67,123},{68,124},{69,125},{70,126},{71... | collective-permute-start | bytes 110600 | tf_op jit(solution)/shard_map/ppermute | solution.py:392
  12.4 1.0 %collective-permute-done.2.edge1 = bf16[2,24,384]{2,1,0:T(8,128)(2,1)S(1)} collective-permute-done((bf16[2,24,384]{2,1,0:T(8,128)(2,1)S(1)}, bf16[2,24,384]{2,1,0:T(8,128)(2,1)S(1)}, u32[]{:S(2)}, u32[]{:S(2)}) %collective-permute-start.2) | collective-permute-done | bytes 36896 | tf_op jit(solution)/shard_map/ppermute | solution.py:392
  13.5 5.0 %collective-permute-start.3 = (bf16[2,40,384]{2,1,0:T(8,128)(2,1)S(1)}, bf16[2,40,384]{2,1,0:T(8,128)(2,1)S(1)}, u32[]{:S(2)}, u32[]{:S(2)}) collective-permute-start(bf16[2,40,384]{2,1,0:T(8,128)(2,1)S(1)} %get-tuple-element.41), channel_id=1, source_target_pairs={{0,135},{1,128},{2,129},{3,130},{4,131},{5,132},{6,133},{7,134},{8... | collective-permute-start | bytes 184328 | tf_op jit(solution)/shard_map/ppermute | solution.py:392
  19.1 1.4 %collective-permute-start.5 = (bf16[2,40,384]{2,1,0:T(8,128)(2,1)S(1)}, bf16[2,40,384]{2,1,0:T(8,128)(2,1)S(1)}, u32[]{:S(2)}, u32[]{:S(2)}) collective-permute-start(bf16[2,40,384]{2,1,0:T(8,128)(2,1)S(1)} %get-tuple-element.43), channel_id=1, source_target_pairs={{0,7},{1,0},{2,1},{3,2},{4,3},{5,4},{6,5},{7,6},{8,15},{9,8},{10,9... | collective-permute-start | bytes 184328 | tf_op jit(solution)/shard_map/ppermute | solution.py:392
  20.4 1.0 %collective-permute-done.3.lon_x = bf16[2,40,384]{2,1,0:T(8,128)(2,1)S(1)} collective-permute-done((bf16[2,40,384]{2,1,0:T(8,128)(2,1)S(1)}, bf16[2,40,384]{2,1,0:T(8,128)(2,1)S(1)}, u32[]{:S(2)}, u32[]{:S(2)}) %collective-permute-start.3) | collective-permute-done | bytes 61472 | tf_op jit(solution)/shard_map/ppermute | solution.py:392
  21.4 2.3 %collective-permute-done.4.near_x = bf16[2,40,384]{2,1,0:T(8,128)(2,1)S(1)} collective-permute-done((bf16[2,40,384]{2,1,0:T(8,128)(2,1)S(1)}, bf16[2,40,384]{2,1,0:T(8,128)(2,1)S(1)}, u32[]{:S(2)}, u32[]{:S(2)}) %collective-permute-start.4) | collective-permute-done | bytes 61472 | tf_op jit(solution)/shard_map/ppermute | solution.py:392
  23.8 8.0 %window_steps.1 = (bf16[2176,128]{1,0:T(8,128)(2,1)S(1)}, bf16[2176,128]{1,0:T(8,128)(2,1)S(1)}) custom-call(bf16[2,40,384]{2,1,0:T(8,128)(2,1)S(1)} %collective-permute-done.3.lon_x, bf16[2,40,384]{2,1,0:T(8,128)(2,1)S(1)} %collective-permute-done.4.near_x, bf16[2,40,384]{2,1,0:T(8,128)(2,1)S(1)} %collective-permute-done.5.lon_own, ...), custom_call_target="tpu_custom_call" | custom-call | tf_op jit(solution)/shard_map/window_steps/pallas_call | solution.py:456
  31.7 0.8 collective-permute-start.6
  32.5 1.6 %collective-permute-done.6.arrived = bf16[2176,128]{1,0:T(8,128)(2,1)S(1)} collective-permute-done((bf16[2176,128]{1,0:T(8,128)(2,1)S(1)}, bf16[2176,128]{1,0:T(8,128)(2,1)S(1)}, u32[]{:S(2)}, u32[]{:S(2)}) %collective-permute-start.6) | collective-permute-done | bytes 557088 | tf_op jit(solution)/shard_map/ppermute | solution.py:396
  34.2 15.5 %all_to_all.15.terms = bf16[16,112,128]{2,1,0:T(8,128)(2,1)S(1)} all-to-all(bf16[16,112,128]{2,1,0:T(8,128)(2,1)S(1)} %get-tuple-element.49), channel_id=1, replica_groups=mesh['xh'=2,'core'=2,'lat'=8,'lon'=8] {'xh','lon'}, dimensions={0} | all-to-all | bytes 917504 | tf_op jit(solution)/shard_map/all_to_all | solution.py:400
  50.4 3.4 %all-to-all-start.1 = ((bf16[8,112,128]{2,1,0:T(8,128)(2,1)}), bf16[8,112,128]{2,1,0:T(8,128)(2,1)S(1)}, u32[]{:S(2)}, u32[]{:S(2)}) async-start(bf16[8,112,128]{2,1,0:T(8,128)(2,1)} %sum_group.1), calls=%async_computation.1 | async-start | bytes 458752 | tf_op jit(solution)/shard_map/all_to_all | solution.py:400
  53.9 1.0 %collective-permute-start.7 = (bf16[2,192,128]{2,1,0:T(8,128)(2,1)S(1)}, bf16[2,192,128]{2,1,0:T(8,128)(2,1)S(1)}, u32[]{:S(2)}, u32[]{:S(2)}) collective-permute-start(bf16[2,192,128]{2,1,0:T(8,128)(2,1)S(1)} %get-tuple-element.51), channel_id=1, source_target_pairs={{0,128},{128,0},{1,129},{129,1},{2,130},{130,2},{3,131},{131,3},{4... | collective-permute-start | bytes 294920 | tf_op jit(solution)/shard_map/ppermute | solution.py:396
  54.9 4.0 %collective-permute-done.7.arrived = bf16[2,192,128]{2,1,0:T(8,128)(2,1)S(1)} collective-permute-done((bf16[2,192,128]{2,1,0:T(8,128)(2,1)S(1)}, bf16[2,192,128]{2,1,0:T(8,128)(2,1)S(1)}, u32[]{:S(2)}, u32[]{:S(2)}) %collective-permute-start.7) | collective-permute-done | bytes 98336 | tf_op jit(solution)/shard_map/ppermute | solution.py:396
  58.9 3.7 %all-to-all-done.1.terms = bf16[8,112,128]{2,1,0:T(8,128)(2,1)S(1)} async-done(((bf16[8,112,128]{2,1,0:T(8,128)(2,1)}), bf16[8,112,128]{2,1,0:T(8,128)(2,1)S(1)}, u32[]{:S(2)}, u32[]{:S(2)}) %all-to-all-start.1) | async-done | bytes 229408 | tf_op jit(solution)/shard_map/all_to_all | solution.py:400
  62.6 0.8 %sum_column.1 = (bf16[16,112,128]{2,1,0:T(8,128)(2,1)}, bf16[4,96,128]{2,1,0:T(8,128)(2,1)S(1)}, bf16[4,96,128]{2,1,0:T(8,128)(2,1)S(1)}, bf16[96,128]{1,0:T(8,128)(2,1)S(1)}, bf16[96,128]{1,0:T(8,128)(2,1)S(1)}) custom-call(bf16[8,112,128]{2,1,0:T(8,128)(2,1)S(1)} %all-to-all-done.1.terms, bf16[2,192,128]{2,1,0:T(8,128)(2,1)S(1)} %get-tuple-element.50.kept, ...), custom_call_target="tpu_custom_call" | custom-call | tf_op jit(solution)/shard_map/sum_column/pallas_call | solution.py:499
  63.5 3.8 %all-to-all-start.2 = ((bf16[16,112,128]{2,1,0:T(8,128)(2,1)}), bf16[16,112,128]{2,1,0:T(8,128)(2,1)S(1)}, u32[]{:S(2)}, u32[]{:S(2)}) async-start(bf16[16,112,128]{2,1,0:T(8,128)(2,1)} %get-tuple-element.53), calls=%async_computation.2 | async-start | bytes 917504 | tf_op jit(solution)/shard_map/all_to_all | solution.py:400
  67.3 1.4 %collective-permute-start.8 = (bf16[4,96,128]{2,1,0:T(8,128)(2,1)S(1)}, bf16[4,96,128]{2,1,0:T(8,128)(2,1)S(1)}, u32[]{:S(2)}, u32[]{:S(2)}) collective-permute-start(bf16[4,96,128]{2,1,0:T(8,128)(2,1)S(1)} %get-tuple-element.54), channel_id=1, source_target_pairs={{0,1},{1,2},{2,3},{3,4},{4,5},{5,6},{6,7},{7,0},{8,9},{9,10},{10,1... | collective-permute-start | bytes 294920 | tf_op jit(solution)/shard_map/ppermute | solution.py:392
  68.7 1.1 %collective-permute-start.10 = (bf16[96,128]{1,0:T(8,128)(2,1)S(1)}, bf16[96,128]{1,0:T(8,128)(2,1)S(1)}, u32[]{:S(2)}, u32[]{:S(2)}) collective-permute-start(bf16[96,128]{1,0:T(8,128)(2,1)S(1)} %get-tuple-element.56), channel_id=1, source_target_pairs={{0,9},{1,10},{2,11},{3,12},{4,13},{5,14},{6,15},{7,8},{8,17},{9,18... | collective-permute-start | bytes 73736 | tf_op jit(solution)/shard_map/ppermute | solution.py:392
  69.8 6.8 %collective-permute-done.10.from_both = bf16[96,128]{1,0:T(8,128)(2,1)S(1)} collective-permute-done((bf16[96,128]{1,0:T(8,128)(2,1)S(1)}, bf16[96,128]{1,0:T(8,128)(2,1)S(1)}, u32[]{:S(2)}, u32[]{:S(2)}) %collective-permute-start.10) | collective-permute-done | bytes 24608 | tf_op jit(solution)/shard_map/ppermute | solution.py:392
  76.6 4.4 %collective-permute-start.11 = (bf16[1792,128]{1,0:T(8,128)(2,1)S(1)}, bf16[1792,128]{1,0:T(8,128)(2,1)S(1)}, u32[]{:S(2)}, u32[]{:S(2)}) collective-permute-start(bf16[1792,128]{1,0:T(8,128)(2,1)S(1)} %bitcast.19), channel_id=1, source_target_pairs={{0,64},{64,0},{1,65},{65,1},{2,66},{66,2},{3,67},{67,3},{4,68},{68... | collective-permute-start | bytes 1376264 | tf_op jit(solution)/shard_map/ppermute | solution.py:396
  82.4 1.3 %unpack_sums.1 = (f32[192,576]{1,0:T(8,128)}, f32[192,192]{1,0:T(8,128)}, f32[192,768]{1,0:T(8,128)}, f32[192,768]{1,0:T(8,128)}, f32[1,192]{1,0:T(1,128)}, /*index=5*/f32[1,192]{1,0:T(1,128)}, f32[1,192]{1,0:T(1,128)}) custom-call(bf16[1792,128]{1,0:T(8,128)(2,1)S(1)} %bitcast.20, bf16[1792,128]{1,0:T(8,128)(2,1)S(1)} %collective-permute-done.11.other), custom_call_target="tpu_custom_call" | custom-call | tf_op jit(solution)/shard_map/unpack_sums/pallas_call | solution.py:516
  (19 shorter events, 3.0 us)
Async XLA Ops:
  0.6 23.1 %copy-start.1 = (bf16[768,192]{0,1:T(8,128)(2,1)S(1)}, bf16[768,192]{0,1:T(8,128)(2,1)}, u32[]{:S(2)}) copy-start(bf16[768,192]{0,1:T(8,128)(2,1)} %param.19) | copy-start | bytes 884740
  0.6 23.1 %copy-start.2 = (bf16[192,192]{1,0:T(8,128)(2,1)S(1)}, bf16[192,192]{1,0:T(8,128)(2,1)}, u32[]{:S(2)}) copy-start(bf16[192,192]{1,0:T(8,128)(2,1)} %wout.1) | copy-start | bytes 221188
  2.0 21.8 %copy-start = (bf16[192,768]{1,0:T(8,128)(2,1)S(1)}, bf16[192,768]{1,0:T(8,128)(2,1)}, u32[]{:S(2)}) copy-start(bf16[192,768]{1,0:T(8,128)(2,1)} %wup.1) | copy-start | bytes 884740
  2.0 11.4 %collective-permute-start = (bf16[2,2,40,384]{3,2,1,0:T(8,128)(2,1)S(1)}, bf16[2,2,40,384]{3,2,1,0:T(8,128)(2,1)S(1)}, u32[]{:S(2)}, u32[]{:S(2)}) collective-permute-start(bf16[2,2,40,384]{3,2,1,0:T(8,128)(2,1)S(1)} %get-tuple-element.39), channel_id=1, source_target_pairs={{0,64},{64,0},{1,65},{65,1},{2,66},{66,2},{3,67},{67,3},{4,68},{68... | collective-permute-start | bytes 368648 | tf_op jit(solution)/shard_map/ppermute | solution.py:396
  5.3 7.0 %collective-permute-start.1 = (bf16[2,24,384]{2,1,0:T(8,128)(2,1)S(1)}, bf16[2,24,384]{2,1,0:T(8,128)(2,1)S(1)}, u32[]{:S(2)}, u32[]{:S(2)}) collective-permute-start(bf16[2,24,384]{2,1,0:T(8,128)(2,1)S(1)} %get-tuple-element.40), channel_id=1, source_target_pairs={{0,120},{1,121},{2,122},{3,123},{4,124},{5,125},{6,126},{7,127},{8... | collective-permute-start | bytes 110600 | tf_op jit(solution)/shard_map/ppermute | solution.py:392
  6.6 6.8 %collective-permute-start.2 = (bf16[2,24,384]{2,1,0:T(8,128)(2,1)S(1)}, bf16[2,24,384]{2,1,0:T(8,128)(2,1)S(1)}, u32[]{:S(2)}, u32[]{:S(2)}) collective-permute-start(bf16[2,24,384]{2,1,0:T(8,128)(2,1)S(1)} %get-tuple-element.40), channel_id=1, source_target_pairs={{64,120},{65,121},{66,122},{67,123},{68,124},{69,125},{70,126},{71... | collective-permute-start | bytes 110600 | tf_op jit(solution)/shard_map/ppermute | solution.py:392
  13.5 7.9 %collective-permute-start.3 = (bf16[2,40,384]{2,1,0:T(8,128)(2,1)S(1)}, bf16[2,40,384]{2,1,0:T(8,128)(2,1)S(1)}, u32[]{:S(2)}, u32[]{:S(2)}) collective-permute-start(bf16[2,40,384]{2,1,0:T(8,128)(2,1)S(1)} %get-tuple-element.41), channel_id=1, source_target_pairs={{0,135},{1,128},{2,129},{3,130},{4,131},{5,132},{6,133},{7,134},{8... | collective-permute-start | bytes 184328 | tf_op jit(solution)/shard_map/ppermute | solution.py:392
  18.5 5.2 %collective-permute-start.4 = (bf16[2,40,384]{2,1,0:T(8,128)(2,1)S(1)}, bf16[2,40,384]{2,1,0:T(8,128)(2,1)S(1)}, u32[]{:S(2)}, u32[]{:S(2)}) collective-permute-start(bf16[2,40,384]{2,1,0:T(8,128)(2,1)S(1)} %get-tuple-element.42), channel_id=1, source_target_pairs={{0,128},{1,129},{2,130},{3,131},{4,132},{5,133},{6,134},{7,135},{8... | collective-permute-start | bytes 184328 | tf_op jit(solution)/shard_map/ppermute | solution.py:392
  19.1 4.7 %collective-permute-start.5 = (bf16[2,40,384]{2,1,0:T(8,128)(2,1)S(1)}, bf16[2,40,384]{2,1,0:T(8,128)(2,1)S(1)}, u32[]{:S(2)}, u32[]{:S(2)}) collective-permute-start(bf16[2,40,384]{2,1,0:T(8,128)(2,1)S(1)} %get-tuple-element.43), channel_id=1, source_target_pairs={{0,7},{1,0},{2,1},{3,2},{4,3},{5,4},{6,5},{7,6},{8,15},{9,8},{10,9... | collective-permute-start | bytes 184328 | tf_op jit(solution)/shard_map/ppermute | solution.py:392
  31.7 2.4 %collective-permute-start.6 = (bf16[2176,128]{1,0:T(8,128)(2,1)S(1)}, bf16[2176,128]{1,0:T(8,128)(2,1)S(1)}, u32[]{:S(2)}, u32[]{:S(2)}) collective-permute-start(bf16[2176,128]{1,0:T(8,128)(2,1)S(1)} %get-tuple-element.48), channel_id=1, source_target_pairs={{0,64},{64,0},{1,65},{65,1},{2,66},{66,2},{3,67},{67,3},{4,68},{68... | collective-permute-start | bytes 1671176 | tf_op jit(solution)/shard_map/ppermute | solution.py:396
  50.4 12.2 %all-to-all-start.1 = ((bf16[8,112,128]{2,1,0:T(8,128)(2,1)}), bf16[8,112,128]{2,1,0:T(8,128)(2,1)S(1)}, u32[]{:S(2)}, u32[]{:S(2)}) async-start(bf16[8,112,128]{2,1,0:T(8,128)(2,1)} %sum_group.1), calls=%async_computation.1 | async-start | bytes 458752 | tf_op jit(solution)/shard_map/all_to_all | solution.py:400
  53.9 5.1 %collective-permute-start.7 = (bf16[2,192,128]{2,1,0:T(8,128)(2,1)S(1)}, bf16[2,192,128]{2,1,0:T(8,128)(2,1)S(1)}, u32[]{:S(2)}, u32[]{:S(2)}) collective-permute-start(bf16[2,192,128]{2,1,0:T(8,128)(2,1)S(1)} %get-tuple-element.51), channel_id=1, source_target_pairs={{0,128},{128,0},{1,129},{129,1},{2,130},{130,2},{3,131},{131,3},{4... | collective-permute-start | bytes 294920 | tf_op jit(solution)/shard_map/ppermute | solution.py:396
  63.5 13.1 %all-to-all-start.2 = ((bf16[16,112,128]{2,1,0:T(8,128)(2,1)}), bf16[16,112,128]{2,1,0:T(8,128)(2,1)S(1)}, u32[]{:S(2)}, u32[]{:S(2)}) async-start(bf16[16,112,128]{2,1,0:T(8,128)(2,1)} %get-tuple-element.53), calls=%async_computation.2 | async-start | bytes 917504 | tf_op jit(solution)/shard_map/all_to_all | solution.py:400
  67.3 9.2 %collective-permute-start.8 = (bf16[4,96,128]{2,1,0:T(8,128)(2,1)S(1)}, bf16[4,96,128]{2,1,0:T(8,128)(2,1)S(1)}, u32[]{:S(2)}, u32[]{:S(2)}) collective-permute-start(bf16[4,96,128]{2,1,0:T(8,128)(2,1)S(1)} %get-tuple-element.54), channel_id=1, source_target_pairs={{0,1},{1,2},{2,3},{3,4},{4,5},{5,6},{6,7},{7,0},{8,9},{9,10},{10,1... | collective-permute-start | bytes 294920 | tf_op jit(solution)/shard_map/ppermute | solution.py:392
  68.7 7.8 %collective-permute-start.10 = (bf16[96,128]{1,0:T(8,128)(2,1)S(1)}, bf16[96,128]{1,0:T(8,128)(2,1)S(1)}, u32[]{:S(2)}, u32[]{:S(2)}) collective-permute-start(bf16[96,128]{1,0:T(8,128)(2,1)S(1)} %get-tuple-element.56), channel_id=1, source_target_pairs={{0,9},{1,10},{2,11},{3,12},{4,13},{5,14},{6,15},{7,8},{8,17},{9,18... | collective-permute-start | bytes 73736 | tf_op jit(solution)/shard_map/ppermute | solution.py:392
  69.8 6.8 %collective-permute-start.9 = (bf16[96,128]{1,0:T(8,128)(2,1)S(1)}, bf16[96,128]{1,0:T(8,128)(2,1)S(1)}, u32[]{:S(2)}, u32[]{:S(2)}) collective-permute-start(bf16[96,128]{1,0:T(8,128)(2,1)S(1)} %get-tuple-element.55), channel_id=1, source_target_pairs={{0,8},{1,9},{2,10},{3,11},{4,12},{5,13},{6,14},{7,15},{8,16},{9,17... | collective-permute-start | bytes 73736 | tf_op jit(solution)/shard_map/ppermute | solution.py:392
  76.6 5.8 %collective-permute-start.11 = (bf16[1792,128]{1,0:T(8,128)(2,1)S(1)}, bf16[1792,128]{1,0:T(8,128)(2,1)S(1)}, u32[]{:S(2)}, u32[]{:S(2)}) collective-permute-start(bf16[1792,128]{1,0:T(8,128)(2,1)S(1)} %bitcast.19), channel_id=1, source_target_pairs={{0,64},{64,0},{1,65},{65,1},{2,66},{66,2},{3,67},{67,3},{4,68},{68... | collective-permute-start | bytes 1376264 | tf_op jit(solution)/shard_map/ppermute | solution.py:396
